TPU v7x, 32 devices: a whole 2x2x4 slice. The times are simulated.
32 devices in a mesh: segment: 4 (over z), ctx: 4 (over x, core), tp: 2 (over y).
Axes of the slice: x: 2, y: 2, z: 4, core: 2. Of those that a mesh axis runs over, the one named last changes fastest.
Arguments:
- hidden_in: bfloat16 [4, 512, 4096], P('segment', 'ctx')
- norm_gain: bfloat16 [4, 4096], P('segment'), may hold values from 0.5 to 1.5
- query_weight: bfloat16 [4, 4096, 4096], P('segment', None, 'tp')
- keyval_weight: bfloat16 [4, 4096, 2048], P('segment', None, 'tp')
- output_weight: bfloat16 [4, 4096, 4096], P('segment', 'tp'), may hold values from -0.1875 to 0.1875
- windows: int32 [4], P('segment'), may hold values from 192 to 384, as said below
Outputs:
- handed: bfloat16 [4, 512, 4096], P('segment', 'ctx', 'tp')
Inputs may be any that keep to these rules, and one draw needn't show every extreme that they name: `windows`: one section's window is exactly 384 tokens.
All inputs are finite; a program needn't handle non-finite values.
Results may differ from a plain program's by a relative error of at most 0.006.
The roundings to bfloat16 on the way count: a program that leaves them out, or rounds other values in their place, can miss the bound.
Values may be sent and summed in bfloat16 or wider, within the bound.
No kernel may reach another device: no remote copies, remote signals or barrier semaphores. Data moves between devices by JAX's collectives and lax.ppermute only.
A program may use at most 128 MiB of HBM per device.

v0:
```python
import jax
import jax.numpy as jnp
from jax import lax
from jax.sharding import PartitionSpec as P

HD = 128
REACH = 3


NORM_EPS = 1e-05


def from_behind(value, axis, steps):
    count = lax.axis_size(axis)
    initial, last = (max(0, -steps), min(count, count - steps))
    return lax.ppermute(value, axis, [(source, source + steps) for source in range(initial, last)])


def passed_along(value, axis, steps):
    count = lax.axis_size(axis)
    pairs = [(source, (source + steps) % count) for source in range(count)]
    return lax.ppermute(value, axis, pairs)


def rotate(vector, positions):
    half_dim = vector.shape[-1] // 2
    inverse = 10000.0 ** (-jnp.arange(half_dim, dtype=jnp.float32) / half_dim)
    angles = positions.astype(jnp.float32)[:, None, None] * inverse[None, None, :]
    cosine = jnp.cos(angles)
    sine = jnp.sin(angles)
    first_half = vector[..., :half_dim]
    second_half = vector[..., half_dim:]
    return jnp.concatenate(
        [first_half * cosine - second_half * sine, second_half * cosine + first_half * sine],
        axis=-1,
    )


def attend(queries, keys, values, query_pos, key_pos, width):
    scores = jnp.einsum("qgd,kd->gqk", queries, keys, preferred_element_type=jnp.float32) * HD ** (
        -0.5
    )
    distance = query_pos[:, None] - key_pos[None, :]
    inside = ((distance >= 0) & (distance < width) & (key_pos[None, :] >= 0))[None]
    scores = jnp.where(inside, scores, jnp.float32(-1e30))
    highest = jnp.max(scores, axis=2, keepdims=True)
    expo = jnp.where(inside, jnp.exp(scores - highest), jnp.float32(0.0))
    probs = (expo / jnp.sum(expo, axis=2, keepdims=True)).astype(jnp.bfloat16)
    return jnp.einsum("gqk,kd->qgd", probs, values, preferred_element_type=jnp.float32).astype(
        jnp.bfloat16
    )


def normalize(token_rows, gain_row):
    wide_rows = token_rows.astype(jnp.float32)
    mean_square = jnp.mean(wide_rows * wide_rows, axis=1, keepdims=True)
    return (
        wide_rows * lax.rsqrt(mean_square + NORM_EPS) * gain_row.astype(jnp.float32)[None, :]
    ).astype(jnp.bfloat16)


def body(hidden_in, norm_gain, query_weight, keyval_weight, output_weight, windows):
    token_rows = hidden_in[0]
    row_count = token_rows.shape[0]
    head_count = query_weight.shape[2] // HD
    kv_count = keyval_weight.shape[2] // (2 * HD)
    group = head_count // kv_count
    normed = normalize(token_rows, norm_gain[0])
    first_row = lax.axis_index("ctx") * row_count
    local_pos = first_row + jnp.arange(row_count, dtype=jnp.int32)
    queries = jnp.dot(normed, query_weight[0], preferred_element_type=jnp.float32).reshape(
        row_count, head_count, HD
    )
    queries = rotate(queries, local_pos).astype(jnp.bfloat16)
    key_value = jnp.dot(normed, keyval_weight[0], preferred_element_type=jnp.float32).reshape(
        normed.shape[0], kv_count, 2, HD
    )
    own_keys = rotate(key_value[:, :, 0], local_pos).astype(jnp.bfloat16)
    own_values = key_value[:, :, 1].astype(jnp.bfloat16)
    key_list = []
    value_list = []
    paired = jnp.stack([own_keys, own_values], axis=2).reshape(row_count, kv_count * 2 * HD)
    for offset in range(REACH, 0, -1):
        earlier = from_behind(paired, "ctx", offset).reshape(row_count, kv_count, 2, HD)
        key_list.append(earlier[:, :, 0])
        value_list.append(earlier[:, :, 1])
    all_keys = jnp.concatenate(key_list + [own_keys], axis=0)
    all_values = jnp.concatenate(value_list + [own_values], axis=0)
    key_pos = first_row - REACH * row_count + jnp.arange((REACH + 1) * row_count, dtype=jnp.int32)
    outs_list = []
    for kv_index in range(kv_count):
        outs_list.append(
            attend(
                queries[:, kv_index * group : (kv_index + 1) * group],
                all_keys[:, kv_index],
                all_values[:, kv_index],
                local_pos,
                key_pos,
                windows[0],
            )
        )
    attn = jnp.concatenate(outs_list, axis=1).reshape(row_count, head_count * HD)
    head_term = jnp.dot(attn, output_weight[0], preferred_element_type=jnp.float32)
    summed = lax.psum_scatter(head_term, "tp", scatter_dimension=1, tiled=True).astype(jnp.bfloat16)
    passed = passed_along(summed, "segment", 1)
    return passed[None]


def solution(mesh):
    in_specs = (
        P("segment", "ctx", None),
        P("segment", None),
        P("segment", None, "tp"),
        P("segment", None, "tp"),
        P("segment", "tp", None),
        P("segment"),
    )
    out_specs = P("segment", "ctx", "tp")
    return jax.shard_map(body, mesh=mesh, in_specs=in_specs, out_specs=out_specs, check_vma=False)
```

profile of v0, /device:TPU:0, one launch (start us, length us, event | category | flops | bytes accessed | tf_op | source)
XLA Modules:
  0.0 136.8 jit_solution(15518448277667658753)
XLA Ops:
  6.5 0.7 mul.170
  7.3 1.5 %fusion.6 = f32[128]{0:T(128)S(1)} fusion(bf16[1,128,4096]{2,1,0:T(8,128)(2,1)} %param.6), kind=kLoop, calls=%fused_computation.8 | loop fusion | flops 1572736 | bytes 1049088 | tf_op jit(solution)/shard_map/reduce_sum | solution.py:56
  8.8 11.4 %copy.58 = bf16[1024,4096]{1,0:T(8,128)(2,1)} copy(bf16[1024,4096]{0,1:T(8,128)(2,1)} %bitcast.209) | data formatting | bytes 16777216 | tf_op jit(solution)/shard_map/dot_general | solution.py:75
  20.2 5.8 %fusion.33 = f32[128,4,2,128]{0,3,2,1:T(8,128)S(1)} fusion(bf16[4,2,128,4096]{3,2,1,0:T(8,128)(2,1)} %bitcast.210, bf16[1,128,4096]{2,1,0:T(8,128)(2,1)S(1)} %copy-done, f32[4096]{0:T(1024)S(1)} %bitcast.221, f32[128]{0:T(128)S(1)} %add_rsqrt_fusion), kind=kOutput, calls=%fused_computation.43 | convolution fusion | flops 1075838976 | bytes 9978368 | tf_op jit(solution)/shard_map/dot_general | solution.py:75
  26.0 0.2 multiply_cosine_fusion
  26.3 2.4 %collective-permute-start.2 = (bf16[128,1024]{0,1:T(8,128)(2,1)S(1)}, bf16[128,1024]{0,1:T(8,128)(2,1)S(1)}, u32[]{:S(2)}, u32[]{:S(2)}) collective-permute-start(bf16[128,1024]{0,1:T(8,128)(2,1)S(1)} %bitcast.215), channel_id=1, source_target_pairs={{0,2},{2,4},{4,6},{1,3},{3,5},{5,7},{8,10},{10,12},{12,14},{9,11},... | collective-permute-start | bytes 786440 | tf_op jit(solution)/shard_map/ppermute | solution.py:16
  28.7 4.4 %collective-permute-start.1 = (bf16[128,1024]{0,1:T(8,128)(2,1)S(1)}, bf16[128,1024]{0,1:T(8,128)(2,1)S(1)}, u32[]{:S(2)}, u32[]{:S(2)}) collective-permute-start(bf16[128,1024]{0,1:T(8,128)(2,1)S(1)} %bitcast.216), channel_id=1, source_target_pairs={{0,4},{2,6},{1,5},{3,7},{8,12},{10,14},{9,13},{11,15},{16,20},{18,... | collective-permute-start | bytes 786440 | tf_op jit(solution)/shard_map/ppermute | solution.py:16
  33.1 1.5 %collective-permute-start = (bf16[128,1024]{0,1:T(8,128)(2,1)S(1)}, bf16[128,1024]{0,1:T(8,128)(2,1)S(1)}, u32[]{:S(2)}, u32[]{:S(2)}) collective-permute-start(bf16[128,1024]{0,1:T(8,128)(2,1)S(1)} %bitcast.217), channel_id=1, source_target_pairs={{0,6},{1,7},{8,14},{9,15},{16,22},{17,23},{24,30},{25,31}} | collective-permute-start | bytes 786440 | tf_op jit(solution)/shard_map/ppermute | solution.py:16
  34.7 20.7 %copy.60 = bf16[2048,4096]{1,0:T(8,128)(2,1)} copy(bf16[2048,4096]{0,1:T(8,128)(2,1)} %bitcast.208) | data formatting | bytes 33554432 | tf_op jit(solution)/shard_map/dot_general | solution.py:71
  55.4 8.2 %fusion.35 = f32[128,16,128]{0,2,1:T(8,128)S(1)} fusion(bf16[16,128,4096]{2,1,0:T(8,128)(2,1)} %bitcast.207, bf16[1,128,4096]{2,1,0:T(8,128)(2,1)S(1)} %copy-done, f32[4096]{0:T(1024)S(1)} %bitcast.222, f32[128]{0:T(128)S(1)} %add_rsqrt_fusion), kind=kOutput, calls=%fused_computation.45 | convolution fusion | flops 2149580800 | bytes 18891264 | tf_op jit(solution)/shard_map/dot_general | solution.py:71
  63.6 0.2 subtract_convert_fusion
  64.4 0.2 fusion.40
  64.6 0.0 collective-permute-done.2
  64.7 0.0 collective-permute-done.1
  64.8 0.1 maximum_maximum_fusion
  64.8 0.6 fusion.133
  65.4 0.6 fusion.134
  66.0 0.6 fusion.137
  66.6 0.6 fusion.140
  67.2 0.1 pad_maximum_fusion
  67.3 0.8 fusion.32
  68.1 0.8 fusion.31
  68.9 0.8 fusion.30
  69.6 0.8 fusion.29
  70.4 0.1 pad_maximum_fusion.1
  70.5 9.5 %fusion.4 = f32[128,4096]{1,0:T(8,128)} fusion(bf16[128,2048]{0,1:T(8,128)(2,1)S(1)} %bitcast.211, bf16[1,2048,4096]{2,1,0:T(8,128)(2,1)} %param.10), kind=kOutput, calls=%fused_computation.4 | convolution fusion | flops 2147483648 | bytes 19398656 | tf_op jit(solution)/shard_map/dot_general | solution.py:103
  80.0 0.0 reduce-scatter.2.cloned.1.call-update
  80.0 32.3 %reduce-scatter.2.cloned.1.call-done = f32[128,2048]{1,0:T(8,128)} async-done(((f32[128,4096]{1,0:T(8,128)}), f32[128,2048]{1,0:T(8,128)}) %reduce-scatter.2.cloned.1.call-update) | async-done | bytes 1048592 | tf_op jit(solution)/shard_map/reduce_scatter | solution.py:104
  112.3 1.3 convert_element_type.96
  113.6 1.5 %collective-permute-start.3 = (bf16[128,2048]{1,0:T(8,128)(2,1)S(1)}, bf16[128,2048]{1,0:T(8,128)(2,1)S(1)}, u32[]{:S(2)}, u32[]{:S(2)}) collective-permute-start(bf16[128,2048]{1,0:T(8,128)(2,1)S(1)} %convert_element_type.96), channel_id=1, source_target_pairs={{0,8},{8,16},{16,24},{24,0},{1,9},{9,17},{17,25},{25,1},{2,10},{10... | collective-permute-start | bytes 1572872 | tf_op jit(solution)/shard_map/ppermute | solution.py:22
  115.2 14.0 %collective-permute-done.3 = bf16[128,2048]{1,0:T(8,128)(2,1)S(1)} collective-permute-done((bf16[128,2048]{1,0:T(8,128)(2,1)S(1)}, bf16[128,2048]{1,0:T(8,128)(2,1)S(1)}, u32[]{:S(2)}, u32[]{:S(2)}) %collective-permute-start.3) | collective-permute-done | bytes 524320 | tf_op jit(solution)/shard_map/ppermute | solution.py:22
  129.1 0.8 copy.73
  (17 shorter events, 0.2 us)
Async XLA Ops:
  6.5 105.8 %reduce-scatter.2.cloned.1.call-start = ((), (), s32[]{:S(2)}) async-start(), calls=%async_computation.1 | async-start | bytes 3145728 | tf_op jit(solution)/shard_map/reduce_scatter | solution.py:104
  8.8 11.4 %copy-start = (bf16[1,128,4096]{2,1,0:T(8,128)(2,1)S(1)}, bf16[1,128,4096]{2,1,0:T(8,128)(2,1)}, u32[]{:S(2)}) copy-start(bf16[1,128,4096]{2,1,0:T(8,128)(2,1)} %param.6) | copy-start | bytes 3145732
  26.3 38.3 %collective-permute-start.2 = (bf16[128,1024]{0,1:T(8,128)(2,1)S(1)}, bf16[128,1024]{0,1:T(8,128)(2,1)S(1)}, u32[]{:S(2)}, u32[]{:S(2)}) collective-permute-start(bf16[128,1024]{0,1:T(8,128)(2,1)S(1)} %bitcast.215), channel_id=1, source_target_pairs={{0,2},{2,4},{4,6},{1,3},{3,5},{5,7},{8,10},{10,12},{12,14},{9,11},... | collective-permute-start | bytes 786440 | tf_op jit(solution)/shard_map/ppermute | solution.py:16
  28.7 36.0 %collective-permute-start.1 = (bf16[128,1024]{0,1:T(8,128)(2,1)S(1)}, bf16[128,1024]{0,1:T(8,128)(2,1)S(1)}, u32[]{:S(2)}, u32[]{:S(2)}) collective-permute-start(bf16[128,1024]{0,1:T(8,128)(2,1)S(1)} %bitcast.216), channel_id=1, source_target_pairs={{0,4},{2,6},{1,5},{3,7},{8,12},{10,14},{9,13},{11,15},{16,20},{18,... | collective-permute-start | bytes 786440 | tf_op jit(solution)/shard_map/ppermute | solution.py:16
  33.1 31.6 %collective-permute-start = (bf16[128,1024]{0,1:T(8,128)(2,1)S(1)}, bf16[128,1024]{0,1:T(8,128)(2,1)S(1)}, u32[]{:S(2)}, u32[]{:S(2)}) collective-permute-start(bf16[128,1024]{0,1:T(8,128)(2,1)S(1)} %bitcast.217), channel_id=1, source_target_pairs={{0,6},{1,7},{8,14},{9,15},{16,22},{17,23},{24,30},{25,31}} | collective-permute-start | bytes 786440 | tf_op jit(solution)/shard_map/ppermute | solution.py:16
  113.6 15.5 %collective-permute-start.3 = (bf16[128,2048]{1,0:T(8,128)(2,1)S(1)}, bf16[128,2048]{1,0:T(8,128)(2,1)S(1)}, u32[]{:S(2)}, u32[]{:S(2)}) collective-permute-start(bf16[128,2048]{1,0:T(8,128)(2,1)S(1)} %convert_element_type.96), channel_id=1, source_target_pairs={{0,8},{8,16},{16,24},{24,0},{1,9},{9,17},{17,25},{25,1},{2,10},{10... | collective-permute-start | bytes 1572872 | tf_op jit(solution)/shard_map/ppermute | solution.py:22
Sparse Core Ops, SparseCore 0:
  80.2 32.1 reduce-scatter.1
where the time goes:
time: 138 us; the launch traced here: 137 us
  waiting for transfers between devices  46.3 us (34%)
  local copies, waits for them, and re-layouts  33 us (24%)
  matrix products  29 us (21%)
  between operations  14.3 us (10%)
  starting transfers between devices  9.79 us (7%)
  other arithmetic  4.38 us (3%)
    reduce_scatter x1, waiting for transfers between devices, body(): lax.psum_scatter(head_term, 'tp', scatter_dimension=1, tiled=True)  32.3 us
    dot_general x1, local copies, waits for them, and re-layouts, body(): jnp.dot(normed, query_weight[0], preferred_element_type=jnp.float32)  20.7 us
    ppermute x1, waiting for transfers between devices, passed_along(): return lax.ppermute(value, axis, pairs)  14 us
    dot_general x1, local copies, waits for them, and re-layouts, body(): jnp.dot(normed, keyval_weight[0], preferred_element_type=jnp.float32)  11.4 us
    dot_general x1, matrix products, body(): jnp.dot(attn, output_weight[0], preferred_element_type=jnp.float32)  9.51 us
    ppermute x3, starting transfers between devices, from_behind(): lax.ppermute(value, axis, [(source, source + steps) for source in range(i...  8.27 us
    dot_general x1, matrix products, body(): jnp.dot(normed, query_weight[0], preferred_element_type=jnp.float32)  8.21 us
    dot_general x1, matrix products, body(): jnp.dot(normed, keyval_weight[0], preferred_element_type=jnp.float32)  5.78 us
  transfers between devices with their start and end apart: 5, of which 2 were waited for; matrix products, arithmetic and copies ran while one was open for 21% of the time, Pallas kernels for 0%

commit v1 on v0

v1 whole, which is shorter than its diff:
```python
import functools

import jax
import jax.numpy as jnp
import numpy as np
from jax import lax
from jax.experimental import pallas as pl
from jax.experimental.pallas import tpu as pltpu
from jax.sharding import PartitionSpec as P

HD = 128
REACH = 3
NORM_EPS = 1e-05
CHUNKS = 4
VMEM_BYTES = 48 * 1024 * 1024

ANY = pl.BlockSpec(memory_space=pl.ANY)
VMEM = pl.BlockSpec(memory_space=pltpu.VMEM)
SMEM = pl.BlockSpec(memory_space=pltpu.SMEM)


def rotary_tables(tokens):
    half = HD // 2
    inverse = 10000.0 ** (-np.arange(half, dtype=np.float32) / np.float32(half))
    angles = np.arange(tokens, dtype=np.float32)[:, None] * inverse.astype(np.float32)[None, :]
    cosine = np.cos(angles.astype(np.float64)).astype(np.float32)
    sine = np.sin(angles.astype(np.float64)).astype(np.float32)
    return np.concatenate([cosine, cosine, -sine, sine], axis=1)


def turned(head, table):
    return head * table[:, :HD] + pltpu.roll(head, HD // 2, 1) * table[:, HD:]


def table_copy(table_hbm, table, sem):
    rows = table.shape[0]
    first = pl.multiple_of(lax.axis_index("ctx") * rows, 8)
    return pltpu.make_async_copy(table_hbm.at[pl.ds(first, rows)], table, sem)


def column_copies(weight_hbm, weight, sems, width):
    return [
        pltpu.make_async_copy(
            weight_hbm.at[0, :, pl.ds(k * width, width)],
            weight.at[:, pl.ds(k * width, width)],
            sems.at[k],
        )
        for k in range(weight.shape[1] // width)
    ]


def keyval_kernel(
    hidden_hbm, gain_ref, table_hbm, weight_hbm, kv_ref, normed_ref, hidden, table, weight, sems, wsems
):
    hidden_copy = pltpu.make_async_copy(hidden_hbm.at[0], hidden, sems.at[0])
    hidden_copy.start()
    copies = column_copies(weight_hbm, weight, wsems, 2 * HD)
    for copy in copies:
        copy.start()
    tcopy = table_copy(table_hbm, table, sems.at[1])
    tcopy.start()
    hidden_copy.wait()
    rows = hidden.shape[0]
    gain = gain_ref[...].astype(jnp.float32)

    @pl.loop(0, rows // 16)
    def _(at):
        span = pl.ds(pl.multiple_of(at * 16, 16), 16)
        wide = hidden[span, :].astype(jnp.float32)
        square = jnp.mean(wide * wide, axis=1, keepdims=True)
        normed_ref[span, :] = (wide * lax.rsqrt(square + NORM_EPS) * gain).astype(jnp.bfloat16)

    tcopy.wait()
    turn = table[...]
    for k, copy in enumerate(copies):
        copy.wait()
        both = jnp.dot(
            normed_ref[...], weight[:, 2 * HD * k : 2 * HD * (k + 1)], preferred_element_type=jnp.float32
        )
        kv_ref[:, 2 * HD * k : 2 * HD * k + HD] = turned(both[:, :HD], turn).astype(jnp.bfloat16)
        kv_ref[:, 2 * HD * k + HD : 2 * HD * (k + 1)] = both[:, HD:].astype(jnp.bfloat16)


def query_kernel(normed_ref, table_hbm, weight_hbm, query_ref, table, weight, sems, wsems):
    copies = column_copies(weight_hbm, weight, wsems, 2 * HD)
    for copy in copies:
        copy.start()
    tcopy = table_copy(table_hbm, table, sems.at[0])
    tcopy.start()
    tcopy.wait()
    turn = table[...]
    for k, copy in enumerate(copies):
        copy.wait()
        both = jnp.dot(
            normed_ref[...], weight[:, 2 * HD * k : 2 * HD * (k + 1)], preferred_element_type=jnp.float32
        )
        for part in range(2):
            at = 2 * HD * k + HD * part
            query_ref[:, at : at + HD] = turned(both[:, HD * part : HD * (part + 1)], turn).astype(
                jnp.bfloat16
            )


def output_copies(weight_hbm, weight, sems, places, width):
    return [
        pltpu.make_async_copy(
            weight_hbm.at[0, :, pl.ds(pl.multiple_of(place, 128), width)],
            weight.at[:, pl.ds(k * width, width)],
            sems.at[k],
        )
        for k, place in enumerate(places)
    ]


def peer_place(steps, half):
    count = lax.axis_size("tp")
    return lax.rem(lax.axis_index("tp") + steps, count) * half


def attend_kernel(block_count, half, width, *refs):
    window_ref, query_ref = refs[:2]
    kv_refs = refs[2 : 2 + block_count]
    weight_hbm = refs[2 + block_count]
    peers = lax.axis_size("tp") - 1
    attn_ref = refs[3 + block_count]
    send_refs = refs[4 + block_count : 4 + block_count + peers]
    weight, wsems = refs[4 + block_count + peers :]
    copies = output_copies(
        weight_hbm, weight, wsems, [peer_place(d, half) for d in range(1, peers + 1)], width
    )
    for copy in copies:
        copy.start()
    rows = query_ref.shape[0]
    kv_count = kv_refs[0].shape[1] // (2 * HD)
    group = query_ref.shape[1] // HD // kv_count
    ctx = lax.axis_index("ctx")
    twin = ctx + 1 - 2 * lax.rem(ctx, 2)
    blocks = [ctx, twin, ctx - 2, twin - 2, twin - 4][:block_count]
    row = lax.broadcasted_iota(jnp.int32, (rows, rows), 0)
    column = lax.broadcasted_iota(jnp.int32, (rows, rows), 1)
    masks = []
    for block in blocks:
        distance = row - column + (ctx - block) * rows
        masks.append((distance >= 0) & (distance < window_ref[0]) & (block >= 0))
    inside = jnp.concatenate(masks, axis=1)[None]
    for g in range(kv_count):
        queries = jnp.concatenate(
            [query_ref[:, HD * (group * g + h) : HD * (group * g + h + 1)] for h in range(group)], axis=0
        )
        keys = jnp.concatenate([r[:, 2 * HD * g : 2 * HD * g + HD] for r in kv_refs], axis=0)
        values = jnp.concatenate([r[:, 2 * HD * g + HD : 2 * HD * (g + 1)] for r in kv_refs], axis=0)
        scores = lax.dot_general(
            queries, keys, (((1,), (1,)), ((), ())), preferred_element_type=jnp.float32
        ).reshape(group, rows, block_count * rows)
        scores = jnp.where(inside, scores * HD ** (-0.5), jnp.float32(-1e30))
        highest = jnp.max(scores, axis=2, keepdims=True)
        expo = jnp.exp(scores - highest)
        total = jnp.sum(expo, axis=2, keepdims=True)
        probs = (expo * (1.0 / total)).astype(jnp.bfloat16).reshape(group * rows, block_count * rows)
        out = jnp.dot(probs, values, preferred_element_type=jnp.float32).astype(jnp.bfloat16)
        for h in range(group):
            at = HD * (group * g + h)
            attn_ref[:, at : at + HD] = out[h * rows : (h + 1) * rows]
    for d in range(peers):
        copies[d].wait()
        send_refs[d][...] = jnp.dot(
            attn_ref[...], weight[:, d * width : (d + 1) * width], preferred_element_type=jnp.float32
        ).astype(jnp.bfloat16)


def peers_kernel(half, width, chunks, attn_ref, weight_hbm, *refs):
    peers = lax.axis_size("tp") - 1
    count = peers * len(chunks)
    send_refs = refs[:count]
    weight, wsems = refs[count:]
    copies = output_copies(
        weight_hbm,
        weight,
        wsems,
        [peer_place(d, half) + j * width for j in chunks for d in range(1, peers + 1)],
        width,
    )
    for copy in copies:
        copy.start()
    for k in range(count):
        copies[k].wait()
        send_refs[k][...] = jnp.dot(
            attn_ref[...], weight[:, k * width : (k + 1) * width], preferred_element_type=jnp.float32
        ).astype(jnp.bfloat16)


def own_kernel(half, width, attn_ref, weight_hbm, after_ref, own_ref, weight, wsems):
    count = half // width
    copies = output_copies(
        weight_hbm, weight, wsems, [peer_place(0, half) + k * width for k in range(count)], width
    )
    for copy in copies:
        copy.start()
    for k in range(count):
        copies[k].wait()
        own_ref[:, k * width : (k + 1) * width] = jnp.dot(
            attn_ref[...], weight[:, k * width : (k + 1) * width], preferred_element_type=jnp.float32
        )


def call(kernel, name, outs, in_specs, scratch, flops, moved):
    return pl.pallas_call(
        kernel,
        out_shape=outs,
        in_specs=in_specs,
        out_specs=jax.tree.map(lambda _: VMEM, outs),
        scratch_shapes=scratch,
        compiler_params=pltpu.CompilerParams(vmem_limit_bytes=VMEM_BYTES),
        cost_estimate=pl.CostEstimate(flops=flops, bytes_accessed=moved, transcendentals=0),
        name=name,
    )


def moved_by(value, axis, steps):
    count = lax.axis_size(axis)
    return lax.ppermute(value, axis, [(source, (source + steps) % count) for source in range(count)])


def twins(value):
    count = lax.axis_size("ctx")
    return lax.ppermute(value, "ctx", [(source, source ^ 1) for source in range(count)])


def body(hidden_in, norm_gain, query_weight, keyval_weight, output_weight, windows):
    bf16, f32 = jnp.bfloat16, jnp.float32
    dma = pltpu.SemaphoreType.DMA
    _, rows, features = hidden_in.shape
    query_columns = query_weight.shape[2]
    kv_columns = keyval_weight.shape[2]
    ctx_count = lax.axis_size("ctx")
    tp_count = lax.axis_size("tp")
    assert ctx_count % 2 == 0
    table = jnp.asarray(rotary_tables(rows * ctx_count))
    own_kv, normed = call(
        keyval_kernel,
        "keyval",
        (jax.ShapeDtypeStruct((rows, kv_columns), bf16), jax.ShapeDtypeStruct((rows, features), bf16)),
        [ANY, VMEM, ANY, ANY],
        [
            pltpu.VMEM((rows, features), bf16),
            pltpu.VMEM((rows, 2 * HD), f32),
            pltpu.VMEM((features, kv_columns), bf16),
            dma((2,)),
            dma((kv_columns // (2 * HD),)),
        ],
        2 * rows * features * kv_columns,
        2 * features * kv_columns,
    )(hidden_in, norm_gain, table, keyval_weight)
    behind = moved_by(own_kv, "ctx", 2)
    beside = twins(own_kv)
    queries = call(
        query_kernel,
        "query",
        jax.ShapeDtypeStruct((rows, query_columns), bf16),
        [VMEM, ANY, ANY],
        [
            pltpu.VMEM((rows, 2 * HD), f32),
            pltpu.VMEM((features, query_columns), bf16),
            dma((1,)),
            dma((query_columns // (2 * HD),)),
        ],
        2 * rows * features * query_columns,
        2 * features * query_columns,
    )(normed, table, query_weight)
    behind_beside = twins(behind)
    kv_list = [own_kv, beside, behind, behind_beside]
    if ctx_count > 4:
        kv_list.append(moved_by(behind_beside, "ctx", 2))
    out_columns = output_weight.shape[2]
    half = out_columns // tp_count
    width = half // CHUNKS
    peers = tp_count - 1
    send = jax.ShapeDtypeStruct((rows, width), bf16)
    attn, *first = call(
        functools.partial(attend_kernel, len(kv_list), half, width),
        "attend",
        [jax.ShapeDtypeStruct((rows, query_columns), bf16)] + [send] * peers,
        [SMEM, VMEM] + [VMEM] * len(kv_list) + [ANY],
        [pltpu.VMEM((query_columns, peers * width), bf16), dma((peers,))],
        2 * rows * query_columns * width,
        2 * query_columns * width,
    )(windows, queries, *kv_list, output_weight)
    later = range(1, CHUNKS)
    rest = call(
        functools.partial(peers_kernel, half, width, later),
        "peers",
        [send] * (peers * len(later)),
        [VMEM, ANY],
        [pltpu.VMEM((query_columns, peers * len(later) * width), bf16), dma((peers * len(later),))],
        2 * rows * query_columns * width * len(later) * peers,
        2 * query_columns * width * len(later) * peers,
    )(attn, output_weight)
    own = call(
        functools.partial(own_kernel, half, width),
        "own",
        jax.ShapeDtypeStruct((rows, half), f32),
        [VMEM, ANY, ANY],
        [pltpu.VMEM((query_columns, half), bf16), dma((CHUNKS,))],
        2 * rows * query_columns * half,
        2 * query_columns * half,
    )(attn, output_weight, rest[-1])
    sends = list(first) + list(rest)
    pieces = []
    for j in range(CHUNKS):
        total = own[:, j * width : (j + 1) * width]
        for d in range(peers):
            total = total + moved_by(sends[j * peers + d], "tp", d + 1).astype(f32)
        pieces.append(moved_by(total.astype(bf16), "segment", 1))
    return jnp.concatenate(pieces, axis=1)[None]


def solution(mesh):
    in_specs = (
        P("segment", "ctx", None),
        P("segment", None),
        P("segment", None, "tp"),
        P("segment", None, "tp"),
        P("segment", "tp", None),
        P("segment"),
    )
    out_specs = P("segment", "ctx", "tp")
    return jax.shard_map(body, mesh=mesh, in_specs=in_specs, out_specs=out_specs, check_vma=False)
```

time: 138 us -> 63.6 us (0.46)
  matrix products: 29 us -> 0 us
  local copies, waits for them, and re-layouts: 33 us -> 4.02 us
  waiting for transfers between devices: 46.3 us -> 21.4 us
  Pallas kernels: 0 us -> 23.9 us
  between operations: 14.3 us -> 0.74 us
  other arithmetic: 4.38 us -> 1.01 us
  starting transfers between devices: 9.79 us -> 12.2 us
    reduce_scatter x1 -> x0, waiting for transfers between devices: 32.3 us -> none  [body(): lax.psum_scatter(head_term, 'tp', scatter_dimension=1, tiled=True)]
    dot_general x2 -> x0, local copies, waits for them, and re-layouts: 32.1 us -> none  [the longest x1 20.7 us: body(): jnp.dot(normed, query_weight[0], preferred_element_type=jnp.float32)]
    dot_general x7 -> x0, matrix products: 26.6 us -> none  [the longest x1 9.51 us: body(): jnp.dot(attn, output_weight[0], preferred_element_type=jnp.float32)]
    pallas_call x0 -> x5, Pallas kernels: none -> 23.9 us  [the longest x1 7.78 us: body(): call(query_kernel, 'query', jax.ShapeDtypeStruct((rows, query_columns), b...]
    ppermute x4 -> x11, waiting for transfers between devices: 14 us -> 21.4 us  [the longest x9 21.4 us: moved_by(): lax.ppermute(value, axis, [(source, (source + steps) % count) for source...]
    unnamed x3 -> x8, local copies, waits for them, and re-layouts: 0.8 us -> 4.02 us
    ppermute x4 -> x11, starting transfers between devices: 9.79 us -> 12.2 us  [the longest x9 12.2 us: moved_by(): lax.ppermute(value, axis, [(source, (source + steps) % count) for source...]
    sub x4 -> x0, matrix products: 2.38 us -> none  [attend(): expo = jnp.where(inside, jnp.exp(scores - highest), jnp.float32(0.0))]
  transfers between devices with their start and end apart: 5 -> 11, of which waited for: 2 -> 7; matrix products, arithmetic and copies ran while one was open for 21% -> 0% of each run, Pallas kernels for 0% -> 24%
where the time goes in v1:
time: 63.6 us; the launch traced here: 63.2 us
  Pallas kernels  23.9 us (38%)
  waiting for transfers between devices  21.4 us (34%)
  starting transfers between devices  12.2 us (19%)
  local copies, waits for them, and re-layouts  4.02 us (6%)
  other arithmetic  1.01 us (2%)
  between operations  0.74 us (1%)
    ppermute x9, waiting for transfers between devices, moved_by(): lax.ppermute(value, axis, [(source, (source + steps) % count) for source...  21.4 us
    ppermute x9, starting transfers between devices, moved_by(): lax.ppermute(value, axis, [(source, (source + steps) % count) for source...  12.2 us
    pallas_call x1, Pallas kernels, body(): call(query_kernel, 'query', jax.ShapeDtypeStruct((rows, query_columns), b...  7.78 us
    pallas_call x1, Pallas kernels, body(): call(keyval_kernel, 'keyval', (jax.ShapeDtypeStruct((rows, kv_columns), b...  4.75 us
    unnamed x8, local copies, waits for them, and re-layouts  4.02 us
    pallas_call x1, Pallas kernels, body(): call(functools.partial(own_kernel, half, width), 'own', jax.ShapeDtypeStr...  4 us
    pallas_call x1, Pallas kernels, body(): call(functools.partial(attend_kernel, len(kv_list), half, width), 'attend...  3.99 us
    pallas_call x1, Pallas kernels, body(): call(functools.partial(peers_kernel, half, width, later), 'peers', [send]...  3.36 us
  transfers between devices with their start and end apart: 11, of which 7 were waited for; matrix products, arithmetic and copies ran while one was open for 0% of the time, Pallas kernels for 24%

profile of v1, /device:TPU:0, one launch (start us, length us, event | category | flops | bytes accessed | tf_op | source)
XLA Modules:
  0.0 63.2 jit_solution(5613042883803396405)
XLA Ops:
  0.0 1.0 %copy-done = f32[512,256]{1,0:T(8,128)S(1)} copy-done((f32[512,256]{1,0:T(8,128)S(1)}, f32[512,256]{1,0:T(8,128)}, u32[]{:S(2)}) %copy-start) | copy-done | bytes 524312
  1.0 1.2 %copy-done.2 = bf16[1,128,4096]{2,1,0:T(8,128)(2,1)S(1)} copy-done((bf16[1,128,4096]{2,1,0:T(8,128)(2,1)S(1)}, bf16[1,128,4096]{2,1,0:T(8,128)(2,1)}, u32[]{:S(2)}) %copy-start.2) | copy-done | bytes 1048600
  2.3 0.7 %copy-done.3 = bf16[1,4096]{1,0:T(2,128)(2,1)S(1)} copy-done((bf16[1,4096]{1,0:T(2,128)(2,1)S(1)}, bf16[1,4096]{1,0:T(2,128)(2,1)}, u32[]{:S(2)}) %copy-start.3) | copy-done | bytes 8216
  3.0 4.8 %keyval.1 = (bf16[128,1024]{1,0:T(8,128)(2,1)S(1)}, bf16[128,4096]{1,0:T(8,128)(2,1)S(1)}) custom-call(bf16[1,128,4096]{2,1,0:T(8,128)(2,1)S(1)} %copy-done.2, bf16[1,4096]{1,0:T(2,128)(2,1)S(1)} %copy-done.3, f32[512,256]{1,0:T(8,128)S(1)} %copy-done, bf16[1,4096,1024]{2,1,0:T(8,128)(2,1)} %weight_hbm.4), custom_call_target="tpu_custom_call" | custom-call | flops 1073741824 | bytes 8388608 | tf_op jit(solution)/shard_map/keyval/pallas_call | solution.py:239
  7.7 3.0 %collective-permute-start.1 = (bf16[128,1024]{1,0:T(8,128)(2,1)S(1)}, bf16[128,1024]{1,0:T(8,128)(2,1)S(1)}, u32[]{:S(2)}, u32[]{:S(2)}) collective-permute-start(bf16[128,1024]{1,0:T(8,128)(2,1)S(1)} %get-tuple-element.13.refs_2_), channel_id=1, source_target_pairs={{0,4},{2,6},{4,0},{6,2},{1,5},{3,7},{5,1},{7,3},{8,12},{10,14},{12... | collective-permute-start | bytes 786440 | tf_op jit(solution)/shard_map/ppermute | solution.py:221
  10.8 0.0 collective-permute-start
  10.8 6.3 %collective-permute-done.1.refs_4_ = bf16[128,1024]{1,0:T(8,128)(2,1)S(1)} collective-permute-done((bf16[128,1024]{1,0:T(8,128)(2,1)S(1)}, bf16[128,1024]{1,0:T(8,128)(2,1)S(1)}, u32[]{:S(2)}, u32[]{:S(2)}) %collective-permute-start.1) | collective-permute-done | bytes 262176 | tf_op jit(solution)/shard_map/ppermute | solution.py:221
  17.1 0.0 collective-permute-start.2
  17.7 0.0 copy-start.1
  17.7 1.0 %copy-done.1 = f32[512,256]{1,0:T(8,128)S(1)} copy-done((f32[512,256]{1,0:T(8,128)S(1)}, f32[512,256]{1,0:T(8,128)}, u32[]{:S(2)}) %copy-start.1) | copy-done | bytes 524312
  18.8 7.8 %query.1.refs_1_ = bf16[128,2048]{1,0:T(8,128)(2,1)S(1)} custom-call(bf16[128,4096]{1,0:T(8,128)(2,1)S(1)} %get-tuple-element.12.normed_ref, f32[512,256]{1,0:T(8,128)S(1)} %copy-done.1, bf16[1,4096,2048]{2,1,0:T(8,128)(2,1)} %weight_hbm.5), custom_call_target="tpu_custom_call" | custom-call | flops 2147483648 | bytes 16777216 | tf_op jit(solution)/shard_map/query/pallas_call | solution.py:256
  26.5 0.0 collective-permute-done.refs_3_
  26.6 4.0 %attend.1 = (bf16[128,2048]{1,0:T(8,128)(2,1)S(1)}, bf16[128,512]{1,0:T(8,128)(2,1)S(1)}) custom-call(s32[1]{0:T(128)S(6)} %copy.8.refs_0_, bf16[128,2048]{1,0:T(8,128)(2,1)S(1)} %query.1.refs_1_, bf16[128,1024]{1,0:T(8,128)(2,1)S(1)} %get-tuple-element.13.refs_2_, bf16[128,1024]{1,0:T(8,128)(2,1)S(1)} %collective-permute-done.refs_3_, ...), custom_call_target="tpu_custom_call" | custom-call | flops 268435456 | bytes 2097152 | tf_op jit(solution)/shard_map/attend/pallas_call | solution.py:279
  30.6 1.8 %collective-permute-start.3 = (bf16[128,512]{1,0:T(8,128)(2,1)S(1)}, bf16[128,512]{1,0:T(8,128)(2,1)S(1)}, u32[]{:S(2)}, u32[]{:S(2)}) collective-permute-start(bf16[128,512]{1,0:T(8,128)(2,1)S(1)} %get-tuple-element.16), channel_id=1, source_target_pairs={{0,1},{1,0},{2,3},{3,2},{4,5},{5,4},{6,7},{7,6},{8,9},{9,8},{10,11... | collective-permute-start | bytes 393224 | tf_op jit(solution)/shard_map/ppermute | solution.py:221
  32.4 3.4 %peers.1 = (bf16[128,512]{1,0:T(8,128)(2,1)S(1)}, bf16[128,512]{1,0:T(8,128)(2,1)S(1)}, bf16[128,512]{1,0:T(8,128)(2,1)S(1)}) custom-call(bf16[128,2048]{1,0:T(8,128)(2,1)S(1)} %get-tuple-element.14.attn_ref, bf16[1,2048,4096]{2,1,0:T(8,128)(2,1)} %weight_hbm.7), custom_call_target="tpu_custom_call" | custom-call | flops 805306368 | bytes 6291456 | tf_op jit(solution)/shard_map/peers/pallas_call | solution.py:289
  35.8 0.3 collective-permute-start.5
  36.1 1.8 %collective-permute-start.7 = (bf16[128,512]{1,0:T(8,128)(2,1)S(1)}, bf16[128,512]{1,0:T(8,128)(2,1)S(1)}, u32[]{:S(2)}, u32[]{:S(2)}) collective-permute-start(bf16[128,512]{1,0:T(8,128)(2,1)S(1)} %get-tuple-element.18), channel_id=1, source_target_pairs={{0,1},{1,0},{2,3},{3,2},{4,5},{5,4},{6,7},{7,6},{8,9},{9,8},{10,11... | collective-permute-start | bytes 393224 | tf_op jit(solution)/shard_map/ppermute | solution.py:221
  37.9 0.3 collective-permute-start.9
  38.1 4.0 %own.1 = f32[128,2048]{1,0:T(8,128)S(1)} custom-call(bf16[128,2048]{1,0:T(8,128)(2,1)S(1)} %get-tuple-element.14.attn_ref, bf16[1,2048,4096]{2,1,0:T(8,128)(2,1)} %weight_hbm.7, bf16[128,512]{1,0:T(8,128)(2,1)S(1)} %get-tuple-element.15.after_ref), custom_call_target="tpu_custom_call" | custom-call | flops 1073741824 | bytes 8388608 | tf_op jit(solution)/shard_map/own/pallas_call | solution.py:298
  42.1 0.0 collective-permute-done.5
  42.2 2.8 %collective-permute-done.7 = bf16[128,512]{1,0:T(8,128)(2,1)S(1)} collective-permute-done((bf16[128,512]{1,0:T(8,128)(2,1)S(1)}, bf16[128,512]{1,0:T(8,128)(2,1)S(1)}, u32[]{:S(2)}, u32[]{:S(2)}) %collective-permute-start.7) | collective-permute-done | bytes 131104 | tf_op jit(solution)/shard_map/ppermute | solution.py:221
  45.0 2.1 %collective-permute-done.9 = bf16[128,512]{1,0:T(8,128)(2,1)S(1)} collective-permute-done((bf16[128,512]{1,0:T(8,128)(2,1)S(1)}, bf16[128,512]{1,0:T(8,128)(2,1)S(1)}, u32[]{:S(2)}, u32[]{:S(2)}) %collective-permute-start.9) | collective-permute-done | bytes 131104 | tf_op jit(solution)/shard_map/ppermute | solution.py:221
  47.1 0.2 fusion.3
  47.2 1.6 %collective-permute-start.4 = (bf16[128,512]{1,0:T(8,128)(2,1)S(1)}, bf16[128,512]{1,0:T(8,128)(2,1)S(1)}, u32[]{:S(2)}, u32[]{:S(2)}) collective-permute-start(bf16[128,512]{1,0:T(8,128)(2,1)S(1)} %get-tuple-element.19), channel_id=1, source_target_pairs={{0,8},{8,16},{16,24},{24,0},{1,9},{9,17},{17,25},{25,1},{2,10},{10... | collective-permute-start | bytes 393224 | tf_op jit(solution)/shard_map/ppermute | solution.py:221
  48.9 1.6 %collective-permute-start.10 = (bf16[128,512]{1,0:T(8,128)(2,1)S(1)}, bf16[128,512]{1,0:T(8,128)(2,1)S(1)}, u32[]{:S(2)}, u32[]{:S(2)}) collective-permute-start(bf16[128,512]{1,0:T(8,128)(2,1)S(1)} %get-tuple-element.20), channel_id=1, source_target_pairs={{0,8},{8,16},{16,24},{24,0},{1,9},{9,17},{17,25},{25,1},{2,10},{10... | collective-permute-start | bytes 393224 | tf_op jit(solution)/shard_map/ppermute | solution.py:221
  50.5 1.6 %collective-permute-start.8 = (bf16[128,512]{1,0:T(8,128)(2,1)S(1)}, bf16[128,512]{1,0:T(8,128)(2,1)S(1)}, u32[]{:S(2)}, u32[]{:S(2)}) collective-permute-start(bf16[128,512]{1,0:T(8,128)(2,1)S(1)} %get-tuple-element.21), channel_id=1, source_target_pairs={{0,8},{8,16},{16,24},{24,0},{1,9},{9,17},{17,25},{25,1},{2,10},{10... | collective-permute-start | bytes 393224 | tf_op jit(solution)/shard_map/ppermute | solution.py:221
  52.0 0.2 collective-permute-start.6
  52.3 3.3 %collective-permute-done.4 = bf16[128,512]{1,0:T(8,128)(2,1)S(1)} collective-permute-done((bf16[128,512]{1,0:T(8,128)(2,1)S(1)}, bf16[128,512]{1,0:T(8,128)(2,1)S(1)}, u32[]{:S(2)}, u32[]{:S(2)}) %collective-permute-start.4) | collective-permute-done | bytes 131104 | tf_op jit(solution)/shard_map/ppermute | solution.py:221
  55.5 2.8 %collective-permute-done.10 = bf16[128,512]{1,0:T(8,128)(2,1)S(1)} collective-permute-done((bf16[128,512]{1,0:T(8,128)(2,1)S(1)}, bf16[128,512]{1,0:T(8,128)(2,1)S(1)}, u32[]{:S(2)}, u32[]{:S(2)}) %collective-permute-start.10) | collective-permute-done | bytes 131104 | tf_op jit(solution)/shard_map/ppermute | solution.py:221
  58.3 2.6 %collective-permute-done.8 = bf16[128,512]{1,0:T(8,128)(2,1)S(1)} collective-permute-done((bf16[128,512]{1,0:T(8,128)(2,1)S(1)}, bf16[128,512]{1,0:T(8,128)(2,1)S(1)}, u32[]{:S(2)}, u32[]{:S(2)}) %collective-permute-start.8) | collective-permute-done | bytes 131104 | tf_op jit(solution)/shard_map/ppermute | solution.py:221
  61.0 1.4 %collective-permute-done.6 = bf16[128,512]{1,0:T(8,128)(2,1)S(1)} collective-permute-done((bf16[128,512]{1,0:T(8,128)(2,1)S(1)}, bf16[128,512]{1,0:T(8,128)(2,1)S(1)}, u32[]{:S(2)}, u32[]{:S(2)}) %collective-permute-start.6) | collective-permute-done | bytes 131104 | tf_op jit(solution)/shard_map/ppermute | solution.py:221
  62.4 0.8 %maximum_bitcast_fusion = bf16[1,128,2048]{2,1,0:T(8,128)(2,1)} fusion(bf16[128,512]{1,0:T(8,128)(2,1)S(1)} %collective-permute-done.10, bf16[128,512]{1,0:T(8,128)(2,1)S(1)} %collective-permute-done.8, bf16[128,512]{1,0:T(8,128)(2,1)S(1)} %collective-permute-done.6, bf16[128,512]{1,0:T(8,128)(2,1)S(1)} %collective-permute-done.4), kind=kLoop, calls=%fused_computation | loop fusion | flops 2097152 | bytes 1048576 | tf_op jit(solution)/shard_map/broadcast_in_dim | solution.py:314
  (5 shorter events, 0.0 us)
Async XLA Ops:
  0.0 1.0 %copy-start = (f32[512,256]{1,0:T(8,128)S(1)}, f32[512,256]{1,0:T(8,128)}, u32[]{:S(2)}) copy-start(f32[512,256]{1,0:T(8,128)} %constant.2.clone.table_hbm) | copy-start | bytes 1572868
  1.0 1.2 %copy-start.2 = (bf16[1,128,4096]{2,1,0:T(8,128)(2,1)S(1)}, bf16[1,128,4096]{2,1,0:T(8,128)(2,1)}, u32[]{:S(2)}) copy-start(bf16[1,128,4096]{2,1,0:T(8,128)(2,1)} %hidden_hbm.1) | copy-start | bytes 3145732
  2.3 0.7 %copy-start.3 = (bf16[1,4096]{1,0:T(2,128)(2,1)S(1)}, bf16[1,4096]{1,0:T(2,128)(2,1)}, u32[]{:S(2)}) copy-start(bf16[1,4096]{1,0:T(2,128)(2,1)} %gain_ref.1) | copy-start | bytes 24580
  7.7 9.3 %collective-permute-start.1 = (bf16[128,1024]{1,0:T(8,128)(2,1)S(1)}, bf16[128,1024]{1,0:T(8,128)(2,1)S(1)}, u32[]{:S(2)}, u32[]{:S(2)}) collective-permute-start(bf16[128,1024]{1,0:T(8,128)(2,1)S(1)} %get-tuple-element.13.refs_2_), channel_id=1, source_target_pairs={{0,4},{2,6},{4,0},{6,2},{1,5},{3,7},{5,1},{7,3},{8,12},{10,14},{12... | collective-permute-start | bytes 786440 | tf_op jit(solution)/shard_map/ppermute | solution.py:221
  10.8 15.8 %collective-permute-start = (bf16[128,1024]{1,0:T(8,128)(2,1)S(1)}, bf16[128,1024]{1,0:T(8,128)(2,1)S(1)}, u32[]{:S(2)}, u32[]{:S(2)}) collective-permute-start(bf16[128,1024]{1,0:T(8,128)(2,1)S(1)} %get-tuple-element.13.refs_2_), channel_id=1, source_target_pairs={{0,2},{2,0},{4,6},{6,4},{1,3},{3,1},{5,7},{7,5},{8,10},{10,8},{12,... | collective-permute-start | bytes 786440 | tf_op jit(solution)/shard_map/ppermute | solution.py:226
  17.1 9.5 %collective-permute-start.2 = (bf16[128,1024]{1,0:T(8,128)(2,1)S(1)}, bf16[128,1024]{1,0:T(8,128)(2,1)S(1)}, u32[]{:S(2)}, u32[]{:S(2)}) collective-permute-start(bf16[128,1024]{1,0:T(8,128)(2,1)S(1)} %collective-permute-done.1.refs_4_), channel_id=1, source_target_pairs={{0,2},{2,0},{4,6},{6,4},{1,3},{3,1},{5,7},{7,5},{8,10},{10,8},{12,... | collective-permute-start | bytes 786440 | tf_op jit(solution)/shard_map/ppermute | solution.py:226
  17.7 1.0 %copy-start.1 = (f32[512,256]{1,0:T(8,128)S(1)}, f32[512,256]{1,0:T(8,128)}, u32[]{:S(2)}) copy-start(f32[512,256]{1,0:T(8,128)} %constant.2.clone.table_hbm) | copy-start | bytes 1572868
  30.6 11.6 %collective-permute-start.3 = (bf16[128,512]{1,0:T(8,128)(2,1)S(1)}, bf16[128,512]{1,0:T(8,128)(2,1)S(1)}, u32[]{:S(2)}, u32[]{:S(2)}) collective-permute-start(bf16[128,512]{1,0:T(8,128)(2,1)S(1)} %get-tuple-element.16), channel_id=1, source_target_pairs={{0,1},{1,0},{2,3},{3,2},{4,5},{5,4},{6,7},{7,6},{8,9},{9,8},{10,11... | collective-permute-start | bytes 393224 | tf_op jit(solution)/shard_map/ppermute | solution.py:221
  35.8 6.4 %collective-permute-start.5 = (bf16[128,512]{1,0:T(8,128)(2,1)S(1)}, bf16[128,512]{1,0:T(8,128)(2,1)S(1)}, u32[]{:S(2)}, u32[]{:S(2)}) collective-permute-start(bf16[128,512]{1,0:T(8,128)(2,1)S(1)} %get-tuple-element.17), channel_id=1, source_target_pairs={{0,1},{1,0},{2,3},{3,2},{4,5},{5,4},{6,7},{7,6},{8,9},{9,8},{10,11... | collective-permute-start | bytes 393224 | tf_op jit(solution)/shard_map/ppermute | solution.py:221
  36.1 8.9 %collective-permute-start.7 = (bf16[128,512]{1,0:T(8,128)(2,1)S(1)}, bf16[128,512]{1,0:T(8,128)(2,1)S(1)}, u32[]{:S(2)}, u32[]{:S(2)}) collective-permute-start(bf16[128,512]{1,0:T(8,128)(2,1)S(1)} %get-tuple-element.18), channel_id=1, source_target_pairs={{0,1},{1,0},{2,3},{3,2},{4,5},{5,4},{6,7},{7,6},{8,9},{9,8},{10,11... | collective-permute-start | bytes 393224 | tf_op jit(solution)/shard_map/ppermute | solution.py:221
  37.9 9.2 %collective-permute-start.9 = (bf16[128,512]{1,0:T(8,128)(2,1)S(1)}, bf16[128,512]{1,0:T(8,128)(2,1)S(1)}, u32[]{:S(2)}, u32[]{:S(2)}) collective-permute-start(bf16[128,512]{1,0:T(8,128)(2,1)S(1)} %get-tuple-element.15.after_ref), channel_id=1, source_target_pairs={{0,1},{1,0},{2,3},{3,2},{4,5},{5,4},{6,7},{7,6},{8,9},{9,8},{10,11... | collective-permute-start | bytes 393224 | tf_op jit(solution)/shard_map/ppermute | solution.py:221
  47.2 8.3 %collective-permute-start.4 = (bf16[128,512]{1,0:T(8,128)(2,1)S(1)}, bf16[128,512]{1,0:T(8,128)(2,1)S(1)}, u32[]{:S(2)}, u32[]{:S(2)}) collective-permute-start(bf16[128,512]{1,0:T(8,128)(2,1)S(1)} %get-tuple-element.19), channel_id=1, source_target_pairs={{0,8},{8,16},{16,24},{24,0},{1,9},{9,17},{17,25},{25,1},{2,10},{10... | collective-permute-start | bytes 393224 | tf_op jit(solution)/shard_map/ppermute | solution.py:221
  48.9 9.5 %collective-permute-start.10 = (bf16[128,512]{1,0:T(8,128)(2,1)S(1)}, bf16[128,512]{1,0:T(8,128)(2,1)S(1)}, u32[]{:S(2)}, u32[]{:S(2)}) collective-permute-start(bf16[128,512]{1,0:T(8,128)(2,1)S(1)} %get-tuple-element.20), channel_id=1, source_target_pairs={{0,8},{8,16},{16,24},{24,0},{1,9},{9,17},{17,25},{25,1},{2,10},{10... | collective-permute-start | bytes 393224 | tf_op jit(solution)/shard_map/ppermute | solution.py:221
  50.5 10.5 %collective-permute-start.8 = (bf16[128,512]{1,0:T(8,128)(2,1)S(1)}, bf16[128,512]{1,0:T(8,128)(2,1)S(1)}, u32[]{:S(2)}, u32[]{:S(2)}) collective-permute-start(bf16[128,512]{1,0:T(8,128)(2,1)S(1)} %get-tuple-element.21), channel_id=1, source_target_pairs={{0,8},{8,16},{16,24},{24,0},{1,9},{9,17},{17,25},{25,1},{2,10},{10... | collective-permute-start | bytes 393224 | tf_op jit(solution)/shard_map/ppermute | solution.py:221
  52.0 10.3 %collective-permute-start.6 = (bf16[128,512]{1,0:T(8,128)(2,1)S(1)}, bf16[128,512]{1,0:T(8,128)(2,1)S(1)}, u32[]{:S(2)}, u32[]{:S(2)}) collective-permute-start(bf16[128,512]{1,0:T(8,128)(2,1)S(1)} %get-tuple-element.22), channel_id=1, source_target_pairs={{0,8},{8,16},{16,24},{24,0},{1,9},{9,17},{17,25},{25,1},{2,10},{10... | collective-permute-start | bytes 393224 | tf_op jit(solution)/shard_map/ppermute | solution.py:221

commit v2 on v1

--- a/solution.py
+++ b/solution.py
@@ -12,9 +12,9 @@
 REACH = 3
 NORM_EPS = 1e-05
 CHUNKS = 4
-VMEM_BYTES = 48 * 1024 * 1024
-
-ANY = pl.BlockSpec(memory_space=pl.ANY)
+MIB = 1024 * 1024
+
+HBM = pl.BlockSpec(memory_space=pltpu.HBM)
 VMEM = pl.BlockSpec(memory_space=pltpu.VMEM)
 SMEM = pl.BlockSpec(memory_space=pltpu.SMEM)
 
@@ -50,25 +50,28 @@
 
 
 def keyval_kernel(
-    hidden_hbm, gain_ref, table_hbm, weight_hbm, kv_ref, normed_ref, hidden, table, weight, sems, wsems
+    hidden_hbm, gain_hbm, table_hbm, weight_hbm, kv_ref, normed_ref, table, hidden, gain, weight, sems, wsems
 ):
     hidden_copy = pltpu.make_async_copy(hidden_hbm.at[0], hidden, sems.at[0])
     hidden_copy.start()
+    gain_copy = pltpu.make_async_copy(gain_hbm, gain, sems.at[2])
+    gain_copy.start()
     copies = column_copies(weight_hbm, weight, wsems, 2 * HD)
     for copy in copies:
         copy.start()
     tcopy = table_copy(table_hbm, table, sems.at[1])
     tcopy.start()
     hidden_copy.wait()
+    gain_copy.wait()
     rows = hidden.shape[0]
-    gain = gain_ref[...].astype(jnp.float32)
+    scale = gain[...].astype(jnp.float32)
 
     @pl.loop(0, rows // 16)
     def _(at):
         span = pl.ds(pl.multiple_of(at * 16, 16), 16)
         wide = hidden[span, :].astype(jnp.float32)
         square = jnp.mean(wide * wide, axis=1, keepdims=True)
-        normed_ref[span, :] = (wide * lax.rsqrt(square + NORM_EPS) * gain).astype(jnp.bfloat16)
+        normed_ref[span, :] = (wide * lax.rsqrt(square + NORM_EPS) * scale).astype(jnp.bfloat16)
 
     tcopy.wait()
     turn = table[...]
@@ -81,13 +84,10 @@
         kv_ref[:, 2 * HD * k + HD : 2 * HD * (k + 1)] = both[:, HD:].astype(jnp.bfloat16)
 
 
-def query_kernel(normed_ref, table_hbm, weight_hbm, query_ref, table, weight, sems, wsems):
+def query_kernel(normed_ref, table, weight_hbm, query_ref, weight, wsems):
     copies = column_copies(weight_hbm, weight, wsems, 2 * HD)
     for copy in copies:
         copy.start()
-    tcopy = table_copy(table_hbm, table, sems.at[0])
-    tcopy.start()
-    tcopy.wait()
     turn = table[...]
     for k, copy in enumerate(copies):
         copy.wait()
@@ -189,8 +189,10 @@
         ).astype(jnp.bfloat16)
 
 
-def own_kernel(half, width, attn_ref, weight_hbm, after_ref, own_ref, weight, wsems):
+def own_kernel(half, width, attn_ref, weight_hbm, after_ref, *refs):
     count = half // width
+    own_refs = refs[:count]
+    weight, wsems = refs[count:]
     copies = output_copies(
         weight_hbm, weight, wsems, [peer_place(0, half) + k * width for k in range(count)], width
     )
@@ -198,19 +200,26 @@
         copy.start()
     for k in range(count):
         copies[k].wait()
-        own_ref[:, k * width : (k + 1) * width] = jnp.dot(
+        own_refs[k][...] = jnp.dot(
             attn_ref[...], weight[:, k * width : (k + 1) * width], preferred_element_type=jnp.float32
         )
 
 
-def call(kernel, name, outs, in_specs, scratch, flops, moved):
+def add_kernel(own_ref, *refs):
+    total = own_ref[...]
+    for peer_ref in refs[: lax.axis_size("tp") - 1]:
+        total = total + peer_ref[...].astype(jnp.float32)
+    refs[-1][...] = total.astype(jnp.bfloat16)
+
+
+def call(kernel, name, outs, in_specs, scratch, mib, flops=0, moved=0):
     return pl.pallas_call(
         kernel,
         out_shape=outs,
         in_specs=in_specs,
         out_specs=jax.tree.map(lambda _: VMEM, outs),
         scratch_shapes=scratch,
-        compiler_params=pltpu.CompilerParams(vmem_limit_bytes=VMEM_BYTES),
+        compiler_params=pltpu.CompilerParams(vmem_limit_bytes=mib * MIB),
         cost_estimate=pl.CostEstimate(flops=flops, bytes_accessed=moved, transcendentals=0),
         name=name,
     )
@@ -236,18 +245,27 @@
     tp_count = lax.axis_size("tp")
     assert ctx_count % 2 == 0
     table = jnp.asarray(rotary_tables(rows * ctx_count))
-    own_kv, normed = call(
+    hidden_in, norm_gain, table, query_weight, keyval_weight, output_weight = (
+        pltpu.with_memory_space_constraint(value, pltpu.HBM)
+        for value in (hidden_in, norm_gain, table, query_weight, keyval_weight, output_weight)
+    )
+    own_kv, normed, turns = call(
         keyval_kernel,
         "keyval",
-        (jax.ShapeDtypeStruct((rows, kv_columns), bf16), jax.ShapeDtypeStruct((rows, features), bf16)),
-        [ANY, VMEM, ANY, ANY],
+        (
+            jax.ShapeDtypeStruct((rows, kv_columns), bf16),
+            jax.ShapeDtypeStruct((rows, features), bf16),
+            jax.ShapeDtypeStruct((rows, 2 * HD), f32),
+        ),
+        [HBM, HBM, HBM, HBM],
         [
             pltpu.VMEM((rows, features), bf16),
-            pltpu.VMEM((rows, 2 * HD), f32),
+            pltpu.VMEM((1, features), bf16),
             pltpu.VMEM((features, kv_columns), bf16),
-            dma((2,)),
+            dma((3,)),
             dma((kv_columns // (2 * HD),)),
         ],
+        48,
         2 * rows * features * kv_columns,
         2 * features * kv_columns,
     )(hidden_in, norm_gain, table, keyval_weight)
@@ -257,16 +275,16 @@
         query_kernel,
         "query",
         jax.ShapeDtypeStruct((rows, query_columns), bf16),
-        [VMEM, ANY, ANY],
+        [VMEM, VMEM, HBM],
         [
-            pltpu.VMEM((rows, 2 * HD), f32),
             pltpu.VMEM((features, query_columns), bf16),
-            dma((1,)),
             dma((query_columns // (2 * HD),)),
         ],
+        48,
         2 * rows * features * query_columns,
         2 * features * query_columns,
-    )(normed, table, query_weight)
+    )(normed, turns, query_weight)
+    behind, queries = lax.optimization_barrier((behind, queries))
     behind_beside = twins(behind)
     kv_list = [own_kv, beside, behind, behind_beside]
     if ctx_count > 4:
@@ -280,37 +298,40 @@
         functools.partial(attend_kernel, len(kv_list), half, width),
         "attend",
         [jax.ShapeDtypeStruct((rows, query_columns), bf16)] + [send] * peers,
-        [SMEM, VMEM] + [VMEM] * len(kv_list) + [ANY],
+        [SMEM, VMEM] + [VMEM] * len(kv_list) + [HBM],
         [pltpu.VMEM((query_columns, peers * width), bf16), dma((peers,))],
-        2 * rows * query_columns * width,
-        2 * query_columns * width,
+        48,
     )(windows, queries, *kv_list, output_weight)
     later = range(1, CHUNKS)
     rest = call(
         functools.partial(peers_kernel, half, width, later),
         "peers",
         [send] * (peers * len(later)),
-        [VMEM, ANY],
+        [VMEM, HBM],
         [pltpu.VMEM((query_columns, peers * len(later) * width), bf16), dma((peers * len(later),))],
-        2 * rows * query_columns * width * len(later) * peers,
-        2 * query_columns * width * len(later) * peers,
+        48,
     )(attn, output_weight)
     own = call(
         functools.partial(own_kernel, half, width),
         "own",
-        jax.ShapeDtypeStruct((rows, half), f32),
-        [VMEM, ANY, ANY],
+        [jax.ShapeDtypeStruct((rows, width), f32)] * CHUNKS,
+        [VMEM, HBM, VMEM],
         [pltpu.VMEM((query_columns, half), bf16), dma((CHUNKS,))],
-        2 * rows * query_columns * half,
-        2 * query_columns * half,
+        48,
     )(attn, output_weight, rest[-1])
     sends = list(first) + list(rest)
     pieces = []
+    totals = []
+    came = [
+        [moved_by(sends[j * peers + d], "tp", d + 1) for d in range(peers)] for j in range(CHUNKS)
+    ]
     for j in range(CHUNKS):
-        total = own[:, j * width : (j + 1) * width]
-        for d in range(peers):
-            total = total + moved_by(sends[j * peers + d], "tp", d + 1).astype(f32)
-        pieces.append(moved_by(total.astype(bf16), "segment", 1))
+        parts = [own[j]] + came[j] + pieces[max(0, j - 2) : max(0, j - 1)] + totals[-1:]
+        total = call(
+            add_kernel, "add", send, [VMEM] * len(parts), [], 16
+        )(*parts)
+        totals.append(total)
+        pieces.append(moved_by(total, "segment", 1))
     return jnp.concatenate(pieces, axis=1)[None]
 
 

time: 63.6 us -> 53.9 us (0.85)
  waiting for transfers between devices: 21.4 us -> 13.6 us
  local copies, waits for them, and re-layouts: 4.02 us -> 0 us
  Pallas kernels: 23.9 us -> 26.1 us
    ppermute x9, waiting for transfers between devices: 21.4 us -> 13.1 us  [moved_by(): lax.ppermute(value, axis, [(source, (source + steps) % count) for source...]
    unnamed x8 -> x0, local copies, waits for them, and re-layouts: 4.02 us -> none
    pallas_call x1, Pallas kernels: 4.75 us -> 6.86 us  [body(): call(keyval_kernel, 'keyval', (jax.ShapeDtypeStruct((rows, kv_columns), b...]
    pallas_call x1 -> x5, Pallas kernels: 4 us -> 4.1 us  [the longest x1 4 us: body(): call(functools.partial(own_kernel, half, width), 'own', [jax.ShapeDtypeSt...]
  transfers between devices with their start and end apart: 11 -> 11, of which waited for: 7 -> 6; matrix products, arithmetic and copies ran while one was open for 0% -> 0% of each run, Pallas kernels for 24% -> 28%
where the time goes in v2:
time: 53.9 us; the launch traced here: 53.8 us
  Pallas kernels  26.1 us (48%)
  waiting for transfers between devices  13.6 us (25%)
  starting transfers between devices  12.4 us (23%)
  other arithmetic  0.85 us (2%)
  between operations  0.75 us (1%)
    ppermute x9, waiting for transfers between devices, moved_by(): lax.ppermute(value, axis, [(source, (source + steps) % count) for source...  13.1 us
    ppermute x9, starting transfers between devices, moved_by(): lax.ppermute(value, axis, [(source, (source + steps) % count) for source...  11.9 us
    pallas_call x1, Pallas kernels, body(): call(query_kernel, 'query', jax.ShapeDtypeStruct((rows, query_columns), b...  7.77 us
    pallas_call x1, Pallas kernels, body(): call(keyval_kernel, 'keyval', (jax.ShapeDtypeStruct((rows, kv_columns), b...  6.86 us
    pallas_call x1, Pallas kernels, body(): call(functools.partial(own_kernel, half, width), 'own', [jax.ShapeDtypeSt...  4 us
    pallas_call x1, Pallas kernels, body(): call(functools.partial(attend_kernel, len(kv_list), half, width), 'attend...  3.99 us
    pallas_call x1, Pallas kernels, body(): call(functools.partial(peers_kernel, half, width, later), 'peers', [send]...  3.36 us
  transfers between devices with their start and end apart: 11, of which 6 were waited for; matrix products, arithmetic and copies ran while one was open for 0% of the time, Pallas kernels for 28%

profile of v2, /device:TPU:0, one launch (start us, length us, event | category | flops | bytes accessed | tf_op | source)
XLA Modules:
  0.0 53.8 jit_solution(10296653974060246241)
XLA Ops:
  0.0 6.9 %keyval.1 = (bf16[128,1024]{1,0:T(8,128)(2,1)S(1)}, bf16[128,4096]{1,0:T(8,128)(2,1)S(1)}, f32[128,256]{1,0:T(8,128)S(1)}) custom-call(bf16[1,128,4096]{2,1,0:T(8,128)(2,1)} %hidden_hbm.1, bf16[1,4096]{1,0:T(2,128)(2,1)} %gain_hbm.1, f32[512,256]{1,0:T(8,128)} %constant.2.clone.table_hbm, bf16[1,4096,1024]{2,1,0:T(8,128)(2,1)} %weight_hbm.4), custom_call_target="tpu_custom_call" | custom-call | flops 1073741824 | bytes 8388608 | tf_op jit(solution)/shard_map/keyval/pallas_call | solution.py:252
  6.9 3.0 %collective-permute-start = (bf16[128,1024]{1,0:T(8,128)(2,1)S(1)}, bf16[128,1024]{1,0:T(8,128)(2,1)S(1)}, u32[]{:S(2)}, u32[]{:S(2)}) collective-permute-start(bf16[128,1024]{1,0:T(8,128)(2,1)S(1)} %get-tuple-element.19.refs_2_), channel_id=1, source_target_pairs={{0,4},{2,6},{4,0},{6,2},{1,5},{3,7},{5,1},{7,3},{8,12},{10,14},{12... | collective-permute-start | bytes 786440 | tf_op jit(solution)/shard_map/ppermute | solution.py:230
  9.9 0.0 collective-permute-start.1
  9.9 7.8 %query.1.refs_1_ = bf16[128,2048]{1,0:T(8,128)(2,1)S(1)} custom-call(bf16[128,4096]{1,0:T(8,128)(2,1)S(1)} %get-tuple-element.20.normed_ref, f32[128,256]{1,0:T(8,128)S(1)} %get-tuple-element.21.table, bf16[1,4096,2048]{2,1,0:T(8,128)(2,1)} %weight_hbm.5), custom_call_target="tpu_custom_call" | custom-call | flops 2147483648 | bytes 16777216 | tf_op jit(solution)/shard_map/query/pallas_call | solution.py:274
  17.7 0.0 collective-permute-done.refs_4_
  17.7 0.6 %collective-permute-start.2 = (bf16[128,1024]{1,0:T(8,128)(2,1)S(1)}, bf16[128,1024]{1,0:T(8,128)(2,1)S(1)}, u32[]{:S(2)}, u32[]{:S(2)}) collective-permute-start(bf16[128,1024]{1,0:T(8,128)(2,1)S(1)} %collective-permute-done.refs_4_), channel_id=1, source_target_pairs={{0,2},{2,0},{4,6},{6,4},{1,3},{3,1},{5,7},{7,5},{8,10},{10,8},{12,... | collective-permute-start | bytes 786440 | tf_op jit(solution)/shard_map/ppermute | solution.py:235
  18.9 0.0 collective-permute-done.1.refs_3_
  18.9 0.5 collective-permute-done.2.refs_5_
  19.4 4.0 %attend.1 = (bf16[128,2048]{1,0:T(8,128)(2,1)S(1)}, bf16[128,512]{1,0:T(8,128)(2,1)S(1)}) custom-call(s32[1]{0:T(128)S(6)} %copy.8.refs_0_, bf16[128,2048]{1,0:T(8,128)(2,1)S(1)} %query.1.refs_1_, bf16[128,1024]{1,0:T(8,128)(2,1)S(1)} %get-tuple-element.19.refs_2_, bf16[128,1024]{1,0:T(8,128)(2,1)S(1)} %collective-permute-done.1.refs_3_, ...), custom_call_target="tpu_custom_call" | custom-call | tf_op jit(solution)/shard_map/attend/pallas_call | solution.py:297
  23.4 1.6 %collective-permute-start.3 = (bf16[128,512]{1,0:T(8,128)(2,1)S(1)}, bf16[128,512]{1,0:T(8,128)(2,1)S(1)}, u32[]{:S(2)}, u32[]{:S(2)}) collective-permute-start(bf16[128,512]{1,0:T(8,128)(2,1)S(1)} %get-tuple-element.27), channel_id=1, source_target_pairs={{0,1},{1,0},{2,3},{3,2},{4,5},{5,4},{6,7},{7,6},{8,9},{9,8},{10,11... | collective-permute-start | bytes 393224 | tf_op jit(solution)/shard_map/ppermute | solution.py:230
  25.0 3.4 %peers.1 = (bf16[128,512]{1,0:T(8,128)(2,1)S(1)}, bf16[128,512]{1,0:T(8,128)(2,1)S(1)}, bf16[128,512]{1,0:T(8,128)(2,1)S(1)}) custom-call(bf16[128,2048]{1,0:T(8,128)(2,1)S(1)} %get-tuple-element.24.attn_ref, bf16[1,2048,4096]{2,1,0:T(8,128)(2,1)} %weight_hbm.7), custom_call_target="tpu_custom_call" | custom-call | tf_op jit(solution)/shard_map/peers/pallas_call | solution.py:306
  28.4 0.6 %collective-permute-start.5 = (bf16[128,512]{1,0:T(8,128)(2,1)S(1)}, bf16[128,512]{1,0:T(8,128)(2,1)S(1)}, u32[]{:S(2)}, u32[]{:S(2)}) collective-permute-start(bf16[128,512]{1,0:T(8,128)(2,1)S(1)} %get-tuple-element.29), channel_id=1, source_target_pairs={{0,1},{1,0},{2,3},{3,2},{4,5},{5,4},{6,7},{7,6},{8,9},{9,8},{10,11... | collective-permute-start | bytes 393224 | tf_op jit(solution)/shard_map/ppermute | solution.py:230
  28.9 1.5 %collective-permute-start.9 = (bf16[128,512]{1,0:T(8,128)(2,1)S(1)}, bf16[128,512]{1,0:T(8,128)(2,1)S(1)}, u32[]{:S(2)}, u32[]{:S(2)}) collective-permute-start(bf16[128,512]{1,0:T(8,128)(2,1)S(1)} %get-tuple-element.25.after_ref), channel_id=1, source_target_pairs={{0,1},{1,0},{2,3},{3,2},{4,5},{5,4},{6,7},{7,6},{8,9},{9,8},{10,11... | collective-permute-start | bytes 393224 | tf_op jit(solution)/shard_map/ppermute | solution.py:230
  30.5 4.0 %own.1 = (f32[128,512]{1,0:T(8,128)S(1)}, f32[128,512]{1,0:T(8,128)S(1)}, f32[128,512]{1,0:T(8,128)S(1)}, f32[128,512]{1,0:T(8,128)S(1)}) custom-call(bf16[128,2048]{1,0:T(8,128)(2,1)S(1)} %get-tuple-element.24.attn_ref, bf16[1,2048,4096]{2,1,0:T(8,128)(2,1)} %weight_hbm.7, bf16[128,512]{1,0:T(8,128)(2,1)S(1)} %get-tuple-element.25.after_ref), custom_call_target="tpu_custom_call" | custom-call | tf_op jit(solution)/shard_map/own/pallas_call | solution.py:314
  34.5 0.6 %collective-permute-start.7 = (bf16[128,512]{1,0:T(8,128)(2,1)S(1)}, bf16[128,512]{1,0:T(8,128)(2,1)S(1)}, u32[]{:S(2)}, u32[]{:S(2)}) collective-permute-start(bf16[128,512]{1,0:T(8,128)(2,1)S(1)} %get-tuple-element.31), channel_id=1, source_target_pairs={{0,1},{1,0},{2,3},{3,2},{4,5},{5,4},{6,7},{7,6},{8,9},{9,8},{10,11... | collective-permute-start | bytes 393224 | tf_op jit(solution)/shard_map/ppermute | solution.py:230
  35.0 0.0 collective-permute-done.3.refs_0_
  35.1 1.6 %collective-permute-start.4 = (bf16[128,512]{1,0:T(8,128)(2,1)S(1)}, bf16[128,512]{1,0:T(8,128)(2,1)S(1)}, u32[]{:S(2)}, u32[]{:S(2)}) collective-permute-start(bf16[128,512]{1,0:T(8,128)(2,1)S(1)} %add.4.refs_1_), channel_id=1, source_target_pairs={{0,8},{8,16},{16,24},{24,0},{1,9},{9,17},{17,25},{25,1},{2,10},{10... | collective-permute-start | bytes 393224 | tf_op jit(solution)/shard_map/ppermute | solution.py:230
  36.7 0.0 collective-permute-done.5.refs_0_
  36.7 1.6 %collective-permute-start.6 = (bf16[128,512]{1,0:T(8,128)(2,1)S(1)}, bf16[128,512]{1,0:T(8,128)(2,1)S(1)}, u32[]{:S(2)}, u32[]{:S(2)}) collective-permute-start(bf16[128,512]{1,0:T(8,128)(2,1)S(1)} %add.5.refs_2_), channel_id=1, source_target_pairs={{0,8},{8,16},{16,24},{24,0},{1,9},{9,17},{17,25},{25,1},{2,10},{10... | collective-permute-start | bytes 393224 | tf_op jit(solution)/shard_map/ppermute | solution.py:230
  38.4 1.2 %collective-permute-done.7.refs_0_ = bf16[128,512]{1,0:T(8,128)(2,1)S(1)} collective-permute-done((bf16[128,512]{1,0:T(8,128)(2,1)S(1)}, bf16[128,512]{1,0:T(8,128)(2,1)S(1)}, u32[]{:S(2)}, u32[]{:S(2)}) %collective-permute-start.7) | collective-permute-done | bytes 131104 | tf_op jit(solution)/shard_map/ppermute | solution.py:230
  39.5 3.5 %collective-permute-done.4.refs_1_ = bf16[128,512]{1,0:T(8,128)(2,1)S(1)} collective-permute-done((bf16[128,512]{1,0:T(8,128)(2,1)S(1)}, bf16[128,512]{1,0:T(8,128)(2,1)S(1)}, u32[]{:S(2)}, u32[]{:S(2)}) %collective-permute-start.4) | collective-permute-done | bytes 131104 | tf_op jit(solution)/shard_map/ppermute | solution.py:230
  43.1 0.0 collective-permute-done.9.refs_0_
  43.1 1.4 %collective-permute-done.6.refs_1_ = bf16[128,512]{1,0:T(8,128)(2,1)S(1)} collective-permute-done((bf16[128,512]{1,0:T(8,128)(2,1)S(1)}, bf16[128,512]{1,0:T(8,128)(2,1)S(1)}, u32[]{:S(2)}, u32[]{:S(2)}) %collective-permute-start.6) | collective-permute-done | bytes 131104 | tf_op jit(solution)/shard_map/ppermute | solution.py:230
  44.5 0.1 collective-permute-start.10
  44.5 1.3 %collective-permute-start.8 = (bf16[128,512]{1,0:T(8,128)(2,1)S(1)}, bf16[128,512]{1,0:T(8,128)(2,1)S(1)}, u32[]{:S(2)}, u32[]{:S(2)}) collective-permute-start(bf16[128,512]{1,0:T(8,128)(2,1)S(1)} %add.6.refs_2_), channel_id=1, source_target_pairs={{0,8},{8,16},{16,24},{24,0},{1,9},{9,17},{17,25},{25,1},{2,10},{10... | collective-permute-start | bytes 393224 | tf_op jit(solution)/shard_map/ppermute | solution.py:230
  45.8 5.7 %collective-permute-done.10 = bf16[128,512]{1,0:T(8,128)(2,1)S(1)} collective-permute-done((bf16[128,512]{1,0:T(8,128)(2,1)S(1)}, bf16[128,512]{1,0:T(8,128)(2,1)S(1)}, u32[]{:S(2)}, u32[]{:S(2)}) %collective-permute-start.10) | collective-permute-done | bytes 131104 | tf_op jit(solution)/shard_map/ppermute | solution.py:230
  51.5 1.4 %collective-permute-done.8 = bf16[128,512]{1,0:T(8,128)(2,1)S(1)} collective-permute-done((bf16[128,512]{1,0:T(8,128)(2,1)S(1)}, bf16[128,512]{1,0:T(8,128)(2,1)S(1)}, u32[]{:S(2)}, u32[]{:S(2)}) %collective-permute-start.8) | collective-permute-done | bytes 131104 | tf_op jit(solution)/shard_map/ppermute | solution.py:230
  52.9 0.8 %maximum_bitcast_fusion = bf16[1,128,2048]{2,1,0:T(8,128)(2,1)} fusion(bf16[128,512]{1,0:T(8,128)(2,1)S(1)} %collective-permute-done.10, bf16[128,512]{1,0:T(8,128)(2,1)S(1)} %collective-permute-done.8, bf16[128,512]{1,0:T(8,128)(2,1)S(1)} %collective-permute-done.6.refs_1_, bf16[128,512]{1,0:T(8,128)(2,1)S(1)} %collective-permute-done.4.refs_1_), kind=kLoop, calls=%fused_computation | loop fusion | flops 2097152 | bytes 1048576 | tf_op jit(solution)/shard_map/broadcast_in_dim | solution.py:335
  (4 shorter events, 0.1 us)
Async XLA Ops:
  6.9 10.8 %collective-permute-start = (bf16[128,1024]{1,0:T(8,128)(2,1)S(1)}, bf16[128,1024]{1,0:T(8,128)(2,1)S(1)}, u32[]{:S(2)}, u32[]{:S(2)}) collective-permute-start(bf16[128,1024]{1,0:T(8,128)(2,1)S(1)} %get-tuple-element.19.refs_2_), channel_id=1, source_target_pairs={{0,4},{2,6},{4,0},{6,2},{1,5},{3,7},{5,1},{7,3},{8,12},{10,14},{12... | collective-permute-start | bytes 786440 | tf_op jit(solution)/shard_map/ppermute | solution.py:230
  9.9 9.0 %collective-permute-start.1 = (bf16[128,1024]{1,0:T(8,128)(2,1)S(1)}, bf16[128,1024]{1,0:T(8,128)(2,1)S(1)}, u32[]{:S(2)}, u32[]{:S(2)}) collective-permute-start(bf16[128,1024]{1,0:T(8,128)(2,1)S(1)} %get-tuple-element.19.refs_2_), channel_id=1, source_target_pairs={{0,2},{2,0},{4,6},{6,4},{1,3},{3,1},{5,7},{7,5},{8,10},{10,8},{12,... | collective-permute-start | bytes 786440 | tf_op jit(solution)/shard_map/ppermute | solution.py:235
  17.7 1.7 %collective-permute-start.2 = (bf16[128,1024]{1,0:T(8,128)(2,1)S(1)}, bf16[128,1024]{1,0:T(8,128)(2,1)S(1)}, u32[]{:S(2)}, u32[]{:S(2)}) collective-permute-start(bf16[128,1024]{1,0:T(8,128)(2,1)S(1)} %collective-permute-done.refs_4_), channel_id=1, source_target_pairs={{0,2},{2,0},{4,6},{6,4},{1,3},{3,1},{5,7},{7,5},{8,10},{10,8},{12,... | collective-permute-start | bytes 786440 | tf_op jit(solution)/shard_map/ppermute | solution.py:235
  23.4 11.6 %collective-permute-start.3 = (bf16[128,512]{1,0:T(8,128)(2,1)S(1)}, bf16[128,512]{1,0:T(8,128)(2,1)S(1)}, u32[]{:S(2)}, u32[]{:S(2)}) collective-permute-start(bf16[128,512]{1,0:T(8,128)(2,1)S(1)} %get-tuple-element.27), channel_id=1, source_target_pairs={{0,1},{1,0},{2,3},{3,2},{4,5},{5,4},{6,7},{7,6},{8,9},{9,8},{10,11... | collective-permute-start | bytes 393224 | tf_op jit(solution)/shard_map/ppermute | solution.py:230
  28.4 8.3 %collective-permute-start.5 = (bf16[128,512]{1,0:T(8,128)(2,1)S(1)}, bf16[128,512]{1,0:T(8,128)(2,1)S(1)}, u32[]{:S(2)}, u32[]{:S(2)}) collective-permute-start(bf16[128,512]{1,0:T(8,128)(2,1)S(1)} %get-tuple-element.29), channel_id=1, source_target_pairs={{0,1},{1,0},{2,3},{3,2},{4,5},{5,4},{6,7},{7,6},{8,9},{9,8},{10,11... | collective-permute-start | bytes 393224 | tf_op jit(solution)/shard_map/ppermute | solution.py:230
  28.9 14.1 %collective-permute-start.9 = (bf16[128,512]{1,0:T(8,128)(2,1)S(1)}, bf16[128,512]{1,0:T(8,128)(2,1)S(1)}, u32[]{:S(2)}, u32[]{:S(2)}) collective-permute-start(bf16[128,512]{1,0:T(8,128)(2,1)S(1)} %get-tuple-element.25.after_ref), channel_id=1, source_target_pairs={{0,1},{1,0},{2,3},{3,2},{4,5},{5,4},{6,7},{7,6},{8,9},{9,8},{10,11... | collective-permute-start | bytes 393224 | tf_op jit(solution)/shard_map/ppermute | solution.py:230
  34.5 5.1 %collective-permute-start.7 = (bf16[128,512]{1,0:T(8,128)(2,1)S(1)}, bf16[128,512]{1,0:T(8,128)(2,1)S(1)}, u32[]{:S(2)}, u32[]{:S(2)}) collective-permute-start(bf16[128,512]{1,0:T(8,128)(2,1)S(1)} %get-tuple-element.31), channel_id=1, source_target_pairs={{0,1},{1,0},{2,3},{3,2},{4,5},{5,4},{6,7},{7,6},{8,9},{9,8},{10,11... | collective-permute-start | bytes 393224 | tf_op jit(solution)/shard_map/ppermute | solution.py:230
  35.1 8.0 %collective-permute-start.4 = (bf16[128,512]{1,0:T(8,128)(2,1)S(1)}, bf16[128,512]{1,0:T(8,128)(2,1)S(1)}, u32[]{:S(2)}, u32[]{:S(2)}) collective-permute-start(bf16[128,512]{1,0:T(8,128)(2,1)S(1)} %add.4.refs_1_), channel_id=1, source_target_pairs={{0,8},{8,16},{16,24},{24,0},{1,9},{9,17},{17,25},{25,1},{2,10},{10... | collective-permute-start | bytes 393224 | tf_op jit(solution)/shard_map/ppermute | solution.py:230
  36.7 7.7 %collective-permute-start.6 = (bf16[128,512]{1,0:T(8,128)(2,1)S(1)}, bf16[128,512]{1,0:T(8,128)(2,1)S(1)}, u32[]{:S(2)}, u32[]{:S(2)}) collective-permute-start(bf16[128,512]{1,0:T(8,128)(2,1)S(1)} %add.5.refs_2_), channel_id=1, source_target_pairs={{0,8},{8,16},{16,24},{24,0},{1,9},{9,17},{17,25},{25,1},{2,10},{10... | collective-permute-start | bytes 393224 | tf_op jit(solution)/shard_map/ppermute | solution.py:230
  44.5 7.0 %collective-permute-start.10 = (bf16[128,512]{1,0:T(8,128)(2,1)S(1)}, bf16[128,512]{1,0:T(8,128)(2,1)S(1)}, u32[]{:S(2)}, u32[]{:S(2)}) collective-permute-start(bf16[128,512]{1,0:T(8,128)(2,1)S(1)} %add.7), channel_id=1, source_target_pairs={{0,8},{8,16},{16,24},{24,0},{1,9},{9,17},{17,25},{25,1},{2,10},{10... | collective-permute-start | bytes 393224 | tf_op jit(solution)/shard_map/ppermute | solution.py:230
  44.5 8.4 %collective-permute-start.8 = (bf16[128,512]{1,0:T(8,128)(2,1)S(1)}, bf16[128,512]{1,0:T(8,128)(2,1)S(1)}, u32[]{:S(2)}, u32[]{:S(2)}) collective-permute-start(bf16[128,512]{1,0:T(8,128)(2,1)S(1)} %add.6.refs_2_), channel_id=1, source_target_pairs={{0,8},{8,16},{16,24},{24,0},{1,9},{9,17},{17,25},{25,1},{2,10},{10... | collective-permute-start | bytes 393224 | tf_op jit(solution)/shard_map/ppermute | solution.py:230

commit v3 on v2

v3 whole, which is shorter than its diff:
```python
import functools

import jax
import jax.numpy as jnp
import numpy as np
from jax import lax
from jax.experimental import pallas as pl
from jax.experimental.pallas import tpu as pltpu
from jax.sharding import PartitionSpec as P

HD = 128
REACH = 3
NORM_EPS = 1e-05
SHARES = (5, 6, 5)
LOG2E = 1.4426950408889634
MIB = 1024 * 1024

HBM = pl.BlockSpec(memory_space=pltpu.HBM)
VMEM = pl.BlockSpec(memory_space=pltpu.VMEM)
SMEM = pl.BlockSpec(memory_space=pltpu.SMEM)


def rotary_tables(tokens):
    half = HD // 2
    inverse = 10000.0 ** (-np.arange(half, dtype=np.float32) / np.float32(half))
    angles = np.arange(tokens, dtype=np.float32)[:, None] * inverse.astype(np.float32)[None, :]
    cosine = np.cos(angles.astype(np.float64)).astype(np.float32)
    sine = np.sin(angles.astype(np.float64)).astype(np.float32)
    return np.concatenate([cosine, cosine, -sine, sine], axis=1)


def turned(head, table):
    return head * table[:, :HD] + pltpu.roll(head, HD // 2, 1) * table[:, HD:]


def table_copy(table_hbm, table, sem):
    rows = table.shape[0]
    first = pl.multiple_of(lax.axis_index("ctx") * rows, 8)
    return pltpu.make_async_copy(table_hbm.at[pl.ds(first, rows)], table, sem)


def column_copies(weight_hbm, weight, sems):
    width = weight.shape[1] // sems.shape[0]
    return [
        pltpu.make_async_copy(
            weight_hbm.at[0, :, pl.ds(k * width, width)],
            weight.at[:, pl.ds(k * width, width)],
            sems.at[k],
        )
        for k in range(sems.shape[0])
    ]


def keyval_kernel(
    hidden_hbm, gain_hbm, table_hbm, weight_hbm, kv_ref, normed_ref, table, hidden, gain, weight, sems, wsems
):
    hidden_copy = pltpu.make_async_copy(hidden_hbm.at[0], hidden, sems.at[0])
    hidden_copy.start()
    gain_copy = pltpu.make_async_copy(gain_hbm, gain, sems.at[2])
    gain_copy.start()
    tcopy = table_copy(table_hbm, table, sems.at[1])
    tcopy.start()
    copies = column_copies(weight_hbm, weight, wsems)
    for copy in copies:
        copy.start(priority=1)
    gain_copy.wait()
    hidden_copy.wait()
    rows, features = hidden.shape
    spans = [slice(at, at + HD) for at in range(0, features, HD)]
    squares = jnp.zeros((rows, HD), jnp.float32)
    for span in spans:
        wide = hidden[:, span].astype(jnp.float32)
        squares = squares + wide * wide
    mean = jnp.sum(squares, axis=1, keepdims=True) * (1.0 / features)
    inverse = jnp.broadcast_to(lax.rsqrt(mean + NORM_EPS), (rows, HD))
    for span in spans:
        wide = hidden[:, span].astype(jnp.float32)
        normed_ref[:, span] = (wide * inverse * gain[:, span].astype(jnp.float32)).astype(jnp.bfloat16)
    tcopy.wait()
    turn = table[...]
    width = weight.shape[1] // len(copies)
    for k, copy in enumerate(copies):
        copy.wait()
        both = jnp.dot(
            normed_ref[...], weight[:, width * k : width * (k + 1)], preferred_element_type=jnp.float32
        )
        for part in range(0, width, 2 * HD):
            at = width * k + part
            kv_ref[:, at : at + HD] = turned(both[:, part : part + HD], turn).astype(jnp.bfloat16)
            kv_ref[:, at + HD : at + 2 * HD] = both[:, part + HD : part + 2 * HD].astype(jnp.bfloat16)


def query_kernel(normed_ref, table, weight_hbm, query_ref, weight, wsems):
    copies = column_copies(weight_hbm, weight, wsems)
    for copy in copies:
        copy.start()
    turn = table[...]
    width = weight.shape[1] // len(copies)
    for k, copy in enumerate(copies):
        copy.wait()
        both = jnp.dot(
            normed_ref[...], weight[:, width * k : width * (k + 1)], preferred_element_type=jnp.float32
        )
        for part in range(0, width, HD):
            at = width * k + part
            query_ref[:, at : at + HD] = turned(both[:, part : part + HD], turn).astype(jnp.bfloat16)


def output_copies(weight_hbm, weights, sems, places):
    return [
        pltpu.make_async_copy(
            weight_hbm.at[0, :, pl.ds(pl.multiple_of(place, 128), weight.shape[1])], weight, sems.at[k]
        )
        for k, (weight, place) in enumerate(zip(weights, places))
    ]


def peer_place(steps, half, start):
    count = lax.axis_size("tp")
    return lax.rem(lax.axis_index("tp") + steps, count) * half + start


def steps_of(width):
    return [(at, min(256, width - at)) for at in range(0, width, 256)]


def multiply(attn_ref, weight_ref, out_ref):
    for at, step in steps_of(weight_ref.shape[1]):
        out_ref[:, at : at + step] = jnp.dot(
            attn_ref[...], weight_ref[:, at : at + step], preferred_element_type=jnp.float32
        ).astype(out_ref.dtype)


def attend_kernel(block_count, places, window_ref, query_ref, *refs):
    kv_refs, weight_hbm, refs = refs[:block_count], refs[block_count], refs[block_count + 1 :]
    peers = lax.axis_size("tp") - 1
    attn_ref, send_refs, kept_refs = refs[0], refs[1 : peers + 1], refs[peers + 1 : -peers - 1]
    weights, sems = refs[-peers - 1 : -1], refs[-1]
    copies = output_copies(weight_hbm, weights + kept_refs, sems, [peer_place(*p) for p in places])
    for copy in copies:
        copy.start()
    rows = query_ref.shape[0]
    kv_count = kv_refs[0].shape[1] // (2 * HD)
    group = query_ref.shape[1] // HD // kv_count
    ctx = lax.axis_index("ctx")
    twin = ctx + 1 - 2 * lax.rem(ctx, 2)
    row = lax.broadcasted_iota(jnp.int32, (rows, rows), 0)
    column = lax.broadcasted_iota(jnp.int32, (rows, rows), 1)
    masks = []
    for block in [ctx, twin, ctx - 2, twin - 2, twin - 4][:block_count]:
        distance = row - column + (ctx - block) * rows
        masks.append((distance >= 0) & (distance < window_ref[0]) & (block >= 0))
    inside = jnp.concatenate(masks, axis=1)[None]
    for g in range(kv_count):
        queries = jnp.concatenate(
            [query_ref[:, HD * (group * g + h) : HD * (group * g + h + 1)] for h in range(group)], axis=0
        )
        keys = jnp.concatenate([r[:, 2 * HD * g : 2 * HD * g + HD] for r in kv_refs], axis=0)
        values = jnp.concatenate([r[:, 2 * HD * g + HD : 2 * HD * (g + 1)] for r in kv_refs], axis=0)
        scores = lax.dot_general(
            queries, keys, (((1,), (1,)), ((), ())), preferred_element_type=jnp.float32
        ).reshape(group, rows, block_count * rows)
        scores = jnp.where(inside, scores * (HD ** (-0.5) * LOG2E), jnp.float32(-1e30))
        highest = jnp.max(scores, axis=2, keepdims=True)
        expo = jnp.exp2(scores - highest).astype(jnp.bfloat16).reshape(group * rows, block_count * rows)
        sums = jnp.dot(
            expo, jnp.concatenate([values, jnp.ones_like(values)], axis=1), preferred_element_type=jnp.float32
        )
        out = (sums[:, :HD] * (1.0 / sums[:, HD:])).astype(jnp.bfloat16)
        for h in range(group):
            at = HD * (group * g + h)
            attn_ref[:, at : at + HD] = out[h * rows : (h + 1) * rows]
    for copy, weight, send_ref in zip(copies, weights, send_refs):
        copy.wait()
        multiply(attn_ref, weight, send_ref)
    for copy in copies[peers:]:
        copy.wait()


def multiply_kernel(held, places, attn_ref, *refs):
    held_refs, weight_hbm, refs = refs[:held], refs[held], refs[held + 2 :]
    count = held + len(places)
    out_refs, weights = refs[:count], refs[count : count + len(places)]
    pieces = [
        (k, at, step) for k, weight in enumerate(weights) for at, step in steps_of(weight.shape[1])
    ]
    copies = []
    if places:
        copies = output_copies(
            weight_hbm,
            [weights[k].at[:, pl.ds(at, step)] for k, at, step in pieces],
            refs[-1],
            [peer_place(*places[k]) + at for k, at, _ in pieces],
        )
    for copy in copies:
        copy.start()
    for weight_ref, out_ref in zip(held_refs, out_refs):
        multiply(attn_ref, weight_ref, out_ref)
    for copy, (k, at, step) in zip(copies, pieces):
        copy.wait()
        out_ref = out_refs[held + k]
        out_ref[:, at : at + step] = jnp.dot(
            attn_ref[...], weights[k][:, at : at + step], preferred_element_type=jnp.float32
        ).astype(out_ref.dtype)


def add_kernel(own_ref, *refs):
    total = own_ref[...]
    for peer_ref in refs[: lax.axis_size("tp") - 1]:
        total = total + peer_ref[...].astype(jnp.float32)
    refs[-1][...] = total.astype(jnp.bfloat16)


def call(kernel, name, outs, in_specs, scratch, mib, flops=0, moved=0):
    return pl.pallas_call(
        kernel,
        out_shape=outs,
        in_specs=in_specs,
        out_specs=jax.tree.map(lambda _: VMEM, outs),
        scratch_shapes=scratch,
        compiler_params=pltpu.CompilerParams(vmem_limit_bytes=mib * MIB),
        cost_estimate=pl.CostEstimate(flops=flops, bytes_accessed=moved, transcendentals=0),
        name=name,
    )


def moved_by(value, axis, steps):
    count = lax.axis_size(axis)
    return lax.ppermute(value, axis, [(source, (source + steps) % count) for source in range(count)])


def twins(value):
    count = lax.axis_size("ctx")
    return lax.ppermute(value, "ctx", [(source, source ^ 1) for source in range(count)])


def body(hidden_in, norm_gain, query_weight, keyval_weight, output_weight, windows):
    bf16, f32 = jnp.bfloat16, jnp.float32
    dma = pltpu.SemaphoreType.DMA
    _, rows, features = hidden_in.shape
    query_columns = query_weight.shape[2]
    kv_columns = keyval_weight.shape[2]
    ctx_count = lax.axis_size("ctx")
    tp_count = lax.axis_size("tp")
    assert ctx_count % 2 == 0
    table = jnp.asarray(rotary_tables(rows * ctx_count))
    hidden_in, norm_gain, table, query_weight, keyval_weight, output_weight = (
        pltpu.with_memory_space_constraint(value, pltpu.HBM)
        for value in (hidden_in, norm_gain, table, query_weight, keyval_weight, output_weight)
    )
    own_kv, normed, turns = call(
        keyval_kernel,
        "keyval",
        (
            jax.ShapeDtypeStruct((rows, kv_columns), bf16),
            jax.ShapeDtypeStruct((rows, features), bf16),
            jax.ShapeDtypeStruct((rows, 2 * HD), f32),
        ),
        [HBM, HBM, HBM, HBM],
        [
            pltpu.VMEM((rows, features), bf16),
            pltpu.VMEM((1, features), bf16),
            pltpu.VMEM((features, kv_columns), bf16),
            dma((3,)),
            dma((max(1, kv_columns // 512),)),
        ],
        48,
        2 * rows * features * kv_columns,
        2 * features * kv_columns,
    )(hidden_in, norm_gain, table, keyval_weight)
    behind = moved_by(own_kv, "ctx", 2)
    beside = twins(own_kv)
    queries = call(
        query_kernel,
        "query",
        jax.ShapeDtypeStruct((rows, query_columns), bf16),
        [VMEM, VMEM, HBM],
        [
            pltpu.VMEM((features, query_columns), bf16),
            dma((max(1, query_columns // 512),)),
        ],
        48,
        2 * rows * features * query_columns,
        2 * features * query_columns,
    )(normed, turns, query_weight)
    behind, queries = lax.optimization_barrier((behind, queries))
    behind_beside = twins(behind)
    kv_list = [own_kv, beside, behind, behind_beside]
    if ctx_count > 4:
        kv_list.append(moved_by(behind_beside, "ctx", 2))
    out_columns = output_weight.shape[2]
    half = out_columns // tp_count
    peers = tp_count - 1
    cuts = [half * sum(SHARES[:j]) // sum(SHARES) // 128 * 128 for j in range(len(SHARES) + 1)]
    widths = [end - start for start, end in zip(cuts, cuts[1:])]
    sends = [[jax.ShapeDtypeStruct((rows, width), bf16)] * peers for width in widths]
    owns = [jax.ShapeDtypeStruct((rows, width), f32) for width in widths]

    def away(j):
        return [(d, half, cuts[j]) for d in range(1, peers + 1)]

    def here(j):
        return [(0, half, cuts[j])]

    def weights_of(j):
        return jax.ShapeDtypeStruct((query_columns, widths[j]), bf16)

    def products(name, outs, attn, held, places, columns, after):
        return call(
            functools.partial(multiply_kernel, len(held), places),
            name,
            outs,
            [VMEM] * (1 + len(held)) + [HBM, VMEM],
            [pltpu.VMEM((query_columns, width), bf16) for width in columns]
            + ([dma((sum(len(steps_of(width)) for width in columns),))] if places else []),
            40,
        )(attn, *held, output_weight, after)

    kept = [weights_of(1)] * peers + [weights_of(0)]
    attn, *made = call(
        functools.partial(attend_kernel, len(kv_list), away(0) + away(1) + here(0)),
        "attend",
        [jax.ShapeDtypeStruct((rows, query_columns), bf16)] + sends[0] + kept,
        [SMEM, VMEM] + [VMEM] * len(kv_list) + [HBM],
        [pltpu.VMEM((query_columns, widths[0]), bf16)] * peers + [dma((2 * peers + 1,))],
        40,
    )(windows, queries, *kv_list, output_weight)
    sent = [made[:peers]]
    sent.append(products("away1", sends[1], attn, made[peers : 2 * peers], [], [], made[0]))
    own, *last = products(
        "own0", owns[:1] + sends[2], attn, made[-1:], away(2), [widths[2]] * peers, sent[1][0]
    )
    sent.append(last)
    came = [[moved_by(value, "tp", d + 1) for d, value in enumerate(values)] for values in sent]
    pieces, totals = [], []
    for j in range(len(widths)):
        parts = [own] + came[j] + pieces[max(0, j - 2) : max(0, j - 1)] + totals[-1:]
        total = call(add_kernel, "add", sends[j][0], [VMEM] * len(parts), [], 16)(*parts)
        totals.append(total)
        pieces.append(moved_by(total, "segment", 1))
        if j + 1 < len(widths):
            (own,) = products("own", owns[j + 1 : j + 2], attn, [], here(j + 1), widths[j + 1 : j + 2], total)
    return jnp.concatenate(pieces, axis=1)[None]


def solution(mesh):
    in_specs = (
        P("segment", "ctx", None),
        P("segment", None),
        P("segment", None, "tp"),
        P("segment", None, "tp"),
        P("segment", "tp", None),
        P("segment"),
    )
    out_specs = P("segment", "ctx", "tp")
    return jax.shard_map(body, mesh=mesh, in_specs=in_specs, out_specs=out_specs, check_vma=False)
```

time: 53.9 us -> 44.6 us (0.83)
  waiting for transfers between devices: 13.6 us -> 6.23 us
  Pallas kernels: 26.1 us -> 24.4 us
    ppermute x9 -> x7, waiting for transfers between devices: 13.1 us -> 5.73 us  [moved_by(): lax.ppermute(value, axis, [(source, (source + steps) % count) for source...]
    pallas_call x1, Pallas kernels: 6.86 us -> 4.66 us  [body(): call(keyval_kernel, 'keyval', (jax.ShapeDtypeStruct((rows, kv_columns), b...]
    pallas_call x7 -> x8, Pallas kernels: 11.5 us -> 12.9 us  [the longest x4 8.17 us: products(): call(functools.partial(multiply_kernel, len(held), places), name, outs, [...]
    pallas_call x1, Pallas kernels: 7.77 us -> 6.76 us  [body(): call(query_kernel, 'query', jax.ShapeDtypeStruct((rows, query_columns), b...]
    ppermute x9 -> x7, starting transfers between devices: 11.9 us -> 11.6 us  [moved_by(): lax.ppermute(value, axis, [(source, (source + steps) % count) for source...]
  transfers between devices with their start and end apart: 11 -> 9, of which waited for: 6 -> 4; matrix products, arithmetic and copies ran while one was open for 0% -> 0% of each run, Pallas kernels for 28% -> 34%
where the time goes in v3:
time: 44.6 us; the launch traced here: 44.4 us
  Pallas kernels  24.4 us (55%)
  starting transfers between devices  12.2 us (27%)
  waiting for transfers between devices  6.23 us (14%)
  other arithmetic  0.85 us (2%)
  between operations  0.76 us (2%)
    ppermute x7, starting transfers between devices, moved_by(): lax.ppermute(value, axis, [(source, (source + steps) % count) for source...  11.6 us
    pallas_call x4, Pallas kernels, products(): call(functools.partial(multiply_kernel, len(held), places), name, outs, [...  8.17 us
    pallas_call x1, Pallas kernels, body(): call(query_kernel, 'query', jax.ShapeDtypeStruct((rows, query_columns), b...  6.76 us
    ppermute x7, waiting for transfers between devices, moved_by(): lax.ppermute(value, axis, [(source, (source + steps) % count) for source...  5.73 us
    pallas_call x1, Pallas kernels, body(): call(functools.partial(attend_kernel, len(kv_list), away(0) + away(1) + h...  4.66 us
    pallas_call x1, Pallas kernels, body(): call(keyval_kernel, 'keyval', (jax.ShapeDtypeStruct((rows, kv_columns), b...  4.66 us
  transfers between devices with their start and end apart: 9, of which 4 were waited for; matrix products, arithmetic and copies ran while one was open for 0% of the time, Pallas kernels for 34%

profile of v3, /device:TPU:0, one launch (start us, length us, event | category | flops | bytes accessed | tf_op | source)
XLA Modules:
  0.0 44.4 jit_solution(5883006978771898056)
XLA Ops:
  0.0 4.7 %keyval.1 = (bf16[128,1024]{1,0:T(8,128)(2,1)S(1)}, bf16[128,4096]{1,0:T(8,128)(2,1)S(1)}, f32[128,256]{1,0:T(8,128)S(1)}) custom-call(bf16[1,128,4096]{2,1,0:T(8,128)(2,1)} %hidden_hbm.1, bf16[1,4096]{1,0:T(2,128)(2,1)} %gain_hbm.1, f32[512,256]{1,0:T(8,128)} %constant.2.clone.table_hbm, bf16[1,4096,1024]{2,1,0:T(8,128)(2,1)} %weight_hbm.2), custom_call_target="tpu_custom_call" | custom-call | flops 1073741824 | bytes 8388608 | tf_op jit(solution)/shard_map/keyval/pallas_call | solution.py:251
  4.7 3.0 %collective-permute-start = (bf16[128,1024]{1,0:T(8,128)(2,1)S(1)}, bf16[128,1024]{1,0:T(8,128)(2,1)S(1)}, u32[]{:S(2)}, u32[]{:S(2)}) collective-permute-start(bf16[128,1024]{1,0:T(8,128)(2,1)S(1)} %get-tuple-element.16.refs_0_), channel_id=1, source_target_pairs={{0,4},{2,6},{4,0},{6,2},{1,5},{3,7},{5,1},{7,3},{8,12},{10,14},{12... | collective-permute-start | bytes 786440 | tf_op jit(solution)/shard_map/ppermute | solution.py:229
  7.7 0.0 collective-permute-start.1
  7.7 6.8 %query.1.query_ref = bf16[128,2048]{1,0:T(8,128)(2,1)S(1)} custom-call(bf16[128,4096]{1,0:T(8,128)(2,1)S(1)} %get-tuple-element.17.normed_ref, f32[128,256]{1,0:T(8,128)S(1)} %get-tuple-element.18.table, bf16[1,4096,2048]{2,1,0:T(8,128)(2,1)} %weight_hbm.3), custom_call_target="tpu_custom_call" | custom-call | flops 2147483648 | bytes 16777216 | tf_op jit(solution)/shard_map/query/pallas_call | solution.py:273
  14.4 0.0 collective-permute-done.refs_2_
  14.5 0.6 %collective-permute-start.2 = (bf16[128,1024]{1,0:T(8,128)(2,1)S(1)}, bf16[128,1024]{1,0:T(8,128)(2,1)S(1)}, u32[]{:S(2)}, u32[]{:S(2)}) collective-permute-start(bf16[128,1024]{1,0:T(8,128)(2,1)S(1)} %collective-permute-done.refs_2_), channel_id=1, source_target_pairs={{0,2},{2,0},{4,6},{6,4},{1,3},{3,1},{5,7},{7,5},{8,10},{10,8},{12,... | collective-permute-start | bytes 786440 | tf_op jit(solution)/shard_map/ppermute | solution.py:234
  15.7 0.0 collective-permute-done.1.refs_1_
  15.7 0.5 %collective-permute-done.2.refs_3_ = bf16[128,1024]{1,0:T(8,128)(2,1)S(1)} collective-permute-done((bf16[128,1024]{1,0:T(8,128)(2,1)S(1)}, bf16[128,1024]{1,0:T(8,128)(2,1)S(1)}, u32[]{:S(2)}, u32[]{:S(2)}) %collective-permute-start.2) | collective-permute-done | bytes 262176 | tf_op jit(solution)/shard_map/ppermute | solution.py:234
  16.2 4.7 %attend.1 = (bf16[128,2048]{1,0:T(8,128)(2,1)S(1)}, bf16[128,640]{1,0:T(8,128)(2,1)S(1)}, bf16[2048,768]{1,0:T(8,128)(2,1)S(1)}, bf16[2048,640]{1,0:T(8,128)(2,1)S(1)}) custom-call(s32[1]{0:T(128)S(6)} %copy.8.window_ref, bf16[128,2048]{1,0:T(8,128)(2,1)S(1)} %query.1.query_ref, bf16[128,1024]{1,0:T(8,128)(2,1)S(1)} %get-tuple-element.16.refs_0_, ...), custom_call_target="tpu_custom_call" | custom-call | tf_op jit(solution)/shard_map/attend/pallas_call | solution.py:320
  20.9 1.6 %collective-permute-start.3 = (bf16[128,640]{1,0:T(8,128)(2,1)S(1)}, bf16[128,640]{1,0:T(8,128)(2,1)S(1)}, u32[]{:S(2)}, u32[]{:S(2)}) collective-permute-start(bf16[128,640]{1,0:T(8,128)(2,1)S(1)} %get-tuple-element.24.refs_2_), channel_id=1, source_target_pairs={{0,1},{1,0},{2,3},{3,2},{4,5},{5,4},{6,7},{7,6},{8,9},{9,8},{10,11... | collective-permute-start | bytes 491528 | tf_op jit(solution)/shard_map/ppermute | solution.py:229
  22.5 0.6 %away1.1.refs_2_ = bf16[128,768]{1,0:T(8,128)(2,1)S(1)} custom-call(bf16[128,2048]{1,0:T(8,128)(2,1)S(1)} %get-tuple-element.21.attn_ref, bf16[2048,768]{1,0:T(8,128)(2,1)S(1)} %get-tuple-element.23.refs_0_, bf16[1,2048,4096]{2,1,0:T(8,128)(2,1)} %refs_0_.3, bf16[128,640]{1,0:T(8,128)(2,1)S(1)} %get-tuple-element.24.refs_2_), custom_call_target="tpu_custom_call" | custom-call | tf_op jit(solution)/shard_map/away1/pallas_call | solution.py:309
  23.0 0.6 %collective-permute-start.5 = (bf16[128,768]{1,0:T(8,128)(2,1)S(1)}, bf16[128,768]{1,0:T(8,128)(2,1)S(1)}, u32[]{:S(2)}, u32[]{:S(2)}) collective-permute-start(bf16[128,768]{1,0:T(8,128)(2,1)S(1)} %away1.1.refs_2_), channel_id=1, source_target_pairs={{0,1},{1,0},{2,3},{3,2},{4,5},{5,4},{6,7},{7,6},{8,9},{9,8},{10,11... | collective-permute-start | bytes 589832 | tf_op jit(solution)/shard_map/ppermute | solution.py:229
  23.6 2.8 %own0.1 = (f32[128,640]{1,0:T(8,128)S(1)}, bf16[128,640]{1,0:T(8,128)(2,1)S(1)}) custom-call(bf16[128,2048]{1,0:T(8,128)(2,1)S(1)} %get-tuple-element.21.attn_ref, bf16[2048,640]{1,0:T(8,128)(2,1)S(1)} %get-tuple-element.22.refs_0_, bf16[1,2048,4096]{2,1,0:T(8,128)(2,1)} %refs_0_.3, bf16[128,768]{1,0:T(8,128)(2,1)S(1)} %away1.1.refs_2_), custom_call_target="tpu_custom_call" | custom-call | tf_op jit(solution)/shard_map/own0/pallas_call | solution.py:309
  26.4 1.6 %collective-permute-start.7 = (bf16[128,640]{1,0:T(8,128)(2,1)S(1)}, bf16[128,640]{1,0:T(8,128)(2,1)S(1)}, u32[]{:S(2)}, u32[]{:S(2)}) collective-permute-start(bf16[128,640]{1,0:T(8,128)(2,1)S(1)} %get-tuple-element.26), channel_id=1, source_target_pairs={{0,1},{1,0},{2,3},{3,2},{4,5},{5,4},{6,7},{7,6},{8,9},{9,8},{10,11... | collective-permute-start | bytes 491528 | tf_op jit(solution)/shard_map/ppermute | solution.py:229
  28.0 0.0 collective-permute-done.3.refs_0_
  28.0 1.6 %collective-permute-start.4 = (bf16[128,640]{1,0:T(8,128)(2,1)S(1)}, bf16[128,640]{1,0:T(8,128)(2,1)S(1)}, u32[]{:S(2)}, u32[]{:S(2)}) collective-permute-start(bf16[128,640]{1,0:T(8,128)(2,1)S(1)} %add.3.refs_1_), channel_id=1, source_target_pairs={{0,8},{8,16},{16,24},{24,0},{1,9},{9,17},{17,25},{25,1},{2,10},{10... | collective-permute-start | bytes 491528 | tf_op jit(solution)/shard_map/ppermute | solution.py:229
  29.7 2.4 %own.2.own_ref = f32[128,768]{1,0:T(8,128)S(1)} custom-call(bf16[128,2048]{1,0:T(8,128)(2,1)S(1)} %get-tuple-element.21.attn_ref, bf16[1,2048,4096]{2,1,0:T(8,128)(2,1)} %refs_0_.3, bf16[128,640]{1,0:T(8,128)(2,1)S(1)} %add.3.refs_1_), custom_call_target="tpu_custom_call" | custom-call | tf_op jit(solution)/shard_map/own/pallas_call | solution.py:309
  32.1 0.1 collective-permute-done.5.refs_0_
  32.2 1.6 %collective-permute-start.6 = (bf16[128,768]{1,0:T(8,128)(2,1)S(1)}, bf16[128,768]{1,0:T(8,128)(2,1)S(1)}, u32[]{:S(2)}, u32[]{:S(2)}) collective-permute-start(bf16[128,768]{1,0:T(8,128)(2,1)S(1)} %add.4.refs_1_.refs_2_), channel_id=1, source_target_pairs={{0,8},{8,16},{16,24},{24,0},{1,9},{9,17},{17,25},{25,1},{2,10},{10... | collective-permute-start | bytes 589832 | tf_op jit(solution)/shard_map/ppermute | solution.py:229
  33.8 2.4 %own.3.own_ref = f32[128,640]{1,0:T(8,128)S(1)} custom-call(bf16[128,2048]{1,0:T(8,128)(2,1)S(1)} %get-tuple-element.21.attn_ref, bf16[1,2048,4096]{2,1,0:T(8,128)(2,1)} %refs_0_.3, bf16[128,768]{1,0:T(8,128)(2,1)S(1)} %add.4.refs_1_.refs_2_), custom_call_target="tpu_custom_call" | custom-call | tf_op jit(solution)/shard_map/own/pallas_call | solution.py:309
  36.2 0.0 collective-permute-done.7.refs_0_
  36.2 0.0 collective-permute-done.4.refs_1_
  36.3 1.6 %collective-permute-start.8 = (bf16[128,640]{1,0:T(8,128)(2,1)S(1)}, bf16[128,640]{1,0:T(8,128)(2,1)S(1)}, u32[]{:S(2)}, u32[]{:S(2)}) collective-permute-start(bf16[128,640]{1,0:T(8,128)(2,1)S(1)} %add.5), channel_id=1, source_target_pairs={{0,8},{8,16},{16,24},{24,0},{1,9},{9,17},{17,25},{25,1},{2,10},{10... | collective-permute-start | bytes 491528 | tf_op jit(solution)/shard_map/ppermute | solution.py:229
  37.9 2.5 %collective-permute-done.6 = bf16[128,768]{1,0:T(8,128)(2,1)S(1)} collective-permute-done((bf16[128,768]{1,0:T(8,128)(2,1)S(1)}, bf16[128,768]{1,0:T(8,128)(2,1)S(1)}, u32[]{:S(2)}, u32[]{:S(2)}) %collective-permute-start.6) | collective-permute-done | bytes 196640 | tf_op jit(solution)/shard_map/ppermute | solution.py:229
  40.4 3.2 %collective-permute-done.8 = bf16[128,640]{1,0:T(8,128)(2,1)S(1)} collective-permute-done((bf16[128,640]{1,0:T(8,128)(2,1)S(1)}, bf16[128,640]{1,0:T(8,128)(2,1)S(1)}, u32[]{:S(2)}, u32[]{:S(2)}) %collective-permute-start.8) | collective-permute-done | bytes 163872 | tf_op jit(solution)/shard_map/ppermute | solution.py:229
  43.6 0.9 %maximum_bitcast_fusion = bf16[1,128,2048]{2,1,0:T(8,128)(2,1)} fusion(bf16[128,640]{1,0:T(8,128)(2,1)S(1)} %collective-permute-done.8, bf16[128,768]{1,0:T(8,128)(2,1)S(1)} %collective-permute-done.6, bf16[128,640]{1,0:T(8,128)(2,1)S(1)} %collective-permute-done.4.refs_1_), kind=kLoop, calls=%fused_computation | loop fusion | flops 1572864 | bytes 1048576 | tf_op jit(solution)/shard_map/broadcast_in_dim | solution.py:343
  (3 shorter events, 0.1 us)
Async XLA Ops:
  4.7 9.8 %collective-permute-start = (bf16[128,1024]{1,0:T(8,128)(2,1)S(1)}, bf16[128,1024]{1,0:T(8,128)(2,1)S(1)}, u32[]{:S(2)}, u32[]{:S(2)}) collective-permute-start(bf16[128,1024]{1,0:T(8,128)(2,1)S(1)} %get-tuple-element.16.refs_0_), channel_id=1, source_target_pairs={{0,4},{2,6},{4,0},{6,2},{1,5},{3,7},{5,1},{7,3},{8,12},{10,14},{12... | collective-permute-start | bytes 786440 | tf_op jit(solution)/shard_map/ppermute | solution.py:229
  7.7 8.0 %collective-permute-start.1 = (bf16[128,1024]{1,0:T(8,128)(2,1)S(1)}, bf16[128,1024]{1,0:T(8,128)(2,1)S(1)}, u32[]{:S(2)}, u32[]{:S(2)}) collective-permute-start(bf16[128,1024]{1,0:T(8,128)(2,1)S(1)} %get-tuple-element.16.refs_0_), channel_id=1, source_target_pairs={{0,2},{2,0},{4,6},{6,4},{1,3},{3,1},{5,7},{7,5},{8,10},{10,8},{12,... | collective-permute-start | bytes 786440 | tf_op jit(solution)/shard_map/ppermute | solution.py:234
  14.5 1.7 %collective-permute-start.2 = (bf16[128,1024]{1,0:T(8,128)(2,1)S(1)}, bf16[128,1024]{1,0:T(8,128)(2,1)S(1)}, u32[]{:S(2)}, u32[]{:S(2)}) collective-permute-start(bf16[128,1024]{1,0:T(8,128)(2,1)S(1)} %collective-permute-done.refs_2_), channel_id=1, source_target_pairs={{0,2},{2,0},{4,6},{6,4},{1,3},{3,1},{5,7},{7,5},{8,10},{10,8},{12,... | collective-permute-start | bytes 786440 | tf_op jit(solution)/shard_map/ppermute | solution.py:234
  20.9 7.1 %collective-permute-start.3 = (bf16[128,640]{1,0:T(8,128)(2,1)S(1)}, bf16[128,640]{1,0:T(8,128)(2,1)S(1)}, u32[]{:S(2)}, u32[]{:S(2)}) collective-permute-start(bf16[128,640]{1,0:T(8,128)(2,1)S(1)} %get-tuple-element.24.refs_2_), channel_id=1, source_target_pairs={{0,1},{1,0},{2,3},{3,2},{4,5},{5,4},{6,7},{7,6},{8,9},{9,8},{10,11... | collective-permute-start | bytes 491528 | tf_op jit(solution)/shard_map/ppermute | solution.py:229
  23.0 9.1 %collective-permute-start.5 = (bf16[128,768]{1,0:T(8,128)(2,1)S(1)}, bf16[128,768]{1,0:T(8,128)(2,1)S(1)}, u32[]{:S(2)}, u32[]{:S(2)}) collective-permute-start(bf16[128,768]{1,0:T(8,128)(2,1)S(1)} %away1.1.refs_2_), channel_id=1, source_target_pairs={{0,1},{1,0},{2,3},{3,2},{4,5},{5,4},{6,7},{7,6},{8,9},{9,8},{10,11... | collective-permute-start | bytes 589832 | tf_op jit(solution)/shard_map/ppermute | solution.py:229
  26.4 9.8 %collective-permute-start.7 = (bf16[128,640]{1,0:T(8,128)(2,1)S(1)}, bf16[128,640]{1,0:T(8,128)(2,1)S(1)}, u32[]{:S(2)}, u32[]{:S(2)}) collective-permute-start(bf16[128,640]{1,0:T(8,128)(2,1)S(1)} %get-tuple-element.26), channel_id=1, source_target_pairs={{0,1},{1,0},{2,3},{3,2},{4,5},{5,4},{6,7},{7,6},{8,9},{9,8},{10,11... | collective-permute-start | bytes 491528 | tf_op jit(solution)/shard_map/ppermute | solution.py:229
  28.0 8.2 %collective-permute-start.4 = (bf16[128,640]{1,0:T(8,128)(2,1)S(1)}, bf16[128,640]{1,0:T(8,128)(2,1)S(1)}, u32[]{:S(2)}, u32[]{:S(2)}) collective-permute-start(bf16[128,640]{1,0:T(8,128)(2,1)S(1)} %add.3.refs_1_), channel_id=1, source_target_pairs={{0,8},{8,16},{16,24},{24,0},{1,9},{9,17},{17,25},{25,1},{2,10},{10... | collective-permute-start | bytes 491528 | tf_op jit(solution)/shard_map/ppermute | solution.py:229
  32.2 8.2 %collective-permute-start.6 = (bf16[128,768]{1,0:T(8,128)(2,1)S(1)}, bf16[128,768]{1,0:T(8,128)(2,1)S(1)}, u32[]{:S(2)}, u32[]{:S(2)}) collective-permute-start(bf16[128,768]{1,0:T(8,128)(2,1)S(1)} %add.4.refs_1_.refs_2_), channel_id=1, source_target_pairs={{0,8},{8,16},{16,24},{24,0},{1,9},{9,17},{17,25},{25,1},{2,10},{10... | collective-permute-start | bytes 589832 | tf_op jit(solution)/shard_map/ppermute | solution.py:229
  36.3 7.3 %collective-permute-start.8 = (bf16[128,640]{1,0:T(8,128)(2,1)S(1)}, bf16[128,640]{1,0:T(8,128)(2,1)S(1)}, u32[]{:S(2)}, u32[]{:S(2)}) collective-permute-start(bf16[128,640]{1,0:T(8,128)(2,1)S(1)} %add.5), channel_id=1, source_target_pairs={{0,8},{8,16},{16,24},{24,0},{1,9},{9,17},{17,25},{25,1},{2,10},{10... | collective-permute-start | bytes 491528 | tf_op jit(solution)/shard_map/ppermute | solution.py:229

commit v4 on v3

--- a/solution.py
+++ b/solution.py
@@ -90,9 +90,11 @@
             kv_ref[:, at + HD : at + 2 * HD] = both[:, part + HD : part + 2 * HD].astype(jnp.bfloat16)
 
 
-def query_kernel(normed_ref, table, weight_hbm, query_ref, weight, wsems):
+def query_kernel(places, normed_ref, table, weight_hbm, next_hbm, query_ref, *refs):
+    kept_refs, (weight, wsems, sems) = refs[: len(places)], refs[len(places) :]
     copies = column_copies(weight_hbm, weight, wsems)
-    for copy in copies:
+    next_copies = output_copies(next_hbm, kept_refs, sems, [peer_place(*p) for p in places])
+    for copy in copies + next_copies:
         copy.start()
     turn = table[...]
     width = weight.shape[1] // len(copies)
@@ -104,6 +106,8 @@
         for part in range(0, width, HD):
             at = width * k + part
             query_ref[:, at : at + HD] = turned(both[:, part : part + HD], turn).astype(jnp.bfloat16)
+    for copy in next_copies:
+        copy.wait()
 
 
 def output_copies(weight_hbm, weights, sems, places):
@@ -132,48 +136,51 @@
 
 
 def attend_kernel(block_count, places, window_ref, query_ref, *refs):
-    kv_refs, weight_hbm, refs = refs[:block_count], refs[block_count], refs[block_count + 1 :]
     peers = lax.axis_size("tp") - 1
-    attn_ref, send_refs, kept_refs = refs[0], refs[1 : peers + 1], refs[peers + 1 : -peers - 1]
-    weights, sems = refs[-peers - 1 : -1], refs[-1]
-    copies = output_copies(weight_hbm, weights + kept_refs, sems, [peer_place(*p) for p in places])
+    kv_refs, weights, refs = refs[:block_count], refs[block_count : block_count + peers], refs[block_count + peers :]
+    weight_hbm, attn_ref, refs = refs[0], refs[1], refs[2:]
+    send_refs, kept_refs, sems = refs[:peers], refs[peers:-1], refs[-1]
+    copies = output_copies(weight_hbm, kept_refs, sems, [peer_place(*p) for p in places])
     for copy in copies:
         copy.start()
-    rows = query_ref.shape[0]
-    kv_count = kv_refs[0].shape[1] // (2 * HD)
-    group = query_ref.shape[1] // HD // kv_count
     ctx = lax.axis_index("ctx")
-    twin = ctx + 1 - 2 * lax.rem(ctx, 2)
-    row = lax.broadcasted_iota(jnp.int32, (rows, rows), 0)
-    column = lax.broadcasted_iota(jnp.int32, (rows, rows), 1)
-    masks = []
-    for block in [ctx, twin, ctx - 2, twin - 2, twin - 4][:block_count]:
-        distance = row - column + (ctx - block) * rows
-        masks.append((distance >= 0) & (distance < window_ref[0]) & (block >= 0))
-    inside = jnp.concatenate(masks, axis=1)[None]
-    for g in range(kv_count):
-        queries = jnp.concatenate(
-            [query_ref[:, HD * (group * g + h) : HD * (group * g + h + 1)] for h in range(group)], axis=0
-        )
-        keys = jnp.concatenate([r[:, 2 * HD * g : 2 * HD * g + HD] for r in kv_refs], axis=0)
-        values = jnp.concatenate([r[:, 2 * HD * g + HD : 2 * HD * (g + 1)] for r in kv_refs], axis=0)
-        scores = lax.dot_general(
-            queries, keys, (((1,), (1,)), ((), ())), preferred_element_type=jnp.float32
-        ).reshape(group, rows, block_count * rows)
-        scores = jnp.where(inside, scores * (HD ** (-0.5) * LOG2E), jnp.float32(-1e30))
-        highest = jnp.max(scores, axis=2, keepdims=True)
-        expo = jnp.exp2(scores - highest).astype(jnp.bfloat16).reshape(group * rows, block_count * rows)
-        sums = jnp.dot(
-            expo, jnp.concatenate([values, jnp.ones_like(values)], axis=1), preferred_element_type=jnp.float32
-        )
-        out = (sums[:, :HD] * (1.0 / sums[:, HD:])).astype(jnp.bfloat16)
-        for h in range(group):
-            at = HD * (group * g + h)
-            attn_ref[:, at : at + HD] = out[h * rows : (h + 1) * rows]
-    for copy, weight, send_ref in zip(copies, weights, send_refs):
-        copy.wait()
-        multiply(attn_ref, weight, send_ref)
-    for copy in copies[peers:]:
+
+    @pl.when(ctx >= 0)
+    def _():
+        rows = query_ref.shape[0]
+        kv_count = kv_refs[0].shape[1] // (2 * HD)
+        group = query_ref.shape[1] // HD // kv_count
+        twin = ctx + 1 - 2 * lax.rem(ctx, 2)
+        row = lax.broadcasted_iota(jnp.int32, (rows, rows), 0)
+        column = lax.broadcasted_iota(jnp.int32, (rows, rows), 1)
+        masks = []
+        for block in [ctx, twin, ctx - 2, twin - 2, twin - 4][:block_count]:
+            distance = row - column + (ctx - block) * rows
+            masks.append((distance >= 0) & (distance < window_ref[0]) & (block >= 0))
+        inside = jnp.concatenate(masks, axis=1)[None]
+        for g in range(kv_count):
+            queries = jnp.concatenate(
+                [query_ref[:, HD * (group * g + h) : HD * (group * g + h + 1)] for h in range(group)], axis=0
+            )
+            keys = jnp.concatenate([r[:, 2 * HD * g : 2 * HD * g + HD] for r in kv_refs], axis=0)
+            values = jnp.concatenate([r[:, 2 * HD * g + HD : 2 * HD * (g + 1)] for r in kv_refs], axis=0)
+            scores = lax.dot_general(
+                queries, keys, (((1,), (1,)), ((), ())), preferred_element_type=jnp.float32
+            ).reshape(group, rows, block_count * rows)
+            scores = jnp.where(inside, scores * (HD ** (-0.5) * LOG2E), jnp.float32(-1e30))
+            highest = jnp.max(scores, axis=2, keepdims=True)
+            expo = jnp.exp2(scores - highest).astype(jnp.bfloat16).reshape(group * rows, block_count * rows)
+            sums = jnp.dot(
+                expo, jnp.concatenate([values, jnp.ones_like(values)], axis=1), preferred_element_type=jnp.float32
+            )
+            out = (sums[:, :HD] * (1.0 / sums[:, HD:])).astype(jnp.bfloat16)
+            for h in range(group):
+                at = HD * (group * g + h)
+                attn_ref[:, at : at + HD] = out[h * rows : (h + 1) * rows]
+        for weight, send_ref in zip(weights, send_refs):
+            multiply(attn_ref, weight, send_ref)
+
+    for copy in copies:
         copy.wait()
 
 
@@ -194,8 +201,12 @@
         )
     for copy in copies:
         copy.start()
-    for weight_ref, out_ref in zip(held_refs, out_refs):
-        multiply(attn_ref, weight_ref, out_ref)
+
+    @pl.when(lax.axis_index("ctx") >= 0)
+    def _():
+        for weight_ref, out_ref in zip(held_refs, out_refs):
+            multiply(attn_ref, weight_ref, out_ref)
+
     for copy, (k, at, step) in zip(copies, pieces):
         copy.wait()
         out_ref = out_refs[held + k]
@@ -270,24 +281,6 @@
     )(hidden_in, norm_gain, table, keyval_weight)
     behind = moved_by(own_kv, "ctx", 2)
     beside = twins(own_kv)
-    queries = call(
-        query_kernel,
-        "query",
-        jax.ShapeDtypeStruct((rows, query_columns), bf16),
-        [VMEM, VMEM, HBM],
-        [
-            pltpu.VMEM((features, query_columns), bf16),
-            dma((max(1, query_columns // 512),)),
-        ],
-        48,
-        2 * rows * features * query_columns,
-        2 * features * query_columns,
-    )(normed, turns, query_weight)
-    behind, queries = lax.optimization_barrier((behind, queries))
-    behind_beside = twins(behind)
-    kv_list = [own_kv, beside, behind, behind_beside]
-    if ctx_count > 4:
-        kv_list.append(moved_by(behind_beside, "ctx", 2))
     out_columns = output_weight.shape[2]
     half = out_columns // tp_count
     peers = tp_count - 1
@@ -316,19 +309,39 @@
             40,
         )(attn, *held, output_weight, after)
 
-    kept = [weights_of(1)] * peers + [weights_of(0)]
+    queries, *held = call(
+        functools.partial(query_kernel, away(0) + here(0)),
+        "query",
+        [jax.ShapeDtypeStruct((rows, query_columns), bf16)] + [weights_of(0)] * (peers + 1),
+        [VMEM, VMEM, HBM, HBM],
+        [
+            pltpu.VMEM((features, query_columns), bf16),
+            dma((max(1, query_columns // 512),)),
+            dma((peers + 1,)),
+        ],
+        44,
+        2 * rows * features * query_columns,
+        2 * features * query_columns,
+    )(normed, turns, query_weight, output_weight)
+    behind, queries = lax.optimization_barrier((behind, queries))
+    behind_beside = twins(behind)
+    kv_list = [own_kv, beside, behind, behind_beside]
+    if ctx_count > 4:
+        kv_list.append(moved_by(behind_beside, "ctx", 2))
+    ahead = away(1)
+    kept = [weights_of(1)] * peers
     attn, *made = call(
-        functools.partial(attend_kernel, len(kv_list), away(0) + away(1) + here(0)),
+        functools.partial(attend_kernel, len(kv_list), ahead),
         "attend",
         [jax.ShapeDtypeStruct((rows, query_columns), bf16)] + sends[0] + kept,
-        [SMEM, VMEM] + [VMEM] * len(kv_list) + [HBM],
-        [pltpu.VMEM((query_columns, widths[0]), bf16)] * peers + [dma((2 * peers + 1,))],
-        40,
-    )(windows, queries, *kv_list, output_weight)
+        [SMEM] + [VMEM] * (1 + len(kv_list) + peers) + [HBM],
+        [dma((len(ahead),))],
+        36,
+    )(windows, queries, *kv_list, *held[:peers], output_weight)
     sent = [made[:peers]]
     sent.append(products("away1", sends[1], attn, made[peers : 2 * peers], [], [], made[0]))
     own, *last = products(
-        "own0", owns[:1] + sends[2], attn, made[-1:], away(2), [widths[2]] * peers, sent[1][0]
+        "own0", owns[:1] + sends[2], attn, held[peers:], away(2), [widths[2]] * peers, sent[1][0]
     )
     sent.append(last)
     came = [[moved_by(value, "tp", d + 1) for d, value in enumerate(values)] for values in sent]

time: 44.6 us -> 42.8 us (0.960)
  Pallas kernels: 24.4 us -> 22.2 us
    pallas_call x2, Pallas kernels: 11.4 us -> 9.71 us  [the longest x1 7.48 us: body(): call(functools.partial(query_kernel, away(0) + here(0)), 'query', [jax.Sh...]
  transfers between devices with their start and end apart: 9 -> 9, of which waited for: 4 -> 5; matrix products, arithmetic and copies ran while one was open for 0% -> 0% of each run, Pallas kernels for 34% -> 36%
where the time goes in v4:
time: 42.8 us; the launch traced here: 42.6 us
  Pallas kernels  22.2 us (52%)
  starting transfers between devices  12.2 us (29%)
  waiting for transfers between devices  6.53 us (15%)
  other arithmetic  0.85 us (2%)
  between operations  0.76 us (2%)
    ppermute x7, starting transfers between devices, moved_by(): lax.ppermute(value, axis, [(source, (source + steps) % count) for source...  11.7 us
    pallas_call x4, Pallas kernels, products(): call(functools.partial(multiply_kernel, len(held), places), name, outs, [...  7.75 us
    pallas_call x1, Pallas kernels, body(): call(functools.partial(query_kernel, away(0) + here(0)), 'query', [jax.Sh...  7.48 us
    ppermute x7, waiting for transfers between devices, moved_by(): lax.ppermute(value, axis, [(source, (source + steps) % count) for source...  6.02 us
    pallas_call x1, Pallas kernels, body(): call(keyval_kernel, 'keyval', (jax.ShapeDtypeStruct((rows, kv_columns), b...  4.66 us
    pallas_call x1, Pallas kernels, body(): call(functools.partial(attend_kernel, len(kv_list), ahead), 'attend', [ja...  2.23 us
  transfers between devices with their start and end apart: 9, of which 5 were waited for; matrix products, arithmetic and copies ran while one was open for 0% of the time, Pallas kernels for 36%

profile of v4, /device:TPU:0, one launch (start us, length us, event | category | flops | bytes accessed | tf_op | source)
XLA Modules:
  0.0 42.6 jit_solution(15913369957767018823)
XLA Ops:
  0.0 4.7 %keyval.1 = (bf16[128,1024]{1,0:T(8,128)(2,1)S(1)}, bf16[128,4096]{1,0:T(8,128)(2,1)S(1)}, f32[128,256]{1,0:T(8,128)S(1)}) custom-call(bf16[1,128,4096]{2,1,0:T(8,128)(2,1)} %hidden_hbm.1, bf16[1,4096]{1,0:T(2,128)(2,1)} %gain_hbm.1, f32[512,256]{1,0:T(8,128)} %constant.2.clone.table_hbm, bf16[1,4096,1024]{2,1,0:T(8,128)(2,1)} %weight_hbm.2), custom_call_target="tpu_custom_call" | custom-call | flops 1073741824 | bytes 8388608 | tf_op jit(solution)/shard_map/keyval/pallas_call | solution.py:262
  4.7 3.0 %collective-permute-start = (bf16[128,1024]{1,0:T(8,128)(2,1)S(1)}, bf16[128,1024]{1,0:T(8,128)(2,1)S(1)}, u32[]{:S(2)}, u32[]{:S(2)}) collective-permute-start(bf16[128,1024]{1,0:T(8,128)(2,1)S(1)} %get-tuple-element.18.refs_0_), channel_id=1, source_target_pairs={{0,4},{2,6},{4,0},{6,2},{1,5},{3,7},{5,1},{7,3},{8,12},{10,14},{12... | collective-permute-start | bytes 786440 | tf_op jit(solution)/shard_map/ppermute | solution.py:240
  7.7 0.0 collective-permute-start.1
  7.7 7.5 %query.1 = (bf16[128,2048]{1,0:T(8,128)(2,1)S(1)}, bf16[2048,640]{1,0:T(8,128)(2,1)S(1)}, bf16[2048,640]{1,0:T(8,128)(2,1)S(1)}) custom-call(bf16[128,4096]{1,0:T(8,128)(2,1)S(1)} %get-tuple-element.19.normed_ref, f32[128,256]{1,0:T(8,128)S(1)} %get-tuple-element.20.table, bf16[1,4096,2048]{2,1,0:T(8,128)(2,1)} %weight_hbm.3, bf16[1,2048,4096]{2,1,0:T(8,128)(2,1)} %refs_0_.3), custom_call_target="tpu_custom_call" | custom-call | flops 2147483648 | bytes 16777216 | tf_op jit(solution)/shard_map/query/pallas_call | solution.py:312
  15.2 0.0 collective-permute-done.refs_2_
  15.2 0.6 %collective-permute-start.2 = (bf16[128,1024]{1,0:T(8,128)(2,1)S(1)}, bf16[128,1024]{1,0:T(8,128)(2,1)S(1)}, u32[]{:S(2)}, u32[]{:S(2)}) collective-permute-start(bf16[128,1024]{1,0:T(8,128)(2,1)S(1)} %collective-permute-done.refs_2_), channel_id=1, source_target_pairs={{0,2},{2,0},{4,6},{6,4},{1,3},{3,1},{5,7},{7,5},{8,10},{10,8},{12,... | collective-permute-start | bytes 786440 | tf_op jit(solution)/shard_map/ppermute | solution.py:245
  16.4 0.0 collective-permute-done.1.refs_1_
  16.4 0.5 %collective-permute-done.2.refs_3_ = bf16[128,1024]{1,0:T(8,128)(2,1)S(1)} collective-permute-done((bf16[128,1024]{1,0:T(8,128)(2,1)S(1)}, bf16[128,1024]{1,0:T(8,128)(2,1)S(1)}, u32[]{:S(2)}, u32[]{:S(2)}) %collective-permute-start.2) | collective-permute-done | bytes 262176 | tf_op jit(solution)/shard_map/ppermute | solution.py:245
  16.9 2.2 %attend.1 = (bf16[128,2048]{1,0:T(8,128)(2,1)S(1)}, bf16[128,640]{1,0:T(8,128)(2,1)S(1)}, bf16[2048,768]{1,0:T(8,128)(2,1)S(1)}) custom-call(s32[1]{0:T(128)S(6)} %copy.8.window_ref, bf16[128,2048]{1,0:T(8,128)(2,1)S(1)} %get-tuple-element.22.query_ref, bf16[128,1024]{1,0:T(8,128)(2,1)S(1)} %get-tuple-element.18.refs_0_, ...), custom_call_target="tpu_custom_call" | custom-call | tf_op jit(solution)/shard_map/attend/pallas_call | solution.py:333
  19.1 1.6 %collective-permute-start.3 = (bf16[128,640]{1,0:T(8,128)(2,1)S(1)}, bf16[128,640]{1,0:T(8,128)(2,1)S(1)}, u32[]{:S(2)}, u32[]{:S(2)}) collective-permute-start(bf16[128,640]{1,0:T(8,128)(2,1)S(1)} %get-tuple-element.28.refs_2_), channel_id=1, source_target_pairs={{0,1},{1,0},{2,3},{3,2},{4,5},{5,4},{6,7},{7,6},{8,9},{9,8},{10,11... | collective-permute-start | bytes 491528 | tf_op jit(solution)/shard_map/ppermute | solution.py:240
  20.7 0.6 %away1.1.refs_2_ = bf16[128,768]{1,0:T(8,128)(2,1)S(1)} custom-call(bf16[128,2048]{1,0:T(8,128)(2,1)S(1)} %get-tuple-element.25.attn_ref, bf16[2048,768]{1,0:T(8,128)(2,1)S(1)} %get-tuple-element.27.refs_0_, bf16[1,2048,4096]{2,1,0:T(8,128)(2,1)} %refs_0_.3, bf16[128,640]{1,0:T(8,128)(2,1)S(1)} %get-tuple-element.28.refs_2_), custom_call_target="tpu_custom_call" | custom-call | tf_op jit(solution)/shard_map/away1/pallas_call | solution.py:302
  21.3 0.6 %collective-permute-start.5 = (bf16[128,768]{1,0:T(8,128)(2,1)S(1)}, bf16[128,768]{1,0:T(8,128)(2,1)S(1)}, u32[]{:S(2)}, u32[]{:S(2)}) collective-permute-start(bf16[128,768]{1,0:T(8,128)(2,1)S(1)} %away1.1.refs_2_), channel_id=1, source_target_pairs={{0,1},{1,0},{2,3},{3,2},{4,5},{5,4},{6,7},{7,6},{8,9},{9,8},{10,11... | collective-permute-start | bytes 589832 | tf_op jit(solution)/shard_map/ppermute | solution.py:240
  21.9 2.4 %own0.1 = (f32[128,640]{1,0:T(8,128)S(1)}, bf16[128,640]{1,0:T(8,128)(2,1)S(1)}) custom-call(bf16[128,2048]{1,0:T(8,128)(2,1)S(1)} %get-tuple-element.25.attn_ref, bf16[2048,640]{1,0:T(8,128)(2,1)S(1)} %get-tuple-element.26.refs_0_, bf16[1,2048,4096]{2,1,0:T(8,128)(2,1)} %refs_0_.3, bf16[128,768]{1,0:T(8,128)(2,1)S(1)} %away1.1.refs_2_), custom_call_target="tpu_custom_call" | custom-call | tf_op jit(solution)/shard_map/own0/pallas_call | solution.py:302
  24.3 1.6 %collective-permute-start.7 = (bf16[128,640]{1,0:T(8,128)(2,1)S(1)}, bf16[128,640]{1,0:T(8,128)(2,1)S(1)}, u32[]{:S(2)}, u32[]{:S(2)}) collective-permute-start(bf16[128,640]{1,0:T(8,128)(2,1)S(1)} %get-tuple-element.30), channel_id=1, source_target_pairs={{0,1},{1,0},{2,3},{3,2},{4,5},{5,4},{6,7},{7,6},{8,9},{9,8},{10,11... | collective-permute-start | bytes 491528 | tf_op jit(solution)/shard_map/ppermute | solution.py:240
  25.9 0.4 collective-permute-done.3.refs_0_
  26.3 1.6 %collective-permute-start.4 = (bf16[128,640]{1,0:T(8,128)(2,1)S(1)}, bf16[128,640]{1,0:T(8,128)(2,1)S(1)}, u32[]{:S(2)}, u32[]{:S(2)}) collective-permute-start(bf16[128,640]{1,0:T(8,128)(2,1)S(1)} %add.3.refs_1_), channel_id=1, source_target_pairs={{0,8},{8,16},{16,24},{24,0},{1,9},{9,17},{17,25},{25,1},{2,10},{10... | collective-permute-start | bytes 491528 | tf_op jit(solution)/shard_map/ppermute | solution.py:240
  27.9 2.4 %own.2.own_ref = f32[128,768]{1,0:T(8,128)S(1)} custom-call(bf16[128,2048]{1,0:T(8,128)(2,1)S(1)} %get-tuple-element.25.attn_ref, bf16[1,2048,4096]{2,1,0:T(8,128)(2,1)} %refs_0_.3, bf16[128,640]{1,0:T(8,128)(2,1)S(1)} %add.3.refs_1_), custom_call_target="tpu_custom_call" | custom-call | tf_op jit(solution)/shard_map/own/pallas_call | solution.py:302
  30.3 0.1 collective-permute-done.5.refs_0_
  30.5 1.6 %collective-permute-start.6 = (bf16[128,768]{1,0:T(8,128)(2,1)S(1)}, bf16[128,768]{1,0:T(8,128)(2,1)S(1)}, u32[]{:S(2)}, u32[]{:S(2)}) collective-permute-start(bf16[128,768]{1,0:T(8,128)(2,1)S(1)} %add.4.refs_1_.refs_2_), channel_id=1, source_target_pairs={{0,8},{8,16},{16,24},{24,0},{1,9},{9,17},{17,25},{25,1},{2,10},{10... | collective-permute-start | bytes 589832 | tf_op jit(solution)/shard_map/ppermute | solution.py:240
  32.1 2.4 %own.3.own_ref = f32[128,640]{1,0:T(8,128)S(1)} custom-call(bf16[128,2048]{1,0:T(8,128)(2,1)S(1)} %get-tuple-element.25.attn_ref, bf16[1,2048,4096]{2,1,0:T(8,128)(2,1)} %refs_0_.3, bf16[128,768]{1,0:T(8,128)(2,1)S(1)} %add.4.refs_1_.refs_2_), custom_call_target="tpu_custom_call" | custom-call | tf_op jit(solution)/shard_map/own/pallas_call | solution.py:302
  34.5 0.0 collective-permute-done.7.refs_0_
  34.5 0.0 collective-permute-done.4.refs_1_
  34.6 1.6 %collective-permute-start.8 = (bf16[128,640]{1,0:T(8,128)(2,1)S(1)}, bf16[128,640]{1,0:T(8,128)(2,1)S(1)}, u32[]{:S(2)}, u32[]{:S(2)}) collective-permute-start(bf16[128,640]{1,0:T(8,128)(2,1)S(1)} %add.5), channel_id=1, source_target_pairs={{0,8},{8,16},{16,24},{24,0},{1,9},{9,17},{17,25},{25,1},{2,10},{10... | collective-permute-start | bytes 491528 | tf_op jit(solution)/shard_map/ppermute | solution.py:240
  36.2 2.4 %collective-permute-done.6 = bf16[128,768]{1,0:T(8,128)(2,1)S(1)} collective-permute-done((bf16[128,768]{1,0:T(8,128)(2,1)S(1)}, bf16[128,768]{1,0:T(8,128)(2,1)S(1)}, u32[]{:S(2)}, u32[]{:S(2)}) %collective-permute-start.6) | collective-permute-done | bytes 196640 | tf_op jit(solution)/shard_map/ppermute | solution.py:240
  38.6 3.1 %collective-permute-done.8 = bf16[128,640]{1,0:T(8,128)(2,1)S(1)} collective-permute-done((bf16[128,640]{1,0:T(8,128)(2,1)S(1)}, bf16[128,640]{1,0:T(8,128)(2,1)S(1)}, u32[]{:S(2)}, u32[]{:S(2)}) %collective-permute-start.8) | collective-permute-done | bytes 163872 | tf_op jit(solution)/shard_map/ppermute | solution.py:240
  41.7 0.9 %maximum_bitcast_fusion = bf16[1,128,2048]{2,1,0:T(8,128)(2,1)} fusion(bf16[128,640]{1,0:T(8,128)(2,1)S(1)} %collective-permute-done.8, bf16[128,768]{1,0:T(8,128)(2,1)S(1)} %collective-permute-done.6, bf16[128,640]{1,0:T(8,128)(2,1)S(1)} %collective-permute-done.4.refs_1_), kind=kLoop, calls=%fused_computation | loop fusion | flops 1572864 | bytes 1048576 | tf_op jit(solution)/shard_map/broadcast_in_dim | solution.py:356
  (3 shorter events, 0.1 us)
Async XLA Ops:
  4.7 10.5 %collective-permute-start = (bf16[128,1024]{1,0:T(8,128)(2,1)S(1)}, bf16[128,1024]{1,0:T(8,128)(2,1)S(1)}, u32[]{:S(2)}, u32[]{:S(2)}) collective-permute-start(bf16[128,1024]{1,0:T(8,128)(2,1)S(1)} %get-tuple-element.18.refs_0_), channel_id=1, source_target_pairs={{0,4},{2,6},{4,0},{6,2},{1,5},{3,7},{5,1},{7,3},{8,12},{10,14},{12... | collective-permute-start | bytes 786440 | tf_op jit(solution)/shard_map/ppermute | solution.py:240
  7.7 8.7 %collective-permute-start.1 = (bf16[128,1024]{1,0:T(8,128)(2,1)S(1)}, bf16[128,1024]{1,0:T(8,128)(2,1)S(1)}, u32[]{:S(2)}, u32[]{:S(2)}) collective-permute-start(bf16[128,1024]{1,0:T(8,128)(2,1)S(1)} %get-tuple-element.18.refs_0_), channel_id=1, source_target_pairs={{0,2},{2,0},{4,6},{6,4},{1,3},{3,1},{5,7},{7,5},{8,10},{10,8},{12,... | collective-permute-start | bytes 786440 | tf_op jit(solution)/shard_map/ppermute | solution.py:245
  15.2 1.7 %collective-permute-start.2 = (bf16[128,1024]{1,0:T(8,128)(2,1)S(1)}, bf16[128,1024]{1,0:T(8,128)(2,1)S(1)}, u32[]{:S(2)}, u32[]{:S(2)}) collective-permute-start(bf16[128,1024]{1,0:T(8,128)(2,1)S(1)} %collective-permute-done.refs_2_), channel_id=1, source_target_pairs={{0,2},{2,0},{4,6},{6,4},{1,3},{3,1},{5,7},{7,5},{8,10},{10,8},{12,... | collective-permute-start | bytes 786440 | tf_op jit(solution)/shard_map/ppermute | solution.py:245
  19.1 7.1 %collective-permute-start.3 = (bf16[128,640]{1,0:T(8,128)(2,1)S(1)}, bf16[128,640]{1,0:T(8,128)(2,1)S(1)}, u32[]{:S(2)}, u32[]{:S(2)}) collective-permute-start(bf16[128,640]{1,0:T(8,128)(2,1)S(1)} %get-tuple-element.28.refs_2_), channel_id=1, source_target_pairs={{0,1},{1,0},{2,3},{3,2},{4,5},{5,4},{6,7},{7,6},{8,9},{9,8},{10,11... | collective-permute-start | bytes 491528 | tf_op jit(solution)/shard_map/ppermute | solution.py:240
  21.3 9.1 %collective-permute-start.5 = (bf16[128,768]{1,0:T(8,128)(2,1)S(1)}, bf16[128,768]{1,0:T(8,128)(2,1)S(1)}, u32[]{:S(2)}, u32[]{:S(2)}) collective-permute-start(bf16[128,768]{1,0:T(8,128)(2,1)S(1)} %away1.1.refs_2_), channel_id=1, source_target_pairs={{0,1},{1,0},{2,3},{3,2},{4,5},{5,4},{6,7},{7,6},{8,9},{9,8},{10,11... | collective-permute-start | bytes 589832 | tf_op jit(solution)/shard_map/ppermute | solution.py:240
  24.3 10.2 %collective-permute-start.7 = (bf16[128,640]{1,0:T(8,128)(2,1)S(1)}, bf16[128,640]{1,0:T(8,128)(2,1)S(1)}, u32[]{:S(2)}, u32[]{:S(2)}) collective-permute-start(bf16[128,640]{1,0:T(8,128)(2,1)S(1)} %get-tuple-element.30), channel_id=1, source_target_pairs={{0,1},{1,0},{2,3},{3,2},{4,5},{5,4},{6,7},{7,6},{8,9},{9,8},{10,11... | collective-permute-start | bytes 491528 | tf_op jit(solution)/shard_map/ppermute | solution.py:240
  26.3 8.2 %collective-permute-start.4 = (bf16[128,640]{1,0:T(8,128)(2,1)S(1)}, bf16[128,640]{1,0:T(8,128)(2,1)S(1)}, u32[]{:S(2)}, u32[]{:S(2)}) collective-permute-start(bf16[128,640]{1,0:T(8,128)(2,1)S(1)} %add.3.refs_1_), channel_id=1, source_target_pairs={{0,8},{8,16},{16,24},{24,0},{1,9},{9,17},{17,25},{25,1},{2,10},{10... | collective-permute-start | bytes 491528 | tf_op jit(solution)/shard_map/ppermute | solution.py:240
  30.5 8.1 %collective-permute-start.6 = (bf16[128,768]{1,0:T(8,128)(2,1)S(1)}, bf16[128,768]{1,0:T(8,128)(2,1)S(1)}, u32[]{:S(2)}, u32[]{:S(2)}) collective-permute-start(bf16[128,768]{1,0:T(8,128)(2,1)S(1)} %add.4.refs_1_.refs_2_), channel_id=1, source_target_pairs={{0,8},{8,16},{16,24},{24,0},{1,9},{9,17},{17,25},{25,1},{2,10},{10... | collective-permute-start | bytes 589832 | tf_op jit(solution)/shard_map/ppermute | solution.py:240
  34.6 7.2 %collective-permute-start.8 = (bf16[128,640]{1,0:T(8,128)(2,1)S(1)}, bf16[128,640]{1,0:T(8,128)(2,1)S(1)}, u32[]{:S(2)}, u32[]{:S(2)}) collective-permute-start(bf16[128,640]{1,0:T(8,128)(2,1)S(1)} %add.5), channel_id=1, source_target_pairs={{0,8},{8,16},{16,24},{24,0},{1,9},{9,17},{17,25},{25,1},{2,10},{10... | collective-permute-start | bytes 491528 | tf_op jit(solution)/shard_map/ppermute | solution.py:240

commit v5 on v4

--- a/solution.py
+++ b/solution.py
@@ -220,6 +220,31 @@
     for peer_ref in refs[: lax.axis_size("tp") - 1]:
         total = total + peer_ref[...].astype(jnp.float32)
     refs[-1][...] = total.astype(jnp.bfloat16)
+
+
+def place_kernel(starts, *refs):
+    pieces, out_hbm, sems = refs[: len(starts)], refs[-2], refs[-1]
+    copies = [
+        pltpu.make_async_copy(piece, out_hbm.at[0, :, pl.ds(start, piece.shape[1])], sems.at[k])
+        for k, (piece, start) in enumerate(zip(pieces, starts))
+    ]
+    for copy in copies:
+        copy.start()
+    for copy in copies:
+        copy.wait()
+
+
+def placed(pieces, starts, shape, before):
+    return pl.pallas_call(
+        functools.partial(place_kernel, starts),
+        out_shape=shape,
+        in_specs=[VMEM] * len(pieces) + [HBM] * len(before),
+        out_specs=HBM,
+        scratch_shapes=[pltpu.SemaphoreType.DMA((len(pieces),))],
+        input_output_aliases={len(pieces): 0} if before else {},
+        compiler_params=pltpu.CompilerParams(vmem_limit_bytes=16 * MIB),
+        name="place",
+    )(*pieces, *before)
 
 
 def call(kernel, name, outs, in_specs, scratch, mib, flops=0, moved=0):
@@ -353,7 +378,9 @@
         pieces.append(moved_by(total, "segment", 1))
         if j + 1 < len(widths):
             (own,) = products("own", owns[j + 1 : j + 2], attn, [], here(j + 1), widths[j + 1 : j + 2], total)
-    return jnp.concatenate(pieces, axis=1)[None]
+    shape = jax.ShapeDtypeStruct((1, rows, half), bf16)
+    most = placed(pieces[:-1], cuts[:-2], shape, [])
+    return placed(pieces[-1:], cuts[-2:-1], shape, [most])
 
 
 def solution(mesh):

time: 42.8 us -> 42.6 us (level)
  Pallas kernels: 22.2 us -> 23.6 us
  other arithmetic: 0.85 us -> 0 us
  waiting for transfers between devices: 6.53 us -> 5.77 us
    pallas_call x0 -> x2, Pallas kernels: none -> 1.42 us  [placed(): pl.pallas_call(functools.partial(place_kernel, starts), out_shape=shape,...]
    broadcast_in_dim x1 -> x0, other arithmetic: 0.85 us -> none  [body(): return jnp.concatenate(pieces, axis=1)[None]]
    ppermute x7, waiting for transfers between devices: 6.02 us -> 5.27 us  [moved_by(): lax.ppermute(value, axis, [(source, (source + steps) % count) for source...]
  transfers between devices with their start and end apart: 9 -> 9, of which waited for: 5 -> 5; matrix products, arithmetic and copies ran while one was open for 0% -> 0% of each run, Pallas kernels for 36% -> 38%
where the time goes in v5:
time: 42.6 us; the launch traced here: 42.4 us
  Pallas kernels  23.6 us (55%)
  starting transfers between devices  12.2 us (29%)
  waiting for transfers between devices  5.77 us (14%)
  between operations  0.77 us (2%)
    ppermute x7, starting transfers between devices, moved_by(): lax.ppermute(value, axis, [(source, (source + steps) % count) for source...  11.7 us
    pallas_call x4, Pallas kernels, products(): call(functools.partial(multiply_kernel, len(held), places), name, outs, [...  7.75 us
    pallas_call x1, Pallas kernels, body(): call(functools.partial(query_kernel, away(0) + here(0)), 'query', [jax.Sh...  7.48 us
    ppermute x7, waiting for transfers between devices, moved_by(): lax.ppermute(value, axis, [(source, (source + steps) % count) for source...  5.27 us
    pallas_call x1, Pallas kernels, body(): call(keyval_kernel, 'keyval', (jax.ShapeDtypeStruct((rows, kv_columns), b...  4.66 us
    pallas_call x1, Pallas kernels, body(): call(functools.partial(attend_kernel, len(kv_list), ahead), 'attend', [ja...  2.23 us
    pallas_call x2, Pallas kernels, placed(): pl.pallas_call(functools.partial(place_kernel, starts), out_shape=shape,...  1.42 us
  transfers between devices with their start and end apart: 9, of which 5 were waited for; matrix products, arithmetic and copies ran while one was open for 0% of the time, Pallas kernels for 38%

profile of v5, /device:TPU:0, one launch (start us, length us, event | category | flops | bytes accessed | tf_op | source)
XLA Modules:
  0.0 42.4 jit_solution(6911895215207794033)
XLA Ops:
  0.0 4.7 %keyval.1 = (bf16[128,1024]{1,0:T(8,128)(2,1)S(1)}, bf16[128,4096]{1,0:T(8,128)(2,1)S(1)}, f32[128,256]{1,0:T(8,128)S(1)}) custom-call(bf16[1,128,4096]{2,1,0:T(8,128)(2,1)} %hidden_hbm.1, bf16[1,4096]{1,0:T(2,128)(2,1)} %gain_hbm.1, f32[512,256]{1,0:T(8,128)} %constant.2.clone.table_hbm, bf16[1,4096,1024]{2,1,0:T(8,128)(2,1)} %weight_hbm.2), custom_call_target="tpu_custom_call" | custom-call | flops 1073741824 | bytes 8388608 | tf_op jit(solution)/shard_map/keyval/pallas_call | solution.py:287
  4.7 3.0 %collective-permute-start = (bf16[128,1024]{1,0:T(8,128)(2,1)S(1)}, bf16[128,1024]{1,0:T(8,128)(2,1)S(1)}, u32[]{:S(2)}, u32[]{:S(2)}) collective-permute-start(bf16[128,1024]{1,0:T(8,128)(2,1)S(1)} %get-tuple-element.18.refs_0_), channel_id=1, source_target_pairs={{0,4},{2,6},{4,0},{6,2},{1,5},{3,7},{5,1},{7,3},{8,12},{10,14},{12... | collective-permute-start | bytes 786440 | tf_op jit(solution)/shard_map/ppermute | solution.py:265
  7.7 0.0 collective-permute-start.1
  7.7 7.5 %query.1 = (bf16[128,2048]{1,0:T(8,128)(2,1)S(1)}, bf16[2048,640]{1,0:T(8,128)(2,1)S(1)}, bf16[2048,640]{1,0:T(8,128)(2,1)S(1)}) custom-call(bf16[128,4096]{1,0:T(8,128)(2,1)S(1)} %get-tuple-element.19.normed_ref, f32[128,256]{1,0:T(8,128)S(1)} %get-tuple-element.20.table, bf16[1,4096,2048]{2,1,0:T(8,128)(2,1)} %weight_hbm.3, bf16[1,2048,4096]{2,1,0:T(8,128)(2,1)} %refs_0_.3), custom_call_target="tpu_custom_call" | custom-call | flops 2147483648 | bytes 16777216 | tf_op jit(solution)/shard_map/query/pallas_call | solution.py:337
  15.2 0.0 collective-permute-done.refs_2_
  15.2 0.6 %collective-permute-start.2 = (bf16[128,1024]{1,0:T(8,128)(2,1)S(1)}, bf16[128,1024]{1,0:T(8,128)(2,1)S(1)}, u32[]{:S(2)}, u32[]{:S(2)}) collective-permute-start(bf16[128,1024]{1,0:T(8,128)(2,1)S(1)} %collective-permute-done.refs_2_), channel_id=1, source_target_pairs={{0,2},{2,0},{4,6},{6,4},{1,3},{3,1},{5,7},{7,5},{8,10},{10,8},{12,... | collective-permute-start | bytes 786440 | tf_op jit(solution)/shard_map/ppermute | solution.py:270
  16.4 0.0 collective-permute-done.1.refs_1_
  16.4 0.5 %collective-permute-done.2.refs_3_ = bf16[128,1024]{1,0:T(8,128)(2,1)S(1)} collective-permute-done((bf16[128,1024]{1,0:T(8,128)(2,1)S(1)}, bf16[128,1024]{1,0:T(8,128)(2,1)S(1)}, u32[]{:S(2)}, u32[]{:S(2)}) %collective-permute-start.2) | collective-permute-done | bytes 262176 | tf_op jit(solution)/shard_map/ppermute | solution.py:270
  16.9 2.2 %attend.1 = (bf16[128,2048]{1,0:T(8,128)(2,1)S(1)}, bf16[128,640]{1,0:T(8,128)(2,1)S(1)}, bf16[2048,768]{1,0:T(8,128)(2,1)S(1)}) custom-call(s32[1]{0:T(128)S(6)} %copy.10.window_ref, bf16[128,2048]{1,0:T(8,128)(2,1)S(1)} %get-tuple-element.22.query_ref, bf16[128,1024]{1,0:T(8,128)(2,1)S(1)} %get-tuple-element.18.refs_0_, ...), custom_call_target="tpu_custom_call" | custom-call | tf_op jit(solution)/shard_map/attend/pallas_call | solution.py:358
  19.1 1.6 %collective-permute-start.3 = (bf16[128,640]{1,0:T(8,128)(2,1)S(1)}, bf16[128,640]{1,0:T(8,128)(2,1)S(1)}, u32[]{:S(2)}, u32[]{:S(2)}) collective-permute-start(bf16[128,640]{1,0:T(8,128)(2,1)S(1)} %get-tuple-element.28.refs_2_), channel_id=1, source_target_pairs={{0,1},{1,0},{2,3},{3,2},{4,5},{5,4},{6,7},{7,6},{8,9},{9,8},{10,11... | collective-permute-start | bytes 491528 | tf_op jit(solution)/shard_map/ppermute | solution.py:265
  20.7 0.6 %away1.1.refs_2_ = bf16[128,768]{1,0:T(8,128)(2,1)S(1)} custom-call(bf16[128,2048]{1,0:T(8,128)(2,1)S(1)} %get-tuple-element.25.attn_ref, bf16[2048,768]{1,0:T(8,128)(2,1)S(1)} %get-tuple-element.27.refs_0_, bf16[1,2048,4096]{2,1,0:T(8,128)(2,1)} %refs_0_.3, bf16[128,640]{1,0:T(8,128)(2,1)S(1)} %get-tuple-element.28.refs_2_), custom_call_target="tpu_custom_call" | custom-call | tf_op jit(solution)/shard_map/away1/pallas_call | solution.py:327
  21.3 0.6 %collective-permute-start.4 = (bf16[128,768]{1,0:T(8,128)(2,1)S(1)}, bf16[128,768]{1,0:T(8,128)(2,1)S(1)}, u32[]{:S(2)}, u32[]{:S(2)}) collective-permute-start(bf16[128,768]{1,0:T(8,128)(2,1)S(1)} %away1.1.refs_2_), channel_id=1, source_target_pairs={{0,1},{1,0},{2,3},{3,2},{4,5},{5,4},{6,7},{7,6},{8,9},{9,8},{10,11... | collective-permute-start | bytes 589832 | tf_op jit(solution)/shard_map/ppermute | solution.py:265
  21.9 2.4 %own0.1 = (f32[128,640]{1,0:T(8,128)S(1)}, bf16[128,640]{1,0:T(8,128)(2,1)S(1)}) custom-call(bf16[128,2048]{1,0:T(8,128)(2,1)S(1)} %get-tuple-element.25.attn_ref, bf16[2048,640]{1,0:T(8,128)(2,1)S(1)} %get-tuple-element.26.refs_0_, bf16[1,2048,4096]{2,1,0:T(8,128)(2,1)} %refs_0_.3, bf16[128,768]{1,0:T(8,128)(2,1)S(1)} %away1.1.refs_2_), custom_call_target="tpu_custom_call" | custom-call | tf_op jit(solution)/shard_map/own0/pallas_call | solution.py:327
  24.3 1.6 %collective-permute-start.5 = (bf16[128,640]{1,0:T(8,128)(2,1)S(1)}, bf16[128,640]{1,0:T(8,128)(2,1)S(1)}, u32[]{:S(2)}, u32[]{:S(2)}) collective-permute-start(bf16[128,640]{1,0:T(8,128)(2,1)S(1)} %get-tuple-element.30), channel_id=1, source_target_pairs={{0,1},{1,0},{2,3},{3,2},{4,5},{5,4},{6,7},{7,6},{8,9},{9,8},{10,11... | collective-permute-start | bytes 491528 | tf_op jit(solution)/shard_map/ppermute | solution.py:265
  25.9 0.4 collective-permute-done.3.refs_0_
  26.3 1.6 %collective-permute-start.6 = (bf16[128,640]{1,0:T(8,128)(2,1)S(1)}, bf16[128,640]{1,0:T(8,128)(2,1)S(1)}, u32[]{:S(2)}, u32[]{:S(2)}) collective-permute-start(bf16[128,640]{1,0:T(8,128)(2,1)S(1)} %add.3.refs_1_), channel_id=1, source_target_pairs={{0,8},{8,16},{16,24},{24,0},{1,9},{9,17},{17,25},{25,1},{2,10},{10... | collective-permute-start | bytes 491528 | tf_op jit(solution)/shard_map/ppermute | solution.py:265
  27.9 2.4 %own.2.own_ref = f32[128,768]{1,0:T(8,128)S(1)} custom-call(bf16[128,2048]{1,0:T(8,128)(2,1)S(1)} %get-tuple-element.25.attn_ref, bf16[1,2048,4096]{2,1,0:T(8,128)(2,1)} %refs_0_.3, bf16[128,640]{1,0:T(8,128)(2,1)S(1)} %add.3.refs_1_), custom_call_target="tpu_custom_call" | custom-call | tf_op jit(solution)/shard_map/own/pallas_call | solution.py:327
  30.3 0.1 collective-permute-done.4.refs_0_
  30.5 1.6 %collective-permute-start.8 = (bf16[128,768]{1,0:T(8,128)(2,1)S(1)}, bf16[128,768]{1,0:T(8,128)(2,1)S(1)}, u32[]{:S(2)}, u32[]{:S(2)}) collective-permute-start(bf16[128,768]{1,0:T(8,128)(2,1)S(1)} %add.4.refs_1_.refs_2_), channel_id=1, source_target_pairs={{0,8},{8,16},{16,24},{24,0},{1,9},{9,17},{17,25},{25,1},{2,10},{10... | collective-permute-start | bytes 589832 | tf_op jit(solution)/shard_map/ppermute | solution.py:265
  32.1 2.4 %own.3.own_ref = f32[128,640]{1,0:T(8,128)S(1)} custom-call(bf16[128,2048]{1,0:T(8,128)(2,1)S(1)} %get-tuple-element.25.attn_ref, bf16[1,2048,4096]{2,1,0:T(8,128)(2,1)} %refs_0_.3, bf16[128,768]{1,0:T(8,128)(2,1)S(1)} %add.4.refs_1_.refs_2_), custom_call_target="tpu_custom_call" | custom-call | tf_op jit(solution)/shard_map/own/pallas_call | solution.py:327
  34.5 0.0 collective-permute-done.5.refs_0_
  34.5 0.0 collective-permute-done.6.refs_1_.refs_0_
  34.6 1.6 %collective-permute-start.7 = (bf16[128,640]{1,0:T(8,128)(2,1)S(1)}, bf16[128,640]{1,0:T(8,128)(2,1)S(1)}, u32[]{:S(2)}, u32[]{:S(2)}) collective-permute-start(bf16[128,640]{1,0:T(8,128)(2,1)S(1)} %add.5), channel_id=1, source_target_pairs={{0,8},{8,16},{16,24},{24,0},{1,9},{9,17},{17,25},{25,1},{2,10},{10... | collective-permute-start | bytes 491528 | tf_op jit(solution)/shard_map/ppermute | solution.py:265
  36.2 2.4 %collective-permute-done.8.refs_1_ = bf16[128,768]{1,0:T(8,128)(2,1)S(1)} collective-permute-done((bf16[128,768]{1,0:T(8,128)(2,1)S(1)}, bf16[128,768]{1,0:T(8,128)(2,1)S(1)}, u32[]{:S(2)}, u32[]{:S(2)}) %collective-permute-start.8) | collective-permute-done | bytes 196640 | tf_op jit(solution)/shard_map/ppermute | solution.py:265
  38.6 0.7 %place.2.refs_1_ = bf16[1,128,2048]{2,1,0:T(8,128)(2,1)} custom-call(bf16[128,640]{1,0:T(8,128)(2,1)S(1)} %collective-permute-done.6.refs_1_.refs_0_, bf16[128,768]{1,0:T(8,128)(2,1)S(1)} %collective-permute-done.8.refs_1_), custom_call_target="tpu_custom_call" | custom-call | tf_op jit(solution)/shard_map/place/pallas_call | solution.py:238
  39.4 2.3 %collective-permute-done.7.refs_0_ = bf16[128,640]{1,0:T(8,128)(2,1)S(1)} collective-permute-done((bf16[128,640]{1,0:T(8,128)(2,1)S(1)}, bf16[128,640]{1,0:T(8,128)(2,1)S(1)}, u32[]{:S(2)}, u32[]{:S(2)}) %collective-permute-start.7) | collective-permute-done | bytes 163872 | tf_op jit(solution)/shard_map/ppermute | solution.py:265
  41.7 0.7 %place.3 = bf16[1,128,2048]{2,1,0:T(8,128)(2,1)} custom-call(bf16[128,640]{1,0:T(8,128)(2,1)S(1)} %collective-permute-done.7.refs_0_, bf16[1,128,2048]{2,1,0:T(8,128)(2,1)} %place.2.refs_1_), custom_call_target="tpu_custom_call", output_to_operand_aliasing={{}: (1, {})} | custom-call | tf_op jit(solution)/shard_map/place/pallas_call | solution.py:238
  (3 shorter events, 0.1 us)
Async XLA Ops:
  4.7 10.5 %collective-permute-start = (bf16[128,1024]{1,0:T(8,128)(2,1)S(1)}, bf16[128,1024]{1,0:T(8,128)(2,1)S(1)}, u32[]{:S(2)}, u32[]{:S(2)}) collective-permute-start(bf16[128,1024]{1,0:T(8,128)(2,1)S(1)} %get-tuple-element.18.refs_0_), channel_id=1, source_target_pairs={{0,4},{2,6},{4,0},{6,2},{1,5},{3,7},{5,1},{7,3},{8,12},{10,14},{12... | collective-permute-start | bytes 786440 | tf_op jit(solution)/shard_map/ppermute | solution.py:265
  7.7 8.7 %collective-permute-start.1 = (bf16[128,1024]{1,0:T(8,128)(2,1)S(1)}, bf16[128,1024]{1,0:T(8,128)(2,1)S(1)}, u32[]{:S(2)}, u32[]{:S(2)}) collective-permute-start(bf16[128,1024]{1,0:T(8,128)(2,1)S(1)} %get-tuple-element.18.refs_0_), channel_id=1, source_target_pairs={{0,2},{2,0},{4,6},{6,4},{1,3},{3,1},{5,7},{7,5},{8,10},{10,8},{12,... | collective-permute-start | bytes 786440 | tf_op jit(solution)/shard_map/ppermute | solution.py:270
  15.2 1.7 %collective-permute-start.2 = (bf16[128,1024]{1,0:T(8,128)(2,1)S(1)}, bf16[128,1024]{1,0:T(8,128)(2,1)S(1)}, u32[]{:S(2)}, u32[]{:S(2)}) collective-permute-start(bf16[128,1024]{1,0:T(8,128)(2,1)S(1)} %collective-permute-done.refs_2_), channel_id=1, source_target_pairs={{0,2},{2,0},{4,6},{6,4},{1,3},{3,1},{5,7},{7,5},{8,10},{10,8},{12,... | collective-permute-start | bytes 786440 | tf_op jit(solution)/shard_map/ppermute | solution.py:270
  19.1 7.1 %collective-permute-start.3 = (bf16[128,640]{1,0:T(8,128)(2,1)S(1)}, bf16[128,640]{1,0:T(8,128)(2,1)S(1)}, u32[]{:S(2)}, u32[]{:S(2)}) collective-permute-start(bf16[128,640]{1,0:T(8,128)(2,1)S(1)} %get-tuple-element.28.refs_2_), channel_id=1, source_target_pairs={{0,1},{1,0},{2,3},{3,2},{4,5},{5,4},{6,7},{7,6},{8,9},{9,8},{10,11... | collective-permute-start | bytes 491528 | tf_op jit(solution)/shard_map/ppermute | solution.py:265
  21.3 9.1 %collective-permute-start.4 = (bf16[128,768]{1,0:T(8,128)(2,1)S(1)}, bf16[128,768]{1,0:T(8,128)(2,1)S(1)}, u32[]{:S(2)}, u32[]{:S(2)}) collective-permute-start(bf16[128,768]{1,0:T(8,128)(2,1)S(1)} %away1.1.refs_2_), channel_id=1, source_target_pairs={{0,1},{1,0},{2,3},{3,2},{4,5},{5,4},{6,7},{7,6},{8,9},{9,8},{10,11... | collective-permute-start | bytes 589832 | tf_op jit(solution)/shard_map/ppermute | solution.py:265
  24.3 10.2 %collective-permute-start.5 = (bf16[128,640]{1,0:T(8,128)(2,1)S(1)}, bf16[128,640]{1,0:T(8,128)(2,1)S(1)}, u32[]{:S(2)}, u32[]{:S(2)}) collective-permute-start(bf16[128,640]{1,0:T(8,128)(2,1)S(1)} %get-tuple-element.30), channel_id=1, source_target_pairs={{0,1},{1,0},{2,3},{3,2},{4,5},{5,4},{6,7},{7,6},{8,9},{9,8},{10,11... | collective-permute-start | bytes 491528 | tf_op jit(solution)/shard_map/ppermute | solution.py:265
  26.3 8.2 %collective-permute-start.6 = (bf16[128,640]{1,0:T(8,128)(2,1)S(1)}, bf16[128,640]{1,0:T(8,128)(2,1)S(1)}, u32[]{:S(2)}, u32[]{:S(2)}) collective-permute-start(bf16[128,640]{1,0:T(8,128)(2,1)S(1)} %add.3.refs_1_), channel_id=1, source_target_pairs={{0,8},{8,16},{16,24},{24,0},{1,9},{9,17},{17,25},{25,1},{2,10},{10... | collective-permute-start | bytes 491528 | tf_op jit(solution)/shard_map/ppermute | solution.py:265
  30.5 8.1 %collective-permute-start.8 = (bf16[128,768]{1,0:T(8,128)(2,1)S(1)}, bf16[128,768]{1,0:T(8,128)(2,1)S(1)}, u32[]{:S(2)}, u32[]{:S(2)}) collective-permute-start(bf16[128,768]{1,0:T(8,128)(2,1)S(1)} %add.4.refs_1_.refs_2_), channel_id=1, source_target_pairs={{0,8},{8,16},{16,24},{24,0},{1,9},{9,17},{17,25},{25,1},{2,10},{10... | collective-permute-start | bytes 589832 | tf_op jit(solution)/shard_map/ppermute | solution.py:265
  34.6 7.2 %collective-permute-start.7 = (bf16[128,640]{1,0:T(8,128)(2,1)S(1)}, bf16[128,640]{1,0:T(8,128)(2,1)S(1)}, u32[]{:S(2)}, u32[]{:S(2)}) collective-permute-start(bf16[128,640]{1,0:T(8,128)(2,1)S(1)} %add.5), channel_id=1, source_target_pairs={{0,8},{8,16},{16,24},{24,0},{1,9},{9,17},{17,25},{25,1},{2,10},{10... | collective-permute-start | bytes 491528 | tf_op jit(solution)/shard_map/ppermute | solution.py:265

commit v6 on v5

--- a/solution.py
+++ b/solution.py
@@ -65,29 +65,35 @@
         copy.start(priority=1)
     gain_copy.wait()
     hidden_copy.wait()
-    rows, features = hidden.shape
-    spans = [slice(at, at + HD) for at in range(0, features, HD)]
-    squares = jnp.zeros((rows, HD), jnp.float32)
-    for span in spans:
-        wide = hidden[:, span].astype(jnp.float32)
-        squares = squares + wide * wide
-    mean = jnp.sum(squares, axis=1, keepdims=True) * (1.0 / features)
-    inverse = jnp.broadcast_to(lax.rsqrt(mean + NORM_EPS), (rows, HD))
-    for span in spans:
-        wide = hidden[:, span].astype(jnp.float32)
-        normed_ref[:, span] = (wide * inverse * gain[:, span].astype(jnp.float32)).astype(jnp.bfloat16)
+
+    @pl.when(lax.axis_index("ctx") >= 0)
+    def _():
+        rows, features = hidden.shape
+        spans = [slice(at, at + HD) for at in range(0, features, HD)]
+        squares = jnp.zeros((rows, HD), jnp.float32)
+        for span in spans:
+            wide = hidden[:, span].astype(jnp.float32)
+            squares = squares + wide * wide
+        mean = jnp.sum(squares, axis=1, keepdims=True) * (1.0 / features)
+        inverse = jnp.broadcast_to(lax.rsqrt(mean + NORM_EPS), (rows, HD))
+        for span in spans:
+            wide = hidden[:, span].astype(jnp.float32)
+            normed_ref[:, span] = (wide * inverse * gain[:, span].astype(jnp.float32)).astype(jnp.bfloat16)
+
     tcopy.wait()
-    turn = table[...]
     width = weight.shape[1] // len(copies)
     for k, copy in enumerate(copies):
         copy.wait()
-        both = jnp.dot(
-            normed_ref[...], weight[:, width * k : width * (k + 1)], preferred_element_type=jnp.float32
-        )
-        for part in range(0, width, 2 * HD):
-            at = width * k + part
-            kv_ref[:, at : at + HD] = turned(both[:, part : part + HD], turn).astype(jnp.bfloat16)
-            kv_ref[:, at + HD : at + 2 * HD] = both[:, part + HD : part + 2 * HD].astype(jnp.bfloat16)
+
+        @pl.when(lax.axis_index("ctx") >= 0)
+        def _(k=k):
+            both = jnp.dot(
+                normed_ref[...], weight[:, width * k : width * (k + 1)], preferred_element_type=jnp.float32
+            )
+            for part in range(0, width, 2 * HD):
+                at = width * k + part
+                kv_ref[:, at : at + HD] = turned(both[:, part : part + HD], table).astype(jnp.bfloat16)
+                kv_ref[:, at + HD : at + 2 * HD] = both[:, part + HD : part + 2 * HD].astype(jnp.bfloat16)
 
 
 def query_kernel(places, normed_ref, table, weight_hbm, next_hbm, query_ref, *refs):
@@ -210,9 +216,12 @@
     for copy, (k, at, step) in zip(copies, pieces):
         copy.wait()
         out_ref = out_refs[held + k]
-        out_ref[:, at : at + step] = jnp.dot(
-            attn_ref[...], weights[k][:, at : at + step], preferred_element_type=jnp.float32
-        ).astype(out_ref.dtype)
+
+        @pl.when(lax.axis_index("ctx") >= 0)
+        def _(k=k, at=at, step=step, out_ref=out_ref):
+            out_ref[:, at : at + step] = jnp.dot(
+                attn_ref[...], weights[k][:, at : at + step], preferred_element_type=jnp.float32
+            ).astype(out_ref.dtype)
 
 
 def add_kernel(own_ref, *refs):
@@ -298,7 +307,7 @@
             pltpu.VMEM((1, features), bf16),
             pltpu.VMEM((features, kv_columns), bf16),
             dma((3,)),
-            dma((max(1, kv_columns // 512),)),
+            dma((kv_columns // (2 * HD),)),
         ],
         48,
         2 * rows * features * kv_columns,

time: 42.6 us -> 42.4 us (level)
  Pallas kernels: 23.6 us -> 22.9 us
  waiting for transfers between devices: 5.77 us -> 6.37 us
    ppermute x7, waiting for transfers between devices: 5.27 us -> 5.86 us  [moved_by(): lax.ppermute(value, axis, [(source, (source + steps) % count) for source...]
    pallas_call x4, Pallas kernels: 7.75 us -> 7.17 us  [products(): call(functools.partial(multiply_kernel, len(held), places), name, outs, [...]
  transfers between devices with their start and end apart: 9 -> 9, of which waited for: 5 -> 5; matrix products, arithmetic and copies ran while one was open for 0% -> 0% of each run, Pallas kernels for 38% -> 37%
where the time goes in v6:
time: 42.4 us; the launch traced here: 42.2 us
  Pallas kernels  22.9 us (54%)
  starting transfers between devices  12.2 us (29%)
  waiting for transfers between devices  6.37 us (15%)
  between operations  0.77 us (2%)
    ppermute x7, starting transfers between devices, moved_by(): lax.ppermute(value, axis, [(source, (source + steps) % count) for source...  11.6 us
    pallas_call x1, Pallas kernels, body(): call(functools.partial(query_kernel, away(0) + here(0)), 'query', [jax.Sh...  7.48 us
    pallas_call x4, Pallas kernels, products(): call(functools.partial(multiply_kernel, len(held), places), name, outs, [...  7.17 us
    ppermute x7, waiting for transfers between devices, moved_by(): lax.ppermute(value, axis, [(source, (source + steps) % count) for source...  5.86 us
    pallas_call x1, Pallas kernels, body(): call(keyval_kernel, 'keyval', (jax.ShapeDtypeStruct((rows, kv_columns), b...  4.47 us
    pallas_call x1, Pallas kernels, body(): call(functools.partial(attend_kernel, len(kv_list), ahead), 'attend', [ja...  2.23 us
    pallas_call x2, Pallas kernels, placed(): pl.pallas_call(functools.partial(place_kernel, starts), out_shape=shape,...  1.42 us
  transfers between devices with their start and end apart: 9, of which 5 were waited for; matrix products, arithmetic and copies ran while one was open for 0% of the time, Pallas kernels for 37%

profile of v6, /device:TPU:0, one launch (start us, length us, event | category | flops | bytes accessed | tf_op | source)
XLA Modules:
  0.0 42.2 jit_solution(1040036132873288100)
XLA Ops:
  0.0 4.5 %keyval.1 = (bf16[128,1024]{1,0:T(8,128)(2,1)S(1)}, bf16[128,4096]{1,0:T(8,128)(2,1)S(1)}, f32[128,256]{1,0:T(8,128)S(1)}) custom-call(bf16[1,128,4096]{2,1,0:T(8,128)(2,1)} %hidden_hbm.1, bf16[1,4096]{1,0:T(2,128)(2,1)} %gain_hbm.1, f32[512,256]{1,0:T(8,128)} %constant.2.clone.table_hbm, bf16[1,4096,1024]{2,1,0:T(8,128)(2,1)} %weight_hbm.2), custom_call_target="tpu_custom_call" | custom-call | flops 1073741824 | bytes 8388608 | tf_op jit(solution)/shard_map/keyval/pallas_call | solution.py:296
  4.5 3.0 %collective-permute-start = (bf16[128,1024]{1,0:T(8,128)(2,1)S(1)}, bf16[128,1024]{1,0:T(8,128)(2,1)S(1)}, u32[]{:S(2)}, u32[]{:S(2)}) collective-permute-start(bf16[128,1024]{1,0:T(8,128)(2,1)S(1)} %get-tuple-element.18.refs_0_), channel_id=1, source_target_pairs={{0,4},{2,6},{4,0},{6,2},{1,5},{3,7},{5,1},{7,3},{8,12},{10,14},{12... | collective-permute-start | bytes 786440 | tf_op jit(solution)/shard_map/ppermute | solution.py:274
  7.5 0.0 collective-permute-start.1
  7.5 7.5 %query.1 = (bf16[128,2048]{1,0:T(8,128)(2,1)S(1)}, bf16[2048,640]{1,0:T(8,128)(2,1)S(1)}, bf16[2048,640]{1,0:T(8,128)(2,1)S(1)}) custom-call(bf16[128,4096]{1,0:T(8,128)(2,1)S(1)} %get-tuple-element.19.normed_ref, f32[128,256]{1,0:T(8,128)S(1)} %get-tuple-element.20.table, bf16[1,4096,2048]{2,1,0:T(8,128)(2,1)} %weight_hbm.3, bf16[1,2048,4096]{2,1,0:T(8,128)(2,1)} %refs_0_.3), custom_call_target="tpu_custom_call" | custom-call | flops 2147483648 | bytes 16777216 | tf_op jit(solution)/shard_map/query/pallas_call | solution.py:346
  15.0 0.0 collective-permute-done.refs_2_
  15.0 0.6 %collective-permute-start.2 = (bf16[128,1024]{1,0:T(8,128)(2,1)S(1)}, bf16[128,1024]{1,0:T(8,128)(2,1)S(1)}, u32[]{:S(2)}, u32[]{:S(2)}) collective-permute-start(bf16[128,1024]{1,0:T(8,128)(2,1)S(1)} %collective-permute-done.refs_2_), channel_id=1, source_target_pairs={{0,2},{2,0},{4,6},{6,4},{1,3},{3,1},{5,7},{7,5},{8,10},{10,8},{12,... | collective-permute-start | bytes 786440 | tf_op jit(solution)/shard_map/ppermute | solution.py:279
  16.2 0.0 collective-permute-done.1.refs_1_
  16.2 0.5 %collective-permute-done.2.refs_3_ = bf16[128,1024]{1,0:T(8,128)(2,1)S(1)} collective-permute-done((bf16[128,1024]{1,0:T(8,128)(2,1)S(1)}, bf16[128,1024]{1,0:T(8,128)(2,1)S(1)}, u32[]{:S(2)}, u32[]{:S(2)}) %collective-permute-start.2) | collective-permute-done | bytes 262176 | tf_op jit(solution)/shard_map/ppermute | solution.py:279
  16.7 2.2 %attend.1 = (bf16[128,2048]{1,0:T(8,128)(2,1)S(1)}, bf16[128,640]{1,0:T(8,128)(2,1)S(1)}, bf16[2048,768]{1,0:T(8,128)(2,1)S(1)}) custom-call(s32[1]{0:T(128)S(6)} %copy.10.window_ref, bf16[128,2048]{1,0:T(8,128)(2,1)S(1)} %get-tuple-element.22.query_ref, bf16[128,1024]{1,0:T(8,128)(2,1)S(1)} %get-tuple-element.18.refs_0_, ...), custom_call_target="tpu_custom_call" | custom-call | tf_op jit(solution)/shard_map/attend/pallas_call | solution.py:367
  19.0 1.6 %collective-permute-start.3 = (bf16[128,640]{1,0:T(8,128)(2,1)S(1)}, bf16[128,640]{1,0:T(8,128)(2,1)S(1)}, u32[]{:S(2)}, u32[]{:S(2)}) collective-permute-start(bf16[128,640]{1,0:T(8,128)(2,1)S(1)} %get-tuple-element.28.refs_2_), channel_id=1, source_target_pairs={{0,1},{1,0},{2,3},{3,2},{4,5},{5,4},{6,7},{7,6},{8,9},{9,8},{10,11... | collective-permute-start | bytes 491528 | tf_op jit(solution)/shard_map/ppermute | solution.py:274
  20.6 0.6 %away1.1.refs_2_ = bf16[128,768]{1,0:T(8,128)(2,1)S(1)} custom-call(bf16[128,2048]{1,0:T(8,128)(2,1)S(1)} %get-tuple-element.25.attn_ref, bf16[2048,768]{1,0:T(8,128)(2,1)S(1)} %get-tuple-element.27.refs_0_, bf16[1,2048,4096]{2,1,0:T(8,128)(2,1)} %refs_0_.3, bf16[128,640]{1,0:T(8,128)(2,1)S(1)} %get-tuple-element.28.refs_2_), custom_call_target="tpu_custom_call" | custom-call | tf_op jit(solution)/shard_map/away1/pallas_call | solution.py:336
  21.1 0.6 %collective-permute-start.4 = (bf16[128,768]{1,0:T(8,128)(2,1)S(1)}, bf16[128,768]{1,0:T(8,128)(2,1)S(1)}, u32[]{:S(2)}, u32[]{:S(2)}) collective-permute-start(bf16[128,768]{1,0:T(8,128)(2,1)S(1)} %away1.1.refs_2_), channel_id=1, source_target_pairs={{0,1},{1,0},{2,3},{3,2},{4,5},{5,4},{6,7},{7,6},{8,9},{9,8},{10,11... | collective-permute-start | bytes 589832 | tf_op jit(solution)/shard_map/ppermute | solution.py:274
  21.7 2.2 %own0.1 = (f32[128,640]{1,0:T(8,128)S(1)}, bf16[128,640]{1,0:T(8,128)(2,1)S(1)}) custom-call(bf16[128,2048]{1,0:T(8,128)(2,1)S(1)} %get-tuple-element.25.attn_ref, bf16[2048,640]{1,0:T(8,128)(2,1)S(1)} %get-tuple-element.26.refs_0_, bf16[1,2048,4096]{2,1,0:T(8,128)(2,1)} %refs_0_.3, bf16[128,768]{1,0:T(8,128)(2,1)S(1)} %away1.1.refs_2_), custom_call_target="tpu_custom_call" | custom-call | tf_op jit(solution)/shard_map/own0/pallas_call | solution.py:336
  23.9 1.6 %collective-permute-start.5 = (bf16[128,640]{1,0:T(8,128)(2,1)S(1)}, bf16[128,640]{1,0:T(8,128)(2,1)S(1)}, u32[]{:S(2)}, u32[]{:S(2)}) collective-permute-start(bf16[128,640]{1,0:T(8,128)(2,1)S(1)} %get-tuple-element.30), channel_id=1, source_target_pairs={{0,1},{1,0},{2,3},{3,2},{4,5},{5,4},{6,7},{7,6},{8,9},{9,8},{10,11... | collective-permute-start | bytes 491528 | tf_op jit(solution)/shard_map/ppermute | solution.py:274
  25.5 0.6 %collective-permute-done.3.refs_0_ = bf16[128,640]{1,0:T(8,128)(2,1)S(1)} collective-permute-done((bf16[128,640]{1,0:T(8,128)(2,1)S(1)}, bf16[128,640]{1,0:T(8,128)(2,1)S(1)}, u32[]{:S(2)}, u32[]{:S(2)}) %collective-permute-start.3) | collective-permute-done | bytes 163872 | tf_op jit(solution)/shard_map/ppermute | solution.py:274
  26.1 1.6 %collective-permute-start.6 = (bf16[128,640]{1,0:T(8,128)(2,1)S(1)}, bf16[128,640]{1,0:T(8,128)(2,1)S(1)}, u32[]{:S(2)}, u32[]{:S(2)}) collective-permute-start(bf16[128,640]{1,0:T(8,128)(2,1)S(1)} %add.3.refs_1_), channel_id=1, source_target_pairs={{0,8},{8,16},{16,24},{24,0},{1,9},{9,17},{17,25},{25,1},{2,10},{10... | collective-permute-start | bytes 491528 | tf_op jit(solution)/shard_map/ppermute | solution.py:274
  27.7 2.2 %own.2.own_ref = f32[128,768]{1,0:T(8,128)S(1)} custom-call(bf16[128,2048]{1,0:T(8,128)(2,1)S(1)} %get-tuple-element.25.attn_ref, bf16[1,2048,4096]{2,1,0:T(8,128)(2,1)} %refs_0_.3, bf16[128,640]{1,0:T(8,128)(2,1)S(1)} %add.3.refs_1_), custom_call_target="tpu_custom_call" | custom-call | tf_op jit(solution)/shard_map/own/pallas_call | solution.py:336
  29.9 0.3 collective-permute-done.4.refs_0_
  30.3 1.6 %collective-permute-start.8 = (bf16[128,768]{1,0:T(8,128)(2,1)S(1)}, bf16[128,768]{1,0:T(8,128)(2,1)S(1)}, u32[]{:S(2)}, u32[]{:S(2)}) collective-permute-start(bf16[128,768]{1,0:T(8,128)(2,1)S(1)} %add.4.refs_1_.refs_2_), channel_id=1, source_target_pairs={{0,8},{8,16},{16,24},{24,0},{1,9},{9,17},{17,25},{25,1},{2,10},{10... | collective-permute-start | bytes 589832 | tf_op jit(solution)/shard_map/ppermute | solution.py:274
  31.9 2.2 %own.3.own_ref = f32[128,640]{1,0:T(8,128)S(1)} custom-call(bf16[128,2048]{1,0:T(8,128)(2,1)S(1)} %get-tuple-element.25.attn_ref, bf16[1,2048,4096]{2,1,0:T(8,128)(2,1)} %refs_0_.3, bf16[128,768]{1,0:T(8,128)(2,1)S(1)} %add.4.refs_1_.refs_2_), custom_call_target="tpu_custom_call" | custom-call | tf_op jit(solution)/shard_map/own/pallas_call | solution.py:336
  34.1 0.0 collective-permute-done.5.refs_0_
  34.1 0.0 collective-permute-done.6.refs_1_.refs_0_
  34.2 1.6 %collective-permute-start.7 = (bf16[128,640]{1,0:T(8,128)(2,1)S(1)}, bf16[128,640]{1,0:T(8,128)(2,1)S(1)}, u32[]{:S(2)}, u32[]{:S(2)}) collective-permute-start(bf16[128,640]{1,0:T(8,128)(2,1)S(1)} %add.5), channel_id=1, source_target_pairs={{0,8},{8,16},{16,24},{24,0},{1,9},{9,17},{17,25},{25,1},{2,10},{10... | collective-permute-start | bytes 491528 | tf_op jit(solution)/shard_map/ppermute | solution.py:274
  35.8 2.8 %collective-permute-done.8.refs_1_ = bf16[128,768]{1,0:T(8,128)(2,1)S(1)} collective-permute-done((bf16[128,768]{1,0:T(8,128)(2,1)S(1)}, bf16[128,768]{1,0:T(8,128)(2,1)S(1)}, u32[]{:S(2)}, u32[]{:S(2)}) %collective-permute-start.8) | collective-permute-done | bytes 196640 | tf_op jit(solution)/shard_map/ppermute | solution.py:274
  38.7 0.7 %place.2.refs_1_ = bf16[1,128,2048]{2,1,0:T(8,128)(2,1)} custom-call(bf16[128,640]{1,0:T(8,128)(2,1)S(1)} %collective-permute-done.6.refs_1_.refs_0_, bf16[128,768]{1,0:T(8,128)(2,1)S(1)} %collective-permute-done.8.refs_1_), custom_call_target="tpu_custom_call" | custom-call | tf_op jit(solution)/shard_map/place/pallas_call | solution.py:247
  39.4 2.1 %collective-permute-done.7.refs_0_ = bf16[128,640]{1,0:T(8,128)(2,1)S(1)} collective-permute-done((bf16[128,640]{1,0:T(8,128)(2,1)S(1)}, bf16[128,640]{1,0:T(8,128)(2,1)S(1)}, u32[]{:S(2)}, u32[]{:S(2)}) %collective-permute-start.7) | collective-permute-done | bytes 163872 | tf_op jit(solution)/shard_map/ppermute | solution.py:274
  41.6 0.7 %place.3 = bf16[1,128,2048]{2,1,0:T(8,128)(2,1)} custom-call(bf16[128,640]{1,0:T(8,128)(2,1)S(1)} %collective-permute-done.7.refs_0_, bf16[1,128,2048]{2,1,0:T(8,128)(2,1)} %place.2.refs_1_), custom_call_target="tpu_custom_call", output_to_operand_aliasing={{}: (1, {})} | custom-call | tf_op jit(solution)/shard_map/place/pallas_call | solution.py:247
  (3 shorter events, 0.1 us)
Async XLA Ops:
  4.5 10.5 %collective-permute-start = (bf16[128,1024]{1,0:T(8,128)(2,1)S(1)}, bf16[128,1024]{1,0:T(8,128)(2,1)S(1)}, u32[]{:S(2)}, u32[]{:S(2)}) collective-permute-start(bf16[128,1024]{1,0:T(8,128)(2,1)S(1)} %get-tuple-element.18.refs_0_), channel_id=1, source_target_pairs={{0,4},{2,6},{4,0},{6,2},{1,5},{3,7},{5,1},{7,3},{8,12},{10,14},{12... | collective-permute-start | bytes 786440 | tf_op jit(solution)/shard_map/ppermute | solution.py:274
  7.5 8.7 %collective-permute-start.1 = (bf16[128,1024]{1,0:T(8,128)(2,1)S(1)}, bf16[128,1024]{1,0:T(8,128)(2,1)S(1)}, u32[]{:S(2)}, u32[]{:S(2)}) collective-permute-start(bf16[128,1024]{1,0:T(8,128)(2,1)S(1)} %get-tuple-element.18.refs_0_), channel_id=1, source_target_pairs={{0,2},{2,0},{4,6},{6,4},{1,3},{3,1},{5,7},{7,5},{8,10},{10,8},{12,... | collective-permute-start | bytes 786440 | tf_op jit(solution)/shard_map/ppermute | solution.py:279
  15.0 1.7 %collective-permute-start.2 = (bf16[128,1024]{1,0:T(8,128)(2,1)S(1)}, bf16[128,1024]{1,0:T(8,128)(2,1)S(1)}, u32[]{:S(2)}, u32[]{:S(2)}) collective-permute-start(bf16[128,1024]{1,0:T(8,128)(2,1)S(1)} %collective-permute-done.refs_2_), channel_id=1, source_target_pairs={{0,2},{2,0},{4,6},{6,4},{1,3},{3,1},{5,7},{7,5},{8,10},{10,8},{12,... | collective-permute-start | bytes 786440 | tf_op jit(solution)/shard_map/ppermute | solution.py:279
  19.0 7.1 %collective-permute-start.3 = (bf16[128,640]{1,0:T(8,128)(2,1)S(1)}, bf16[128,640]{1,0:T(8,128)(2,1)S(1)}, u32[]{:S(2)}, u32[]{:S(2)}) collective-permute-start(bf16[128,640]{1,0:T(8,128)(2,1)S(1)} %get-tuple-element.28.refs_2_), channel_id=1, source_target_pairs={{0,1},{1,0},{2,3},{3,2},{4,5},{5,4},{6,7},{7,6},{8,9},{9,8},{10,11... | collective-permute-start | bytes 491528 | tf_op jit(solution)/shard_map/ppermute | solution.py:274
  21.1 9.1 %collective-permute-start.4 = (bf16[128,768]{1,0:T(8,128)(2,1)S(1)}, bf16[128,768]{1,0:T(8,128)(2,1)S(1)}, u32[]{:S(2)}, u32[]{:S(2)}) collective-permute-start(bf16[128,768]{1,0:T(8,128)(2,1)S(1)} %away1.1.refs_2_), channel_id=1, source_target_pairs={{0,1},{1,0},{2,3},{3,2},{4,5},{5,4},{6,7},{7,6},{8,9},{9,8},{10,11... | collective-permute-start | bytes 589832 | tf_op jit(solution)/shard_map/ppermute | solution.py:274
  23.9 10.2 %collective-permute-start.5 = (bf16[128,640]{1,0:T(8,128)(2,1)S(1)}, bf16[128,640]{1,0:T(8,128)(2,1)S(1)}, u32[]{:S(2)}, u32[]{:S(2)}) collective-permute-start(bf16[128,640]{1,0:T(8,128)(2,1)S(1)} %get-tuple-element.30), channel_id=1, source_target_pairs={{0,1},{1,0},{2,3},{3,2},{4,5},{5,4},{6,7},{7,6},{8,9},{9,8},{10,11... | collective-permute-start | bytes 491528 | tf_op jit(solution)/shard_map/ppermute | solution.py:274
  26.1 8.0 %collective-permute-start.6 = (bf16[128,640]{1,0:T(8,128)(2,1)S(1)}, bf16[128,640]{1,0:T(8,128)(2,1)S(1)}, u32[]{:S(2)}, u32[]{:S(2)}) collective-permute-start(bf16[128,640]{1,0:T(8,128)(2,1)S(1)} %add.3.refs_1_), channel_id=1, source_target_pairs={{0,8},{8,16},{16,24},{24,0},{1,9},{9,17},{17,25},{25,1},{2,10},{10... | collective-permute-start | bytes 491528 | tf_op jit(solution)/shard_map/ppermute | solution.py:274
  30.3 8.4 %collective-permute-start.8 = (bf16[128,768]{1,0:T(8,128)(2,1)S(1)}, bf16[128,768]{1,0:T(8,128)(2,1)S(1)}, u32[]{:S(2)}, u32[]{:S(2)}) collective-permute-start(bf16[128,768]{1,0:T(8,128)(2,1)S(1)} %add.4.refs_1_.refs_2_), channel_id=1, source_target_pairs={{0,8},{8,16},{16,24},{24,0},{1,9},{9,17},{17,25},{25,1},{2,10},{10... | collective-permute-start | bytes 589832 | tf_op jit(solution)/shard_map/ppermute | solution.py:274
  34.2 7.4 %collective-permute-start.7 = (bf16[128,640]{1,0:T(8,128)(2,1)S(1)}, bf16[128,640]{1,0:T(8,128)(2,1)S(1)}, u32[]{:S(2)}, u32[]{:S(2)}) collective-permute-start(bf16[128,640]{1,0:T(8,128)(2,1)S(1)} %add.5), channel_id=1, source_target_pairs={{0,8},{8,16},{16,24},{24,0},{1,9},{9,17},{17,25},{25,1},{2,10},{10... | collective-permute-start | bytes 491528 | tf_op jit(solution)/shard_map/ppermute | solution.py:274

commit v7 on v6

--- a/solution.py
+++ b/solution.py
@@ -12,6 +12,7 @@
 REACH = 3
 NORM_EPS = 1e-05
 SHARES = (5, 6, 5)
+PARTS = 4
 LOG2E = 1.4426950408889634
 MIB = 1024 * 1024
 
@@ -233,9 +234,15 @@
 
 def place_kernel(starts, *refs):
     pieces, out_hbm, sems = refs[: len(starts)], refs[-2], refs[-1]
+    rows = pieces[0].shape[0] // PARTS
     copies = [
-        pltpu.make_async_copy(piece, out_hbm.at[0, :, pl.ds(start, piece.shape[1])], sems.at[k])
+        pltpu.make_async_copy(
+            piece.at[pl.ds(part * rows, rows)],
+            out_hbm.at[0, pl.ds(part * rows, rows), pl.ds(start, piece.shape[1])],
+            sems.at[k, part],
+        )
         for k, (piece, start) in enumerate(zip(pieces, starts))
+        for part in range(PARTS)
     ]
     for copy in copies:
         copy.start()
@@ -249,7 +256,7 @@
         out_shape=shape,
         in_specs=[VMEM] * len(pieces) + [HBM] * len(before),
         out_specs=HBM,
-        scratch_shapes=[pltpu.SemaphoreType.DMA((len(pieces),))],
+        scratch_shapes=[pltpu.SemaphoreType.DMA((len(pieces), PARTS))],
         input_output_aliases={len(pieces): 0} if before else {},
         compiler_params=pltpu.CompilerParams(vmem_limit_bytes=16 * MIB),
         name="place",

time: 42.4 us -> 42.4 us (level)
  no operation moved by 1% of the time
where the time goes in v7:
time: 42.4 us; the launch traced here: 42.2 us
  Pallas kernels  22.9 us (54%)
  starting transfers between devices  12.2 us (29%)
  waiting for transfers between devices  6.32 us (15%)
  between operations  0.77 us (2%)
    ppermute x7, starting transfers between devices, moved_by(): lax.ppermute(value, axis, [(source, (source + steps) % count) for source...  11.6 us
    pallas_call x1, Pallas kernels, body(): call(functools.partial(query_kernel, away(0) + here(0)), 'query', [jax.Sh...  7.48 us
    pallas_call x4, Pallas kernels, products(): call(functools.partial(multiply_kernel, len(held), places), name, outs, [...  7.17 us
    ppermute x7, waiting for transfers between devices, moved_by(): lax.ppermute(value, axis, [(source, (source + steps) % count) for source...  5.82 us
    pallas_call x1, Pallas kernels, body(): call(keyval_kernel, 'keyval', (jax.ShapeDtypeStruct((rows, kv_columns), b...  4.47 us
    pallas_call x1, Pallas kernels, body(): call(functools.partial(attend_kernel, len(kv_list), ahead), 'attend', [ja...  2.23 us
    pallas_call x2, Pallas kernels, placed(): pl.pallas_call(functools.partial(place_kernel, starts), out_shape=shape,...  1.48 us
  transfers between devices with their start and end apart: 9, of which 5 were waited for; matrix products, arithmetic and copies ran while one was open for 0% of the time, Pallas kernels for 37%

profile of v7, /device:TPU:0, one launch (start us, length us, event | category | flops | bytes accessed | tf_op | source)
XLA Modules:
  0.0 42.2 jit_solution(17330060441535608407)
XLA Ops:
  0.0 4.5 %keyval.1 = (bf16[128,1024]{1,0:T(8,128)(2,1)S(1)}, bf16[128,4096]{1,0:T(8,128)(2,1)S(1)}, f32[128,256]{1,0:T(8,128)S(1)}) custom-call(bf16[1,128,4096]{2,1,0:T(8,128)(2,1)} %hidden_hbm.1, bf16[1,4096]{1,0:T(2,128)(2,1)} %gain_hbm.1, f32[512,256]{1,0:T(8,128)} %constant.2.clone.table_hbm, bf16[1,4096,1024]{2,1,0:T(8,128)(2,1)} %weight_hbm.2), custom_call_target="tpu_custom_call" | custom-call | flops 1073741824 | bytes 8388608 | tf_op jit(solution)/shard_map/keyval/pallas_call | solution.py:303
  4.5 3.0 %collective-permute-start = (bf16[128,1024]{1,0:T(8,128)(2,1)S(1)}, bf16[128,1024]{1,0:T(8,128)(2,1)S(1)}, u32[]{:S(2)}, u32[]{:S(2)}) collective-permute-start(bf16[128,1024]{1,0:T(8,128)(2,1)S(1)} %get-tuple-element.18.refs_0_), channel_id=1, source_target_pairs={{0,4},{2,6},{4,0},{6,2},{1,5},{3,7},{5,1},{7,3},{8,12},{10,14},{12... | collective-permute-start | bytes 786440 | tf_op jit(solution)/shard_map/ppermute | solution.py:281
  7.5 0.0 collective-permute-start.1
  7.5 7.5 %query.1 = (bf16[128,2048]{1,0:T(8,128)(2,1)S(1)}, bf16[2048,640]{1,0:T(8,128)(2,1)S(1)}, bf16[2048,640]{1,0:T(8,128)(2,1)S(1)}) custom-call(bf16[128,4096]{1,0:T(8,128)(2,1)S(1)} %get-tuple-element.19.normed_ref, f32[128,256]{1,0:T(8,128)S(1)} %get-tuple-element.20.table, bf16[1,4096,2048]{2,1,0:T(8,128)(2,1)} %weight_hbm.3, bf16[1,2048,4096]{2,1,0:T(8,128)(2,1)} %refs_0_.3), custom_call_target="tpu_custom_call" | custom-call | flops 2147483648 | bytes 16777216 | tf_op jit(solution)/shard_map/query/pallas_call | solution.py:353
  15.0 0.0 collective-permute-done.refs_2_
  15.0 0.6 %collective-permute-start.2 = (bf16[128,1024]{1,0:T(8,128)(2,1)S(1)}, bf16[128,1024]{1,0:T(8,128)(2,1)S(1)}, u32[]{:S(2)}, u32[]{:S(2)}) collective-permute-start(bf16[128,1024]{1,0:T(8,128)(2,1)S(1)} %collective-permute-done.refs_2_), channel_id=1, source_target_pairs={{0,2},{2,0},{4,6},{6,4},{1,3},{3,1},{5,7},{7,5},{8,10},{10,8},{12,... | collective-permute-start | bytes 786440 | tf_op jit(solution)/shard_map/ppermute | solution.py:286
  16.2 0.0 collective-permute-done.1.refs_1_
  16.2 0.5 %collective-permute-done.2.refs_3_ = bf16[128,1024]{1,0:T(8,128)(2,1)S(1)} collective-permute-done((bf16[128,1024]{1,0:T(8,128)(2,1)S(1)}, bf16[128,1024]{1,0:T(8,128)(2,1)S(1)}, u32[]{:S(2)}, u32[]{:S(2)}) %collective-permute-start.2) | collective-permute-done | bytes 262176 | tf_op jit(solution)/shard_map/ppermute | solution.py:286
  16.7 2.2 %attend.1 = (bf16[128,2048]{1,0:T(8,128)(2,1)S(1)}, bf16[128,640]{1,0:T(8,128)(2,1)S(1)}, bf16[2048,768]{1,0:T(8,128)(2,1)S(1)}) custom-call(s32[1]{0:T(128)S(6)} %copy.10.window_ref, bf16[128,2048]{1,0:T(8,128)(2,1)S(1)} %get-tuple-element.22.query_ref, bf16[128,1024]{1,0:T(8,128)(2,1)S(1)} %get-tuple-element.18.refs_0_, ...), custom_call_target="tpu_custom_call" | custom-call | tf_op jit(solution)/shard_map/attend/pallas_call | solution.py:374
  19.0 1.6 %collective-permute-start.3 = (bf16[128,640]{1,0:T(8,128)(2,1)S(1)}, bf16[128,640]{1,0:T(8,128)(2,1)S(1)}, u32[]{:S(2)}, u32[]{:S(2)}) collective-permute-start(bf16[128,640]{1,0:T(8,128)(2,1)S(1)} %get-tuple-element.28.refs_2_), channel_id=1, source_target_pairs={{0,1},{1,0},{2,3},{3,2},{4,5},{5,4},{6,7},{7,6},{8,9},{9,8},{10,11... | collective-permute-start | bytes 491528 | tf_op jit(solution)/shard_map/ppermute | solution.py:281
  20.6 0.6 %away1.1.refs_2_ = bf16[128,768]{1,0:T(8,128)(2,1)S(1)} custom-call(bf16[128,2048]{1,0:T(8,128)(2,1)S(1)} %get-tuple-element.25.attn_ref, bf16[2048,768]{1,0:T(8,128)(2,1)S(1)} %get-tuple-element.27.refs_0_, bf16[1,2048,4096]{2,1,0:T(8,128)(2,1)} %refs_0_.3, bf16[128,640]{1,0:T(8,128)(2,1)S(1)} %get-tuple-element.28.refs_2_), custom_call_target="tpu_custom_call" | custom-call | tf_op jit(solution)/shard_map/away1/pallas_call | solution.py:343
  21.1 0.6 %collective-permute-start.4 = (bf16[128,768]{1,0:T(8,128)(2,1)S(1)}, bf16[128,768]{1,0:T(8,128)(2,1)S(1)}, u32[]{:S(2)}, u32[]{:S(2)}) collective-permute-start(bf16[128,768]{1,0:T(8,128)(2,1)S(1)} %away1.1.refs_2_), channel_id=1, source_target_pairs={{0,1},{1,0},{2,3},{3,2},{4,5},{5,4},{6,7},{7,6},{8,9},{9,8},{10,11... | collective-permute-start | bytes 589832 | tf_op jit(solution)/shard_map/ppermute | solution.py:281
  21.7 2.2 %own0.1 = (f32[128,640]{1,0:T(8,128)S(1)}, bf16[128,640]{1,0:T(8,128)(2,1)S(1)}) custom-call(bf16[128,2048]{1,0:T(8,128)(2,1)S(1)} %get-tuple-element.25.attn_ref, bf16[2048,640]{1,0:T(8,128)(2,1)S(1)} %get-tuple-element.26.refs_0_, bf16[1,2048,4096]{2,1,0:T(8,128)(2,1)} %refs_0_.3, bf16[128,768]{1,0:T(8,128)(2,1)S(1)} %away1.1.refs_2_), custom_call_target="tpu_custom_call" | custom-call | tf_op jit(solution)/shard_map/own0/pallas_call | solution.py:343
  23.9 1.6 %collective-permute-start.5 = (bf16[128,640]{1,0:T(8,128)(2,1)S(1)}, bf16[128,640]{1,0:T(8,128)(2,1)S(1)}, u32[]{:S(2)}, u32[]{:S(2)}) collective-permute-start(bf16[128,640]{1,0:T(8,128)(2,1)S(1)} %get-tuple-element.30), channel_id=1, source_target_pairs={{0,1},{1,0},{2,3},{3,2},{4,5},{5,4},{6,7},{7,6},{8,9},{9,8},{10,11... | collective-permute-start | bytes 491528 | tf_op jit(solution)/shard_map/ppermute | solution.py:281
  25.5 0.6 %collective-permute-done.3.refs_0_ = bf16[128,640]{1,0:T(8,128)(2,1)S(1)} collective-permute-done((bf16[128,640]{1,0:T(8,128)(2,1)S(1)}, bf16[128,640]{1,0:T(8,128)(2,1)S(1)}, u32[]{:S(2)}, u32[]{:S(2)}) %collective-permute-start.3) | collective-permute-done | bytes 163872 | tf_op jit(solution)/shard_map/ppermute | solution.py:281
  26.1 1.6 %collective-permute-start.6 = (bf16[128,640]{1,0:T(8,128)(2,1)S(1)}, bf16[128,640]{1,0:T(8,128)(2,1)S(1)}, u32[]{:S(2)}, u32[]{:S(2)}) collective-permute-start(bf16[128,640]{1,0:T(8,128)(2,1)S(1)} %add.3.refs_1_), channel_id=1, source_target_pairs={{0,8},{8,16},{16,24},{24,0},{1,9},{9,17},{17,25},{25,1},{2,10},{10... | collective-permute-start | bytes 491528 | tf_op jit(solution)/shard_map/ppermute | solution.py:281
  27.7 2.2 %own.2.own_ref = f32[128,768]{1,0:T(8,128)S(1)} custom-call(bf16[128,2048]{1,0:T(8,128)(2,1)S(1)} %get-tuple-element.25.attn_ref, bf16[1,2048,4096]{2,1,0:T(8,128)(2,1)} %refs_0_.3, bf16[128,640]{1,0:T(8,128)(2,1)S(1)} %add.3.refs_1_), custom_call_target="tpu_custom_call" | custom-call | tf_op jit(solution)/shard_map/own/pallas_call | solution.py:343
  29.9 0.3 collective-permute-done.4.refs_0_
  30.3 1.6 %collective-permute-start.8 = (bf16[128,768]{1,0:T(8,128)(2,1)S(1)}, bf16[128,768]{1,0:T(8,128)(2,1)S(1)}, u32[]{:S(2)}, u32[]{:S(2)}) collective-permute-start(bf16[128,768]{1,0:T(8,128)(2,1)S(1)} %add.4.refs_1_.refs_2_), channel_id=1, source_target_pairs={{0,8},{8,16},{16,24},{24,0},{1,9},{9,17},{17,25},{25,1},{2,10},{10... | collective-permute-start | bytes 589832 | tf_op jit(solution)/shard_map/ppermute | solution.py:281
  31.9 2.2 %own.3.own_ref = f32[128,640]{1,0:T(8,128)S(1)} custom-call(bf16[128,2048]{1,0:T(8,128)(2,1)S(1)} %get-tuple-element.25.attn_ref, bf16[1,2048,4096]{2,1,0:T(8,128)(2,1)} %refs_0_.3, bf16[128,768]{1,0:T(8,128)(2,1)S(1)} %add.4.refs_1_.refs_2_), custom_call_target="tpu_custom_call" | custom-call | tf_op jit(solution)/shard_map/own/pallas_call | solution.py:343
  34.1 0.0 collective-permute-done.5.refs_0_
  34.1 0.0 collective-permute-done.6.refs_1_.refs_0_
  34.2 1.6 %collective-permute-start.7 = (bf16[128,640]{1,0:T(8,128)(2,1)S(1)}, bf16[128,640]{1,0:T(8,128)(2,1)S(1)}, u32[]{:S(2)}, u32[]{:S(2)}) collective-permute-start(bf16[128,640]{1,0:T(8,128)(2,1)S(1)} %add.5), channel_id=1, source_target_pairs={{0,8},{8,16},{16,24},{24,0},{1,9},{9,17},{17,25},{25,1},{2,10},{10... | collective-permute-start | bytes 491528 | tf_op jit(solution)/shard_map/ppermute | solution.py:281
  35.8 2.8 %collective-permute-done.8.refs_1_ = bf16[128,768]{1,0:T(8,128)(2,1)S(1)} collective-permute-done((bf16[128,768]{1,0:T(8,128)(2,1)S(1)}, bf16[128,768]{1,0:T(8,128)(2,1)S(1)}, u32[]{:S(2)}, u32[]{:S(2)}) %collective-permute-start.8) | collective-permute-done | bytes 196640 | tf_op jit(solution)/shard_map/ppermute | solution.py:281
  38.7 0.8 %place.2.refs_1_ = bf16[1,128,2048]{2,1,0:T(8,128)(2,1)} custom-call(bf16[128,640]{1,0:T(8,128)(2,1)S(1)} %collective-permute-done.6.refs_1_.refs_0_, bf16[128,768]{1,0:T(8,128)(2,1)S(1)} %collective-permute-done.8.refs_1_), custom_call_target="tpu_custom_call" | custom-call | tf_op jit(solution)/shard_map/place/pallas_call | solution.py:254
  39.5 2.1 %collective-permute-done.7.refs_0_ = bf16[128,640]{1,0:T(8,128)(2,1)S(1)} collective-permute-done((bf16[128,640]{1,0:T(8,128)(2,1)S(1)}, bf16[128,640]{1,0:T(8,128)(2,1)S(1)}, u32[]{:S(2)}, u32[]{:S(2)}) %collective-permute-start.7) | collective-permute-done | bytes 163872 | tf_op jit(solution)/shard_map/ppermute | solution.py:281
  41.6 0.7 %place.3 = bf16[1,128,2048]{2,1,0:T(8,128)(2,1)} custom-call(bf16[128,640]{1,0:T(8,128)(2,1)S(1)} %collective-permute-done.7.refs_0_, bf16[1,128,2048]{2,1,0:T(8,128)(2,1)} %place.2.refs_1_), custom_call_target="tpu_custom_call", output_to_operand_aliasing={{}: (1, {})} | custom-call | tf_op jit(solution)/shard_map/place/pallas_call | solution.py:254
  (3 shorter events, 0.1 us)
Async XLA Ops:
  4.5 10.5 %collective-permute-start = (bf16[128,1024]{1,0:T(8,128)(2,1)S(1)}, bf16[128,1024]{1,0:T(8,128)(2,1)S(1)}, u32[]{:S(2)}, u32[]{:S(2)}) collective-permute-start(bf16[128,1024]{1,0:T(8,128)(2,1)S(1)} %get-tuple-element.18.refs_0_), channel_id=1, source_target_pairs={{0,4},{2,6},{4,0},{6,2},{1,5},{3,7},{5,1},{7,3},{8,12},{10,14},{12... | collective-permute-start | bytes 786440 | tf_op jit(solution)/shard_map/ppermute | solution.py:281
  7.5 8.7 %collective-permute-start.1 = (bf16[128,1024]{1,0:T(8,128)(2,1)S(1)}, bf16[128,1024]{1,0:T(8,128)(2,1)S(1)}, u32[]{:S(2)}, u32[]{:S(2)}) collective-permute-start(bf16[128,1024]{1,0:T(8,128)(2,1)S(1)} %get-tuple-element.18.refs_0_), channel_id=1, source_target_pairs={{0,2},{2,0},{4,6},{6,4},{1,3},{3,1},{5,7},{7,5},{8,10},{10,8},{12,... | collective-permute-start | bytes 786440 | tf_op jit(solution)/shard_map/ppermute | solution.py:286
  15.0 1.7 %collective-permute-start.2 = (bf16[128,1024]{1,0:T(8,128)(2,1)S(1)}, bf16[128,1024]{1,0:T(8,128)(2,1)S(1)}, u32[]{:S(2)}, u32[]{:S(2)}) collective-permute-start(bf16[128,1024]{1,0:T(8,128)(2,1)S(1)} %collective-permute-done.refs_2_), channel_id=1, source_target_pairs={{0,2},{2,0},{4,6},{6,4},{1,3},{3,1},{5,7},{7,5},{8,10},{10,8},{12,... | collective-permute-start | bytes 786440 | tf_op jit(solution)/shard_map/ppermute | solution.py:286
  19.0 7.1 %collective-permute-start.3 = (bf16[128,640]{1,0:T(8,128)(2,1)S(1)}, bf16[128,640]{1,0:T(8,128)(2,1)S(1)}, u32[]{:S(2)}, u32[]{:S(2)}) collective-permute-start(bf16[128,640]{1,0:T(8,128)(2,1)S(1)} %get-tuple-element.28.refs_2_), channel_id=1, source_target_pairs={{0,1},{1,0},{2,3},{3,2},{4,5},{5,4},{6,7},{7,6},{8,9},{9,8},{10,11... | collective-permute-start | bytes 491528 | tf_op jit(solution)/shard_map/ppermute | solution.py:281
  21.1 9.1 %collective-permute-start.4 = (bf16[128,768]{1,0:T(8,128)(2,1)S(1)}, bf16[128,768]{1,0:T(8,128)(2,1)S(1)}, u32[]{:S(2)}, u32[]{:S(2)}) collective-permute-start(bf16[128,768]{1,0:T(8,128)(2,1)S(1)} %away1.1.refs_2_), channel_id=1, source_target_pairs={{0,1},{1,0},{2,3},{3,2},{4,5},{5,4},{6,7},{7,6},{8,9},{9,8},{10,11... | collective-permute-start | bytes 589832 | tf_op jit(solution)/shard_map/ppermute | solution.py:281
  23.9 10.2 %collective-permute-start.5 = (bf16[128,640]{1,0:T(8,128)(2,1)S(1)}, bf16[128,640]{1,0:T(8,128)(2,1)S(1)}, u32[]{:S(2)}, u32[]{:S(2)}) collective-permute-start(bf16[128,640]{1,0:T(8,128)(2,1)S(1)} %get-tuple-element.30), channel_id=1, source_target_pairs={{0,1},{1,0},{2,3},{3,2},{4,5},{5,4},{6,7},{7,6},{8,9},{9,8},{10,11... | collective-permute-start | bytes 491528 | tf_op jit(solution)/shard_map/ppermute | solution.py:281
  26.1 8.0 %collective-permute-start.6 = (bf16[128,640]{1,0:T(8,128)(2,1)S(1)}, bf16[128,640]{1,0:T(8,128)(2,1)S(1)}, u32[]{:S(2)}, u32[]{:S(2)}) collective-permute-start(bf16[128,640]{1,0:T(8,128)(2,1)S(1)} %add.3.refs_1_), channel_id=1, source_target_pairs={{0,8},{8,16},{16,24},{24,0},{1,9},{9,17},{17,25},{25,1},{2,10},{10... | collective-permute-start | bytes 491528 | tf_op jit(solution)/shard_map/ppermute | solution.py:281
  30.3 8.4 %collective-permute-start.8 = (bf16[128,768]{1,0:T(8,128)(2,1)S(1)}, bf16[128,768]{1,0:T(8,128)(2,1)S(1)}, u32[]{:S(2)}, u32[]{:S(2)}) collective-permute-start(bf16[128,768]{1,0:T(8,128)(2,1)S(1)} %add.4.refs_1_.refs_2_), channel_id=1, source_target_pairs={{0,8},{8,16},{16,24},{24,0},{1,9},{9,17},{17,25},{25,1},{2,10},{10... | collective-permute-start | bytes 589832 | tf_op jit(solution)/shard_map/ppermute | solution.py:281
  34.2 7.4 %collective-permute-start.7 = (bf16[128,640]{1,0:T(8,128)(2,1)S(1)}, bf16[128,640]{1,0:T(8,128)(2,1)S(1)}, u32[]{:S(2)}, u32[]{:S(2)}) collective-permute-start(bf16[128,640]{1,0:T(8,128)(2,1)S(1)} %add.5), channel_id=1, source_target_pairs={{0,8},{8,16},{16,24},{24,0},{1,9},{9,17},{17,25},{25,1},{2,10},{10... | collective-permute-start | bytes 491528 | tf_op jit(solution)/shard_map/ppermute | solution.py:281
